TPU v7x, 32 devices: a whole 2x2x4 slice. The times are simulated.
32 devices in a mesh: band: 4 (over y, x), stream: 8 (over z, core).
Axes of the slice: x: 2, y: 2, z: 4, core: 2. Of those that a mesh axis runs over, the one named last changes fastest.
Arguments:
- spectrum: float32 [512, 2, 1025], P('stream'), may hold values from -6 to 6
- segments: int32 [8, 64], P('stream'), may hold values from 0 to 2, never falling along the last dimension, each value on 1 to 32 neighbouring positions
- widths: int32 [41], replicated, may hold values from 1 to 128, 1025 in all
- groups: int32 [41], replicated, may hold values from 0 to 3, as said below
- cotangent: float32 [512, 48, 2, 128], P('stream', 'band'), may hold values from -6 to 6
- splitter: float32 [48, 256, 128], P('band', 'stream'), may hold values from -0.375 to 0.375
- widener: float32 [48, 128, 512], P('band', None, 'stream'), may hold values from -0.5 to 0.5
- masker: float32 [48, 512, 512], P('band', 'stream'), may hold values from -0.25 to 0.25
- banding: float32 [48, 1920], P('band', 'stream'), may hold values from -1.5 to 1.5
- intake: float32 [2, 2, 128, 1024], P(None, None, None, 'stream'), may hold values from -0.5 to 0.5
- recurrence: float32 [2, 2, 256, 1024], P(None, None, None, 'stream'), may hold values from -0.375 to 0.375
- outtake: float32 [2, 512, 128], P(None, 'stream'), may hold values from -0.25 to 0.25
- scalers: float32 [2, 2432], P(None, 'stream'), may hold values from -1.5 to 1.5
- splitter_first_moment: float32 [48, 256, 128], P('band', 'stream'), may hold values from -0.001953125 to 0.001953125
- widener_first_moment: float32 [48, 128, 512], P('band', None, 'stream'), may hold values from -0.001953125 to 0.001953125
- masker_first_moment: float32 [48, 512, 512], P('band', 'stream'), may hold values from -0.001953125 to 0.001953125
- banding_first_moment: float32 [48, 1920], P('band', 'stream'), may hold values from -0.0068359375 to 0.0068359375
- intake_mean: float32 [2, 2, 128, 1024], P(None, None, None, 'stream'), may hold values from -0.001953125 to 0.001953125
- recurrence_mean: float32 [2, 2, 256, 1024], P(None, None, None, 'stream'), may hold values from -0.001953125 to 0.001953125
- outtake_mean: float32 [2, 512, 128], P(None, 'stream'), may hold values from -0.001953125 to 0.001953125
- scalers_mean: float32 [2, 2432], P(None, 'stream'), may hold values from -0.0068359375 to 0.0068359375
- splitter_second_moment: float32 [48, 256, 128], P('band', 'stream'), may hold values from 6.5436584e-10 to 1.0469853e-08
- widener_second_moment: float32 [48, 128, 512], P('band', None, 'stream'), may hold values from 6.5436584e-10 to 1.0469853e-08
- masker_second_moment: float32 [48, 512, 512], P('band', 'stream'), may hold values from 6.5436584e-10 to 1.0469853e-08
- banding_second_moment: float32 [48, 1920], P('band', 'stream'), may hold values from 2.0939707e-08 to 3.1409562e-07
- intake_power: float32 [2, 2, 128, 1024], P(None, None, None, 'stream'), may hold values from 6.5436584e-10 to 1.0469853e-08
- recurrence_power: float32 [2, 2, 256, 1024], P(None, None, None, 'stream'), may hold values from 6.5436584e-10 to 1.0469853e-08
- outtake_power: float32 [2, 512, 128], P(None, 'stream'), may hold values from 6.5436584e-10 to 1.0469853e-08
- scalers_power: float32 [2, 2432], P(None, 'stream'), may hold values from 2.0939707e-08 to 3.1409562e-07
Outputs:
- masks: float32 [512, 48, 2, 128], P('stream', 'band')
- spectrum_grad: float32 [512, 2, 1025], P('stream')
- grad_norm: float32 [], replicated
- fresh_splitter: float32 [48, 256, 128], P('band', 'stream')
- fresh_widener: float32 [48, 128, 512], P('band', None, 'stream')
- fresh_masker: float32 [48, 512, 512], P('band', 'stream')
- fresh_banding: float32 [48, 1920], P('band', 'stream')
- fresh_intake: float32 [2, 2, 128, 1024], P(None, None, None, 'stream')
- fresh_recurrence: float32 [2, 2, 256, 1024], P(None, None, None, 'stream')
- fresh_outtake: float32 [2, 512, 128], P(None, 'stream')
- fresh_scalers: float32 [2, 2432], P(None, 'stream')
- mean_splitter: float32 [48, 256, 128], P('band', 'stream')
- mean_widener: float32 [48, 128, 512], P('band', None, 'stream')
- mean_masker: float32 [48, 512, 512], P('band', 'stream')
- mean_banding: float32 [48, 1920], P('band', 'stream')
- mean_intake: float32 [2, 2, 128, 1024], P(None, None, None, 'stream')
- mean_recurrence: float32 [2, 2, 256, 1024], P(None, None, None, 'stream')
- mean_outtake: float32 [2, 512, 128], P(None, 'stream')
- mean_scalers: float32 [2, 2432], P(None, 'stream')
- power_splitter: float32 [48, 256, 128], P('band', 'stream')
- power_widener: float32 [48, 128, 512], P('band', None, 'stream')
- power_masker: float32 [48, 512, 512], P('band', 'stream')
- power_banding: float32 [48, 1920], P('band', 'stream')
- power_intake: float32 [2, 2, 128, 1024], P(None, None, None, 'stream')
- power_recurrence: float32 [2, 2, 256, 1024], P(None, None, None, 'stream')
- power_outtake: float32 [2, 512, 128], P(None, 'stream')
- power_scalers: float32 [2, 2432], P(None, 'stream')
Inputs may be any that keep to these rules, and one draw needn't show every extreme that they name: Each of the 4 groups holds 1 to 12 bands, and one group holds exactly 12. `segments`: in each stream the clip number never falls; each clip has 1 to 32 frames. The widths sum to 1025; the widest band has exactly 128 bins.
All inputs are finite; a program needn't handle non-finite values.
Results may differ from a plain program's by a relative error of at most 0.0003.
Values sent between devices are 32-bit elements; how exact they have to be, the bound alone decides.
A program may use at most 256 MiB of HBM per device.

v0:
```python
from functools import partial

import jax
import jax.numpy as jnp
from jax import lax
from jax.sharding import PartitionSpec as P

STEP = 10


CLIP_NORM = 5.0
LEARN_RATE = 0.5
BETA_ONE = 0.9
BETA_TWO = 0.999
ADAM_EPS = 1e-06
DECAY_RATE = 0.01
NORM_EPS = 1e-05
VAR_FLOOR = 0.25
MATMUL_PRECISION = lax.Precision.HIGHEST


def group_norm(values, gain_raw, shift):
    center = values - jnp.mean(values, axis=-1, keepdims=True)
    spread = jnp.mean(center * center, axis=-1, keepdims=True)
    return center * lax.rsqrt(spread + NORM_EPS) * (1.0 + gain_raw) + shift


def band_valid(band_widths, wmax):
    offsets = jnp.arange(wmax, dtype=jnp.int32)
    inside = (offsets[None, :] < band_widths[:, None]).astype(jnp.float32)
    return jnp.concatenate([inside, inside], axis=1)


def split_forward(spectrum, weight_matrix, vectors, edges, band_widths, wmax, dmodel):
    frames = spectrum.shape[0]
    counted = edges.shape[0]
    offsets = jnp.arange(wmax, dtype=jnp.int32)
    index = jnp.minimum(edges[:, None] + offsets[None, :], spectrum.shape[2] - 1)
    taken = jnp.take(spectrum, index.reshape(-1), axis=2)
    taken = (
        taken.reshape(frames, 2, counted, wmax)
        .transpose(0, 2, 1, 3)
        .reshape(frames, counted, 2 * wmax)
    )
    valid = band_valid(band_widths, wmax)
    entries = jnp.maximum(2 * band_widths, 1).astype(jnp.float32)
    center_mean = jnp.sum(taken * valid, axis=-1) / entries
    center = (taken - center_mean[..., None]) * valid
    spread = jnp.sum(center * center, axis=-1) / entries
    width_two = 2 * wmax
    scaled = center * lax.rsqrt(jnp.maximum(spread, VAR_FLOOR))[..., None]
    normalized_rows = (
        scaled * (1.0 + vectors[:, :width_two]) + vectors[:, width_two : 2 * width_two]
    ) * valid
    projected_rows = jnp.einsum(
        "vwc,wco->vwo", normalized_rows, weight_matrix, precision=MATMUL_PRECISION
    )
    return projected_rows + vectors[:, 2 * width_two : 2 * width_two + dmodel]


def module_gates(values, vector, w_in, dmodel, hidden):
    normalized_rows = group_norm(values, vector[:dmodel], vector[dmodel : 2 * dmodel])
    gates = jnp.einsum("lbd,edk->lebk", normalized_rows, w_in, precision=MATMUL_PRECISION)
    gates = gates + vector[2 * dmodel : 2 * dmodel + 8 * hidden].reshape(2, 1, 4 * hidden)
    return jnp.stack([gates[:, 0], jnp.flip(gates[:, 1], 0)], axis=1)


def module_output(values, states, w_out, vector, dmodel, hidden):
    joined = jnp.concatenate([states[:, 0], jnp.flip(states[:, 1], 0)], axis=-1)
    mixed_in = jnp.einsum("lbj,jd->lbd", joined, w_out, precision=MATMUL_PRECISION)
    return values + mixed_in + vector[2 * dmodel + 8 * hidden :]


def recur_forward(gates, w_rec, keep):
    hidden = w_rec.shape[1]
    start = jnp.zeros((2, gates.shape[2], hidden), jnp.float32)

    def advance(carry, inputs):
        states, memory = carry
        drive, kept = inputs
        prior = states * kept[:, None, None]
        total = drive + jnp.einsum("ebh,ehk->ebk", prior, w_rec, precision=MATMUL_PRECISION)
        ingate = jax.nn.sigmoid(total[..., :hidden])
        forget = jax.nn.sigmoid(total[..., hidden : 2 * hidden])
        candidate = jnp.tanh(total[..., 2 * hidden : 3 * hidden])
        outgate = jax.nn.sigmoid(total[..., 3 * hidden :])
        memory_new = forget * memory * kept[:, None, None] + ingate * candidate
        states_new = outgate * jnp.tanh(memory_new)
        activity = jnp.concatenate([ingate, forget, candidate, outgate], axis=-1)
        return ((states_new, memory_new), (states_new, memory_new, activity))

    unused, outputs = lax.scan(advance, (start, start), (gates, keep), unroll=8)
    return outputs


def recur_backward(grad_states, states, memories, activity, keep, w_rec):
    hidden = w_rec.shape[1]
    zero_row = jnp.zeros_like(states[:1])
    previous = jnp.concatenate([zero_row, states[:-1]], axis=0) * keep[:, :, None, None]
    earlier = jnp.concatenate([zero_row, memories[:-1]], axis=0) * keep[:, :, None, None]

    def retreat(carry, inputs):
        grad_hidden, grad_memory = carry
        grad_out, memory_now, gates_now, prior_memory, kept = inputs
        ingate = gates_now[..., :hidden]
        forget = gates_now[..., hidden : 2 * hidden]
        candidate = gates_now[..., 2 * hidden : 3 * hidden]
        outgate = gates_now[..., 3 * hidden :]
        squashed = jnp.tanh(memory_now)
        total_hidden = grad_out + grad_hidden
        total_memory = grad_memory + total_hidden * outgate * (1.0 - squashed * squashed)
        grad_gates = jnp.concatenate(
            [
                total_memory * candidate * ingate * (1.0 - ingate),
                total_memory * prior_memory * forget * (1.0 - forget),
                total_memory * ingate * (1.0 - candidate * candidate),
                total_hidden * squashed * outgate * (1.0 - outgate),
            ],
            axis=-1,
        )
        back_hidden = (
            jnp.einsum("ebk,ehk->ebh", grad_gates, w_rec, precision=MATMUL_PRECISION)
            * kept[:, None, None]
        )
        back_memory = total_memory * forget * kept[:, None, None]
        return ((back_hidden, back_memory), grad_gates)

    start = jnp.zeros_like(states[0])
    unused, grad_gates = lax.scan(
        retreat,
        (start, start),
        (grad_states, memories, activity, earlier, keep),
        reverse=True,
        unroll=8,
    )
    grad_rec = jnp.einsum("lebh,lebk->ehk", previous, grad_gates, precision=MATMUL_PRECISION)
    return (grad_gates, grad_rec)


def module_forward(values, vector, w_in, w_rec, w_out, keep, dmodel, hidden):
    gates, gates_back = jax.vjp(
        partial(module_gates, dmodel=dmodel, hidden=hidden), values, vector, w_in
    )
    states, memories, activity = recur_forward(gates, w_rec, keep)
    result, output_back = jax.vjp(
        partial(module_output, dmodel=dmodel, hidden=hidden), values, states, w_out, vector
    )
    return (result, (gates_back, output_back, states, memories, activity))


def module_backward(grad_result, saved, keep, w_rec):
    gates_back, output_back, states, memories, activity = saved
    grad_values, grad_states, grad_out, grad_vector = output_back(grad_result)
    grad_gates, grad_rec = recur_backward(grad_states, states, memories, activity, keep, w_rec)
    more_values, more_vector, grad_in = gates_back(grad_gates)
    return (grad_values + more_values, grad_in, grad_rec, grad_out, grad_vector + more_vector)


def mask_forward(values, vectors, w_wide, w_mask, valid, wmax, dmodel, mlp):
    width_two = 2 * wmax
    base = 2 * width_two + dmodel
    normalized_rows = group_norm(
        values, vectors[:, base : base + dmodel], vectors[:, base + dmodel : base + 2 * dmodel]
    )
    widened = jnp.einsum("tsd,sdm->tsm", normalized_rows, w_wide, precision=MATMUL_PRECISION)
    widened = jnp.tanh(widened + vectors[:, base + 2 * dmodel : base + 2 * dmodel + mlp])
    raw_out = jnp.einsum("tsm,smk->tsk", widened, w_mask, precision=MATMUL_PRECISION)
    raw_out = raw_out + vectors[:, base + 2 * dmodel + mlp :]
    result = raw_out[..., :width_two] * jax.nn.sigmoid(raw_out[..., width_two:]) * valid
    return result.reshape(values.shape[0], values.shape[1], 2, wmax)


def keep_flags(segment_row):
    same = (segment_row[1:] == segment_row[:-1]).astype(jnp.float32)
    leading = jnp.zeros((1,), jnp.float32)
    return jnp.stack(
        [jnp.concatenate([leading, same]), jnp.concatenate([leading, jnp.flip(same, 0)])], axis=1
    )


def lamb_moments(gradient, mean_old, power_old, factor):
    clipped = gradient * factor
    mean_new = BETA_ONE * mean_old + (1.0 - BETA_ONE) * clipped
    power_new = BETA_TWO * power_old + (1.0 - BETA_TWO) * clipped * clipped
    return (mean_new, power_new)


def lamb_direction(weight_matrix, mean_new, power_new, decay):
    corrected = mean_new / (1.0 - BETA_ONE**STEP)
    scale_root = jnp.sqrt(power_new / (1.0 - BETA_TWO**STEP)) + ADAM_EPS
    return corrected / scale_root + decay * weight_matrix


def body(
    spectrum,
    segments,
    widths,
    groups,
    cotangent,
    splitter,
    widener,
    masker,
    banding,
    intake,
    recurrence,
    outtake,
    scalers,
    splitter_first_moment,
    widener_first_moment,
    masker_first_moment,
    banding_first_moment,
    intake_mean,
    recurrence_mean,
    outtake_mean,
    scalers_mean,
    splitter_second_moment,
    widener_second_moment,
    masker_second_moment,
    banding_second_moment,
    intake_power,
    recurrence_power,
    outtake_power,
    scalers_power,
):
    gathered = (
        lax.all_gather(splitter, "stream", axis=1, tiled=True),
        lax.all_gather(widener, "stream", axis=2, tiled=True),
        lax.all_gather(masker, "stream", axis=1, tiled=True),
        lax.all_gather(banding, "stream", axis=1, tiled=True),
        lax.all_gather(intake, "stream", axis=3, tiled=True),
        lax.all_gather(recurrence, "stream", axis=3, tiled=True),
        lax.all_gather(outtake, "stream", axis=1, tiled=True),
        lax.all_gather(scalers, "stream", axis=1, tiled=True),
    )
    w_split, w_wide, w_mask, v_band, w_in, w_rec, w_out, v_rnn = gathered
    group_count = lax.axis_size("band")
    my_group = lax.axis_index("band")
    slots = splitter.shape[0]
    frames = spectrum.shape[0]
    quarter = frames // group_count
    wmax = w_split.shape[1] // 2
    dmodel = w_split.shape[2]
    hidden = w_rec.shape[2]
    mlp_width = w_wide.shape[2]
    members = (groups[:, None] == jnp.arange(group_count, dtype=jnp.int32)[None, :]).astype(
        jnp.int32
    )
    ranking = jnp.sum(jnp.cumsum(members, axis=0) * members, axis=1) - 1
    band_slot_index = groups * slots + ranking
    all_slots = jnp.arange(group_count * slots, dtype=jnp.int32)
    placing = (band_slot_index[None, :] == all_slots[:, None]).astype(jnp.float32)
    local_slots = my_group * slots + jnp.arange(slots, dtype=jnp.int32)
    owned = (band_slot_index[None, :] == local_slots[:, None]).astype(jnp.int32)
    edges = jnp.cumsum(widths) - widths
    slot_edges = jnp.sum(owned * edges[None, :], axis=1)
    slot_widths = jnp.sum(owned * widths[None, :], axis=1)
    valid = band_valid(slot_widths, wmax)
    time_keep = keep_flags(segments[0])
    band_keep = jnp.ones((widths.shape[0], 2), jnp.float32)
    split_fn = partial(
        split_forward, edges=slot_edges, band_widths=slot_widths, wmax=wmax, dmodel=dmodel
    )
    embedded, split_back = jax.vjp(split_fn, spectrum, w_split, v_band)
    time_out, time_saved = module_forward(
        embedded, v_rnn[0], w_in[0], w_rec[0], w_out[0], time_keep, dmodel, hidden
    )
    arrived = lax.all_to_all(
        time_out.reshape(group_count, quarter, slots, dmodel),
        "band",
        split_axis=0,
        concat_axis=2,
        tiled=True,
    )
    band_in = jnp.einsum(
        "tsd,sb->btd",
        arrived.reshape(quarter, group_count * slots, dmodel),
        placing,
        precision=MATMUL_PRECISION,
    )
    band_out, band_saved = module_forward(
        band_in, v_rnn[1], w_in[1], w_rec[1], w_out[1], band_keep, dmodel, hidden
    )
    leaving = jnp.einsum("btd,sb->tsd", band_out, placing, precision=MATMUL_PRECISION)
    returned = lax.all_to_all(
        leaving.reshape(quarter, group_count, slots, dmodel),
        "band",
        split_axis=1,
        concat_axis=0,
        tiled=True,
    )
    mixed = returned.reshape(frames, slots, dmodel)
    mask_fn = partial(mask_forward, valid=valid, wmax=wmax, dmodel=dmodel, mlp=mlp_width)
    masks, mask_pullback = jax.vjp(mask_fn, mixed, v_band, w_wide, w_mask)
    mixture_gradient, mask_vector_gradient, widened_gradient, mask_gradient = mask_pullback(
        cotangent
    )
    grad_arrive = lax.all_to_all(
        mixture_gradient.reshape(group_count, quarter, slots, dmodel),
        "band",
        split_axis=0,
        concat_axis=2,
        tiled=True,
    )
    grad_band_out = jnp.einsum(
        "tsd,sb->btd",
        grad_arrive.reshape(quarter, group_count * slots, dmodel),
        placing,
        precision=MATMUL_PRECISION,
    )
    grad_band_in, band_gin, band_grec, band_gout, band_gvec = module_backward(
        grad_band_out, band_saved, band_keep, w_rec[1]
    )
    grad_leave = jnp.einsum("btd,sb->tsd", grad_band_in, placing, precision=MATMUL_PRECISION)
    grad_back = lax.all_to_all(
        grad_leave.reshape(quarter, group_count, slots, dmodel),
        "band",
        split_axis=1,
        concat_axis=0,
        tiled=True,
    )
    grad_time_out = grad_back.reshape(frames, slots, dmodel)
    grad_embedded, time_gin, time_grec, time_gout, time_gvec = module_backward(
        grad_time_out, time_saved, time_keep, w_rec[0]
    )
    grad_spectrum, grad_split, split_vector_gradient = split_back(grad_embedded)
    spectrum_grad = lax.psum(grad_spectrum, "band")
    band_vector_gradient = split_vector_gradient + mask_vector_gradient
    rnn_in_grad = jnp.stack([time_gin, band_gin])
    rnn_rec_grad = jnp.stack([time_grec, band_grec])
    rnn_out_grad = jnp.stack([time_gout, band_gout])
    rnn_vec_grad = jnp.stack([time_gvec, band_gvec])
    rnn_in_grad, rnn_rec_grad, rnn_out_grad, rnn_vec_grad = lax.psum(
        (rnn_in_grad, rnn_rec_grad, rnn_out_grad, rnn_vec_grad), "band"
    )
    reduced = (
        lax.psum_scatter(grad_split, "stream", scatter_dimension=1, tiled=True),
        lax.psum_scatter(widened_gradient, "stream", scatter_dimension=2, tiled=True),
        lax.psum_scatter(mask_gradient, "stream", scatter_dimension=1, tiled=True),
        lax.psum_scatter(band_vector_gradient, "stream", scatter_dimension=1, tiled=True),
        lax.psum_scatter(rnn_in_grad, "stream", scatter_dimension=3, tiled=True),
        lax.psum_scatter(rnn_rec_grad, "stream", scatter_dimension=3, tiled=True),
        lax.psum_scatter(rnn_out_grad, "stream", scatter_dimension=1, tiled=True),
        lax.psum_scatter(rnn_vec_grad, "stream", scatter_dimension=1, tiled=True),
    )
    weights = (splitter, widener, masker, banding, intake, recurrence, outtake, scalers)
    means_old = (
        splitter_first_moment,
        widener_first_moment,
        masker_first_moment,
        banding_first_moment,
        intake_mean,
        recurrence_mean,
        outtake_mean,
        scalers_mean,
    )
    powers_old = (
        splitter_second_moment,
        widener_second_moment,
        masker_second_moment,
        banding_second_moment,
        intake_power,
        recurrence_power,
        outtake_power,
        scalers_power,
    )
    shares = (
        1.0,
        1.0,
        1.0,
        1.0,
        1.0 / group_count,
        1.0 / group_count,
        1.0 / group_count,
        1.0 / group_count,
    )
    decays = (DECAY_RATE, DECAY_RATE, DECAY_RATE, 0.0, DECAY_RATE, DECAY_RATE, DECAY_RATE, 0.0)
    grad_squares = jnp.float32(0.0)
    weight_list = []
    for position in range(8):
        grad_squares = (
            grad_squares + jnp.sum(reduced[position] * reduced[position]) * shares[position]
        )
        weight_list.append(jnp.sum(weights[position] * weights[position]) * shares[position])
    totals = lax.psum((grad_squares, jnp.stack(weight_list)), ("band", "stream"))
    grad_norm = jnp.sqrt(totals[0])
    factor = jnp.minimum(1.0, CLIP_NORM / grad_norm)
    mean_list = []
    power_list = []
    direction_list = []
    update_list = []
    for position in range(8):
        mean_new, power_new = lamb_moments(
            reduced[position], means_old[position], powers_old[position], factor
        )
        direction = lamb_direction(weights[position], mean_new, power_new, decays[position])
        mean_list.append(mean_new)
        power_list.append(power_new)
        direction_list.append(direction)
        update_list.append(jnp.sum(direction * direction) * shares[position])
    update_totals = lax.psum(jnp.stack(update_list), ("band", "stream"))
    ratios = jnp.sqrt(totals[1]) / jnp.sqrt(update_totals + 1e-12)
    fresh_list = []
    for position in range(8):
        fresh_list.append(
            weights[position] - LEARN_RATE * ratios[position] * direction_list[position]
        )
    return (
        masks,
        spectrum_grad,
        grad_norm,
        fresh_list[0],
        fresh_list[1],
        fresh_list[2],
        fresh_list[3],
        fresh_list[4],
        fresh_list[5],
        fresh_list[6],
        fresh_list[7],
        mean_list[0],
        mean_list[1],
        mean_list[2],
        mean_list[3],
        mean_list[4],
        mean_list[5],
        mean_list[6],
        mean_list[7],
        power_list[0],
        power_list[1],
        power_list[2],
        power_list[3],
        power_list[4],
        power_list[5],
        power_list[6],
        power_list[7],
    )


def solution(mesh):
    return jax.shard_map(
        body,
        mesh=mesh,
        in_specs=(
            P("stream", None, None),
            P("stream", None),
            P(),
            P(),
            P("stream", "band", None, None),
            P("band", "stream", None),
            P("band", None, "stream"),
            P("band", "stream", None),
            P("band", "stream"),
            P(None, None, None, "stream"),
            P(None, None, None, "stream"),
            P(None, "stream", None),
            P(None, "stream"),
            P("band", "stream", None),
            P("band", None, "stream"),
            P("band", "stream", None),
            P("band", "stream"),
            P(None, None, None, "stream"),
            P(None, None, None, "stream"),
            P(None, "stream", None),
            P(None, "stream"),
            P("band", "stream", None),
            P("band", None, "stream"),
            P("band", "stream", None),
            P("band", "stream"),
            P(None, None, None, "stream"),
            P(None, None, None, "stream"),
            P(None, "stream", None),
            P(None, "stream"),
        ),
        out_specs=(
            P("stream", "band", None, None),
            P("stream", None, None),
            P(),
            P("band", "stream", None),
            P("band", None, "stream"),
            P("band", "stream", None),
            P("band", "stream"),
            P(None, None, None, "stream"),
            P(None, None, None, "stream"),
            P(None, "stream", None),
            P(None, "stream"),
            P("band", "stream", None),
            P("band", None, "stream"),
            P("band", "stream", None),
            P("band", "stream"),
            P(None, None, None, "stream"),
            P(None, None, None, "stream"),
            P(None, "stream", None),
            P(None, "stream"),
            P("band", "stream", None),
            P("band", None, "stream"),
            P("band", "stream", None),
            P("band", "stream"),
            P(None, None, None, "stream"),
            P(None, None, None, "stream"),
            P(None, "stream", None),
            P(None, "stream"),
        ),
        check_vma=False,
    )
```

profile of v0, /device:TPU:0, one launch (start us, length us, event | category | flops | bytes accessed | tf_op | source)
XLA Modules:
  0.0 1686.0 jit_solution(7849000215804226358)
XLA Ops:
  11.8 15.9 all-gather
  28.6 13.9 all-gather.1
  45.6 5.2 gather_fusion
  56.8 18.0 %all_gather.29 = f32[2,512,128]{2,1,0:T(8,128)} all-gather(f32[2,64,128]{2,1,0:T(8,128)S(1)} %copy-done.80), channel_id=1, replica_groups=mesh['band'=4,'stream'=8] {'stream'}, dimensions={1}, use_global_device_ids=true | all-gather | bytes 589824 | tf_op jit(solution)/shard_map/all_gather | solution.py:232
  78.2 6.5 add_bitcast_fusion
  87.9 6.3 rev.36
  94.2 3.9 copy.421
  99.9 4.2 pad_maximum_fusion.33
  104.2 16.9 %all-gather.12.cloned.1.call-done = f32[2,2,256,1024]{3,2,1,0:T(8,128)} async-done(((f32[2,2,256,128]{3,2,1,0:T(8,128)}), f32[2,2,256,1024]{3,2,1,0:T(8,128)}) %all-gather.12.cloned.1.call-update) | async-done | bytes 4194320 | tf_op jit(solution)/shard_map/all_gather | solution.py:231
  121.0 4.1 slice_bitcast_fusion.21
  125.2 4.4 broadcast.504.clone
  129.6 205.3 %while.76 = (s32[]{:T(128)}, f32[2,12,256]{2,1,0:T(8,128)S(1)}, f32[2,12,256]{2,1,0:T(8,128)S(1)}, f32[8,8,2,12,256]{4,1,0,3,2:T(8,128)}, f32[8,8,2,12,256]{4,3,...) while((s32[]{:T(128)}, f32[2,12,256]{2,1,0:T(8,128)S(1)}, ...), condition=%wide.region_10.11_spmd.clone, body=%wide.region_9.10_spmd.clone.sunk | while | flops 606130176 | bytes 28563560 | solution.py:92
  342.5 4.5 all-to-all-start
  357.9 5.7 add_bitcast_fusion.1
  369.1 148.3 %while.77 = (s32[]{:T(128)}, f32[2,16,256]{2,1,0:T(8,128)S(1)}, f32[2,16,256]{2,1,0:T(8,128)S(1)}, f32[5,8,2,16,256]{4,1,0,3,2:T(8,128)}, f32[5,8,2,16,256]{4,3,...) while((s32[]{:T(128)}, f32[2,16,256]{2,1,0:T(8,128)S(1)}, ...), condition=%wide.region_14.15_spmd.clone, body=%wide.region_13.14_spmd.clone.sunk | while | flops 808042496 | bytes 30967664 | solution.py:92
  528.0 4.0 all-to-all-start.1
  539.6 6.6 add_tanh_fusion
  546.2 11.8 add_bitcast_fusion.3
  559.6 12.9 fusion.303
  577.8 3.5 all-to-all-start.2
  581.4 5.7 pad_maximum_fusion.35
  596.5 164.6 %while.78 = (s32[]{:T(128)}, f32[2,16,256]{2,1,0:T(8,128)}, f32[2,16,256]{2,1,0:T(8,128)}, f32[5,8,2,16,1024]{4,1,0,3,2:T(8,128)}, f32[5,8,2,16,256]{4,3,2,1,0:T...) while((s32[]{:T(128)}, f32[2,16,256]{2,1,0:T(8,128)}, ...), condition=%wide.region_20.21_spmd.clone, body=%wide.region_19.20_spmd.clone.sunk | while | flops 808394752 | bytes 36995532 | solution.py:129
  600.1 3.5 subtract_multiply_fusion.73
  632.9 3.5 subtract_multiply_fusion.73
  665.7 3.5 subtract_multiply_fusion.73
  698.6 3.5 subtract_multiply_fusion.73
  731.4 3.5 subtract_multiply_fusion.73
  763.1 4.1 fusion.300
  767.2 6.4 rev.42
  773.7 8.9 fusion.470
  785.2 4.1 all-to-all-start.3
  789.4 13.7 fusion.317
  803.1 3.4 fusion.341
  818.2 4.4 broadcast.504
  822.6 244.4 %while.79 = (s32[]{:T(128)}, f32[2,12,256]{2,1,0:T(8,128)}, f32[2,12,256]{2,1,0:T(8,128)}, f32[8,8,2,12,1024]{4,3,2,1,0:T(8,128)}, f32[8,8,2,12,256]{4,1,0,3,2:T...) while((s32[]{:T(128)}, f32[2,12,256]{2,1,0:T(8,128)}, ...), condition=%wide.region_24.25_spmd.clone, body=%wide.region_23.24_spmd.clone.sunk | while | flops 606400512 | bytes 28468312 | solution.py:129
  823.0 3.7 constant_dynamic-slice_fusion.23
  853.5 3.3 constant_dynamic-slice_fusion.23
  883.8 3.7 constant_dynamic-slice_fusion.23
  914.3 4.0 constant_dynamic-slice_fusion.23
  945.2 3.7 constant_dynamic-slice_fusion.23
  975.7 3.6 constant_dynamic-slice_fusion.23
  1006.2 3.5 constant_dynamic-slice_fusion.23
  1036.6 3.4 constant_dynamic-slice_fusion.23
  1067.0 9.7 copy.449
  1077.6 3.9 slice_bitcast_fusion.16
  1081.6 6.2 rev.44
  1087.9 13.1 fusion.320
  1103.5 8.9 fusion.301
  1112.4 7.9 convolution_bitcast_fusion
  1124.2 4.9 fusion.467
  1129.2 7.4 fusion.466
  1137.7 8.2 fusion.469
  1148.6 3.3 fusion.468
  1154.4 4.2 fusion.360
  1158.7 7.8 fusion.362
  1174.0 157.9 %scatter_fusion = f32[64,2,1025]{0,1,2:T(2,128)} fusion(f32[64,2,1025]{0,1,2:T(2,128)} %broadcast_in_dim.459, s32[1536]{0:T(1024)S(1)} %copy-done.131, f32[1536,64,2]{1,2,0:T(2,128)} %bitcast.1315), kind=kCustom, calls=%fused_computation.1 | custom fusion | flops 196608 | bytes 2365440 | tf_op jit(solution)/shard_map/transpose(jvp(jit(_take)))/scatter-add | solution.py:39
  1332.0 13.5 fusion.304
  1350.4 7.9 psum.67
  1366.0 41.8 %all-reduce.30.cloned.1.call-done = (f32[64,2,1025]{0,1,2:T(2,128)}, f32[2,2,128,128]{2,3,1,0:T(8,128)}, f32[2,2,256,128]{3,2,1,0:T(8,128)}, f32[2,64,128]{2,1,0:T(8,128)}) async-done(((f32[64,2,1025]{0,1,2:T(2,128)}, f32[2,2,128,128]{2,3,1,0:T(8,128)}, f32[2,2,256,128]{3,2,1,0:T(8,128)}, f32[2,64,128]{2,1,0:T(8,128)}), (f32[64,2,1025]{0,1,2:T(2,128)}, f32[2,2,128,128]{2,3,1,0:T(8,128)}, ...) | async-done | bytes 1376784 | tf_op jit(solution)/shard_map/psum | solution.py:326
  1414.7 124.8 %reduce-scatter.17.cloned.1.call-done = f32[12,64,512]{2,1,0:T(8,128)} async-done(((f32[12,512,512]{2,1,0:T(8,128)}), f32[12,64,512]{2,1,0:T(8,128)}) %reduce-scatter.17.cloned.1.call-update) | async-done | bytes 1572880 | tf_op jit(solution)/shard_map/reduce_scatter | solution.py:338
  1544.4 37.7 %psum.61 = f32[]{:T(128)} all-reduce(f32[]{:T(128)S(6)} %add.1176), channel_id=1, replica_groups=mesh['band'=4,'stream'=8] {'band','stream'}, use_global_device_ids=true, to_apply=%region_66.67 | all-reduce | flops 1 | bytes 8 | tf_op jit(solution)/shard_map/psum | solution.py:384
  1596.4 6.0 multiply_reduce_fusion.1
  1614.2 41.5 %all-reduce.26 = (f32[8]{0:T(128)S(1)}, f32[8]{0:T(128)S(1)}) all-reduce(f32[8]{0:T(128)S(1)} %stack.159, f32[8]{0:T(128)S(1)} %stack.150), channel_id=1, replica_groups=mesh['band'=4,'stream'=8] {'band','stream'}, use_global_device_ids=true, to_apply=%region_84.85 | all-reduce | flops 16 | bytes 128 | tf_op jit(solution)/shard_map/psum | solution.py:400
  1672.4 3.9 multiply_subtract_fusion
  (1770 shorter events, 878.7 us)
Async XLA Ops:
  7.2 21.3 %copy-start.143 = (f32[2,304]{1,0:T(2,128)S(1)}, f32[2,304]{1,0:T(2,128)}, u32[]{:S(2)}) copy-start(f32[2,304]{1,0:T(2,128)} %param.49) | copy-start | bytes 7300
  7.2 37.3 %copy-start.83 = (f32[64,2,1025]{2,1,0:T(2,128)S(1)}, f32[64,2,1025]{2,1,0:T(2,128)}, u32[]{:S(2)}) copy-start(f32[64,2,1025]{2,1,0:T(2,128)} %param.37) | copy-start | bytes 1574404
  7.3 67.6 %all-gather.8.cloned.1.call-start = ((), (), s32[]{:S(2)}) async-start(), calls=%async_computation.12 | async-start | bytes 1769472 | tf_op jit(solution)/shard_map/all_gather | solution.py:226
  8.0 70.1 %all-gather.10.cloned.1.call-start = ((), (), s32[]{:S(2)}) async-start(), calls=%async_computation.13 | async-start | bytes 2359296 | tf_op jit(solution)/shard_map/all_gather | solution.py:230
  8.7 112.3 %all-gather.12.cloned.1.call-start = ((), (), s32[]{:S(2)}) async-start(), calls=%async_computation.14 | async-start | bytes 4718592 | tf_op jit(solution)/shard_map/all_gather | solution.py:231
  9.5 530.1 %all-gather.14.cloned.1.call-start = ((), (), s32[]{:S(2)}) async-start(), calls=%async_computation.15 | async-start | bytes 3538944 | tf_op jit(solution)/shard_map/all_gather | solution.py:227
  10.1 536.1 %all-gather.16.cloned.1.call-start = ((), (), s32[]{:S(2)}) async-start(), calls=%async_computation.16 | async-start | bytes 14155776 | tf_op jit(solution)/shard_map/all_gather | solution.py:228
  11.7 42.6 %copy-start.157 = (f32[12]{0:T(128)}, f32[12]{0:T(128)S(1)}, u32[]{:S(2)}) copy-start(f32[12]{0:T(128)S(1)} %maximum_convert_fusion) | copy-start | bytes 148
  27.9 46.9 %copy-start.78 = (f32[12,256]{1,0:T(8,128)}, f32[12,256]{1,0:T(8,128)S(1)}, u32[]{:S(2)}) copy-start(f32[12,256]{1,0:T(8,128)S(1)} %get-tuple-element.1430) | copy-start | bytes 36868
  28.0 46.9 %copy-start.107 = (f32[12,256]{1,0:T(8,128)}, f32[12,256]{1,0:T(8,128)S(1)}, u32[]{:S(2)}) copy-start(f32[12,256]{1,0:T(8,128)S(1)} %get-tuple-element.1431) | copy-start | bytes 36868
  43.2 35.0 %copy-start.145 = (f32[128]{0:T(128)}, f32[128]{0:T(128)S(1)}, u32[]{:S(2)}) copy-start(f32[128]{0:T(128)S(1)} %get-tuple-element.1437) | copy-start | bytes 1540
  43.2 35.0 %copy-start.159 = (f32[128]{0:T(128)}, f32[128]{0:T(128)S(1)}, u32[]{:S(2)}) copy-start(f32[128]{0:T(128)S(1)} %get-tuple-element.1436) | copy-start | bytes 1540
  53.2 21.7 %copy-start.84 = (f32[64,12]{0,1:T(8,128)}, f32[64,12]{0,1:T(8,128)S(1)}, u32[]{:S(2)}) copy-start(f32[64,12]{0,1:T(8,128)S(1)} %broadcast_divide_fusion.1) | copy-start | bytes 9220
  54.4 23.3 %copy-start.132 = (f32[64,12]{0,1:T(8,128)}, f32[64,12]{0,1:T(8,128)S(1)}, u32[]{:S(2)}) copy-start(f32[64,12]{0,1:T(8,128)S(1)} %copy.417) | copy-start | bytes 9220
  54.4 23.3 %copy-start.97 = (f32[64,12]{0,1:T(8,128)}, f32[64,12]{0,1:T(8,128)S(1)}, u32[]{:S(2)}) copy-start(f32[64,12]{0,1:T(8,128)S(1)} %maximum_rsqrt_fusion) | copy-start | bytes 9220
  55.1 29.6 %copy-start.5 = (f32[64,12,256]{2,0,1:T(8,128)}, f32[64,12,256]{2,0,1:T(8,128)S(1)}, u32[]{:S(2)}) copy-start(f32[64,12,256]{2,0,1:T(8,128)S(1)} %reshape.728) | copy-start | bytes 2359300
  342.5 11.9 all-to-all-start
  528.0 10.7 all-to-all-start.1
  539.4 37.1 %copy-start.99 = (f32[64,12]{0,1:T(8,128)}, f32[64,12]{0,1:T(8,128)S(1)}, u32[]{:S(2)}) copy-start(f32[64,12]{0,1:T(8,128)S(1)} %rsqrt.41) | copy-start | bytes 9220
  539.5 37.0 %copy-start.92 = (f32[64,12]{0,1:T(8,128)}, f32[64,12]{0,1:T(8,128)S(1)}, u32[]{:S(2)}) copy-start(f32[64,12]{0,1:T(8,128)S(1)} %div.386) | copy-start | bytes 9220
  546.2 11.8 copy-start.52
  546.2 13.0 copy-start.3
  559.2 13.3 copy-start.17
  559.2 13.3 copy-start.20
  559.6 13.0 copy-start.22
  577.8 9.3 all-to-all-start.2
  763.1 26.3 %copy-start.69 = (f32[1,2,16,1024]{3,0,2,1:T(1,128)}, f32[1,2,16,1024]{3,0,2,1:T(1,128)S(1)}, u32[]{:S(2)}) copy-start(f32[1,2,16,1024]{3,0,2,1:T(1,128)S(1)} %copy.442) | copy-start | bytes 393220
  773.7 9.0 copy-start.137
  773.7 9.0 copy-start.113
  773.7 9.9 copy-start.40
  773.7 9.9 copy-start.154
  785.2 21.3 %all-to-all-start.3 = ((f32[16,4,12,128]{3,0,2,1:T(8,128)}), f32[16,4,12,128]{3,0,2,1:T(8,128)}, u32[]{:S(2)}, u32[]{:S(2)}) async-start(f32[16,4,12,128]{3,0,2,1:T(8,128)} %bitcast.88), calls=%async_computation.3 | async-start | bytes 786432 | tf_op jit(solution)/shard_map/all_to_all | solution.py:314
  789.3 542.5 %reduce-scatter.23.cloned.1.call-start = ((), (), s32[]{:S(2)}) async-start(), calls=%async_computation.22 | async-start | bytes 589824 | tf_op jit(solution)/shard_map/reduce_scatter | solution.py:342
  789.4 13.7 copy-start.32
  789.4 13.7 copy-start.34
  789.4 13.7 copy-start.41
  1067.0 9.7 copy-start.71
  1067.0 9.7 copy-start.72
  1077.6 254.3 %reduce-scatter.19.cloned.1.call-start = ((), (), s32[]{:S(2)}) async-start(), calls=%async_computation.20 | async-start | bytes 2359296 | tf_op jit(solution)/shard_map/reduce_scatter | solution.py:340
  1087.9 13.1 copy-start.74
  1102.7 9.7 copy-start.63
  1102.7 9.7 copy-start.162
  1102.7 229.2 %reduce-scatter.21.cloned.1.call-start = ((), (), s32[]{:S(2)}) async-start(), calls=%async_computation.21 | async-start | bytes 4718592 | tf_op jit(solution)/shard_map/reduce_scatter | solution.py:341
  1122.7 226.7 %reduce-scatter.27.cloned.1.call-start = ((), (), s32[]{:S(2)}) async-start(), calls=%async_computation.24 | async-start | bytes 1400832
  1152.1 207.5 %reduce-scatter.25.cloned.1.call-start = ((), (), s32[]{:S(2)}) async-start(), calls=%async_computation.23 | async-start | bytes 1105920
  1154.2 207.0 %reduce-scatter.13.cloned.1.call-start = ((), (), s32[]{:S(2)}) async-start(), calls=%async_computation.17 | async-start | bytes 1769472 | tf_op jit(solution)/shard_map/reduce_scatter | solution.py:336
  1158.6 204.2 %reduce-scatter.15.cloned.1.call-start = ((), (), s32[]{:S(2)}) async-start(), calls=%async_computation.18 | async-start | bytes 3538944 | tf_op jit(solution)/shard_map/reduce_scatter | solution.py:337
  1166.6 241.2 %all-reduce.30.cloned.1.call-start = ((), (), s32[]{:S(2)}) async-start(), calls=%async_computation.25 | async-start | bytes 3803136 | tf_op jit(solution)/shard_map/psum | solution.py:326
  1174.0 158.0 %copy-start.19 = (f32[64,12,256]{2,0,1:T(8,128)S(1)}, f32[64,12,256]{2,0,1:T(8,128)}, u32[]{:S(2)}) copy-start(f32[64,12,256]{2,0,1:T(8,128)} %copy-done.17) | copy-start | bytes 2359300
  1331.9 207.6 %reduce-scatter.17.cloned.1.call-start = ((), (), s32[]{:S(2)}) async-start(), calls=%async_computation.19 | async-start | bytes 14155776 | tf_op jit(solution)/shard_map/reduce_scatter | solution.py:338
  1364.5 218.3 %copy-start.144 = (f32[2,304]{1,0:T(2,128)S(1)}, f32[2,304]{1,0:T(2,128)}, u32[]{:S(2)}) copy-start(f32[2,304]{1,0:T(2,128)} %param.49) | copy-start | bytes 7300
  1364.5 218.3 %copy-start.163 = (f32[2,304]{1,0:T(2,128)S(1)}, f32[2,304]{1,0:T(2,128)}, u32[]{:S(2)}) copy-start(f32[2,304]{1,0:T(2,128)} %param.57) | copy-start | bytes 7300
  1364.5 218.3 %copy-start.164 = (f32[2,304]{1,0:T(2,128)S(1)}, f32[2,304]{1,0:T(2,128)}, u32[]{:S(2)}) copy-start(f32[2,304]{1,0:T(2,128)} %param.65) | copy-start | bytes 7300
  1364.5 220.2 %copy-start.81 = (f32[2,64,128]{2,1,0:T(8,128)S(1)}, f32[2,64,128]{2,1,0:T(8,128)}, u32[]{:S(2)}) copy-start(f32[2,64,128]{2,1,0:T(8,128)} %param.48) | copy-start | bytes 196612
  1364.5 220.2 %copy-start.138 = (f32[2,64,128]{2,1,0:T(8,128)S(1)}, f32[2,64,128]{2,1,0:T(8,128)}, u32[]{:S(2)}) copy-start(f32[2,64,128]{2,1,0:T(8,128)} %param.56) | copy-start | bytes 196612
  1364.5 220.2 %copy-start.139 = (f32[2,64,128]{2,1,0:T(8,128)S(1)}, f32[2,64,128]{2,1,0:T(8,128)}, u32[]{:S(2)}) copy-start(f32[2,64,128]{2,1,0:T(8,128)} %param.64) | copy-start | bytes 196612
  1407.8 177.0 %copy-start.96 = (f32[2,64,128]{2,1,0:T(8,128)S(1)}, f32[2,64,128]{2,1,0:T(8,128)}, u32[]{:S(2)}) copy-start(f32[2,64,128]{2,1,0:T(8,128)} %get-tuple-element.1120) | copy-start | bytes 196612
  1409.4 177.3 %copy-start.42 = (f32[2,2,256,128]{3,2,1,0:T(8,128)S(1)}, f32[2,2,256,128]{3,2,1,0:T(8,128)}, u32[]{:S(2)}) copy-start(f32[2,2,256,128]{3,2,1,0:T(8,128)} %param.47) | copy-start | bytes 1572868
  1409.4 177.3 %copy-start.61 = (f32[2,2,256,128]{3,2,1,0:T(8,128)S(1)}, f32[2,2,256,128]{3,2,1,0:T(8,128)}, u32[]{:S(2)}) copy-start(f32[2,2,256,128]{3,2,1,0:T(8,128)} %get-tuple-element.1119) | copy-start | bytes 1572868
  1544.4 48.3 %copy-start.73 = (f32[2,2,128,128]{2,3,1,0:T(8,128)S(1)}, f32[2,2,128,128]{2,3,1,0:T(8,128)}, u32[]{:S(2)}) copy-start(f32[2,2,128,128]{2,3,1,0:T(8,128)} %get-tuple-element.1118) | copy-start | bytes 786436
  1586.8 8.4 copy-start.110
  1586.8 9.6 copy-start.13
  1611.2 56.0 %copy-start.82 = (f32[2,64,128]{2,1,0:T(8,128)S(1)}, f32[2,64,128]{2,1,0:T(8,128)}, u32[]{:S(2)}) copy-start(f32[2,64,128]{2,1,0:T(8,128)} %param.48) | copy-start | bytes 196612
  1660.7 10.3 copy-start.111
  (296 other events, 1205.6 us)
Sparse Core Ops, SparseCore 0:
  9.7 28.1 all-gather.7
  39.5 33.6 all-gather.9
  74.8 46.1 all-gather.11
  122.5 36.5 all-gather.13
  160.5 115.5 all-gather.15
  1077.7 29.8 reduce-scatter.22
  1109.9 33.8 reduce-scatter.18
  1146.3 48.7 reduce-scatter.20
  1198.0 31.2 reduce-scatter.26
  1231.5 30.0 reduce-scatter.24
  1264.5 32.5 reduce-scatter.12
  1299.2 38.3 reduce-scatter.14
  1341.1 66.6 all-reduce.29
  1409.9 129.5 reduce-scatter.16
where the time goes:
time: 1710 us; the launch traced here: 1690 us
  matrix products  683 us (40%)
  other arithmetic  382 us (22%)
  local copies, waits for them, and re-layouts  238 us (14%)
  waiting for transfers between devices  190 us (11%)
  blocking collectives  135 us (8%)
  between operations  34.1 us (2%)
    dot_general x104, matrix products, retreat(): jnp.einsum('ebk,ehk->ebh', grad_gates, w_rec, precision=MATMUL_PRECISION)  283 us
    dot_general x105, matrix products, advance(): jnp.einsum('ebh,ehk->ebk', prior, w_rec, precision=MATMUL_PRECISION)  241 us
    scatter-add x1, other arithmetic, split_forward(): taken = jnp.take(spectrum, index.reshape(-1), axis=2)  158 us
    reduce_scatter x1, waiting for transfers between devices, body(): lax.psum_scatter(mask_gradient, 'stream', scatter_dimension=1, tiled=True)  125 us
    while x273, other arithmetic  64.8 us
    dot_general x6, matrix products, module_gates(): jnp.einsum('lbd,edk->lebk', normalized_rows, w_in, precision=MATMUL_PRECI...  56.2 us
    dynamic_update_slice x52, local copies, waits for them, and re-layouts, recur_forward(): unused, outputs = lax.scan(advance, (start, start), (gates, keep), unroll=8)  51.2 us
    psum x1, waiting for transfers between devices, body(): spectrum_grad = lax.psum(grad_spectrum, 'band')  41.8 us
  transfers between devices with their start and end apart: 18, of which 5 were waited for; matrix products, arithmetic and copies ran while one was open for 45% of the time, Pallas kernels for 0%

commit v1 on v0

v1 whole, which is shorter than its diff:
```python
from functools import partial
import math

import jax
import jax.numpy as jnp
from jax import lax
from jax.experimental import pallas as pl
from jax.experimental.pallas import tpu as pltpu
from jax.sharding import PartitionSpec as P

STEP = 10
CLIP_NORM = 5.0
LEARN_RATE = 0.5
BETA_ONE = 0.9
BETA_TWO = 0.999
ADAM_EPS = 1e-06
DECAY_RATE = 0.01
NORM_EPS = 1e-05
VAR_FLOOR = 0.25
CLIPS = 3
CLIP_MOST = 32
LANES = 128
VMEM_BYTES = 60 * 1024 * 1024

AB = (((1,), (0,)), ((), ()))
ABT = (((1,), (1,)), ((), ()))
ATB = (((0,), (0,)), ((), ()))


def split(x):
    hi = x.astype(jnp.bfloat16)
    lo = (x - hi.astype(jnp.float32)).astype(jnp.bfloat16)
    return hi, lo


def dot1(a, b, dims):
    return lax.dot_general(a, b, dims, preferred_element_type=jnp.float32)


def dot_parts(a, b, dims):
    return dot1(a[0], b[0], dims) + (dot1(a[1], b[0], dims) + dot1(a[0], b[1], dims))


def dot3(a, b, dims):
    return dot_parts(split(a), split(b), dims)


def sigmoid(x):
    return 0.5 * jnp.tanh(0.5 * x) + 0.5


def norm_stats(x):
    center = x - jnp.mean(x, axis=-1, keepdims=True)
    spread = jnp.mean(center * center, axis=-1, keepdims=True)
    scale = lax.rsqrt(spread + NORM_EPS)
    return center * scale, scale


def norm_back(grad_unit, unit, scale):
    first = jnp.mean(grad_unit, axis=-1, keepdims=True)
    second = jnp.mean(grad_unit * unit, axis=-1, keepdims=True)
    return scale * (grad_unit - first - unit * second)


def column_sum(x):
    return jnp.sum(x, axis=0, keepdims=True)


def gates_forward(x_flat, act, w_in, vec, rows, block):
    hidden4 = w_in.shape[2]
    dmodel = w_in.shape[1]
    parts = [split(w_in[e]) for e in range(2)]

    def one(r, carry):
        start = pl.multiple_of(r * block, block)
        unit, unused = norm_stats(x_flat(start, block))
        n = split(unit * (1.0 + vec[0:1, :dmodel]) + vec[0:1, dmodel : 2 * dmodel])
        for e in range(2):
            bias = vec[0:1, 2 * dmodel + hidden4 * e : 2 * dmodel + hidden4 * (e + 1)]
            z = dot_parts(n, parts[e], AB) + bias
            act[e][pl.ds(r * (block // 16), block // 16)] = z.reshape(block // 16, 16, hidden4)
        return carry

    lax.fori_loop(0, rows // block, one, 0)


def run_forward(steps, places, act, tc, cp, hp, h, w_rec, hi_ref, lo_ref, state, memory):
    hidden = w_rec.shape[1]
    for e in range(2):
        hi_ref[e], lo_ref[e] = split(w_rec[e])
        state[e][...] = jnp.zeros_like(state[e])
        memory[e][...] = jnp.zeros_like(memory[e])

    def step(j, carry):
        work = []
        for e in range(2):
            at = places(e, j)
            prior = state[e][...]
            hi, lo = split(prior)
            rows = prior.shape[0]
            first = dot1(jnp.concatenate([hi, lo], axis=0), hi_ref[e], AB)
            drive = [act[e][p] for p in at]
            drive = drive[0] if len(drive) == 1 else jnp.concatenate(drive, axis=0)
            z = first[:rows] + first[rows:] + dot1(hi, lo_ref[e], AB) + drive
            work.append((at, prior, z))
        for e in range(2):
            at, prior, z = work[e]
            ingate = sigmoid(z[:, :hidden])
            forget = sigmoid(z[:, hidden : 2 * hidden])
            candidate = jnp.tanh(z[:, 2 * hidden : 3 * hidden])
            outgate = sigmoid(z[:, 3 * hidden :])
            before = memory[e][...]
            now = forget * before + ingate * candidate
            squashed = jnp.tanh(now)
            out = outgate * squashed
            memory[e][...] = now
            state[e][...] = out
            for k, p in enumerate(at):
                part = slice(16 * k, 16 * (k + 1))
                act[e][p, :, :hidden] = ingate[part]
                act[e][p, :, hidden : 2 * hidden] = forget[part]
                act[e][p, :, 2 * hidden : 3 * hidden] = candidate[part]
                act[e][p, :, 3 * hidden :] = outgate[part]
                tc[e][p] = squashed[part]
                cp[e][p] = before[part]
                hp[e][p] = prior[part]
                h[e][p] = out[part]
        return carry

    lax.fori_loop(0, steps, step, 0)


def output_forward(count, h, w_out, vec):
    hidden = h[0].shape[2]
    dmodel = w_out.shape[1]
    total = vec[0:1, vec.shape[1] - dmodel :]
    for e in range(2):
        states = h[e][:count].reshape(count * 16, hidden)
        total = total + dot3(states, w_out[hidden * e : hidden * (e + 1)], AB)
    return total


def run_backward(steps, places, act, dz_ref, tc, cp, dh, w_rec, hi_ref, lo_ref, grad_h, grad_c):
    hidden = w_rec.shape[1]
    for e in range(2):
        hi_ref[e], lo_ref[e] = split(w_rec[e])
        grad_h[e][...] = jnp.zeros_like(grad_h[e])
        grad_c[e][...] = jnp.zeros_like(grad_c[e])

    def load(ref, at):
        got = [ref[p] for p in at]
        return got[0] if len(got) == 1 else jnp.concatenate(got, axis=0)

    def step(back, carry):
        j = steps - 1 - back
        work = []
        for e in range(2):
            at = places(e, j)
            gates = load(act[e], at)
            ingate = gates[:, :hidden]
            forget = gates[:, hidden : 2 * hidden]
            candidate = gates[:, 2 * hidden : 3 * hidden]
            outgate = gates[:, 3 * hidden :]
            squashed = load(tc[e], at)
            before = load(cp[e], at)
            total_h = load(dh[e], at) + grad_h[e][...]
            total_c = grad_c[e][...] + total_h * outgate * (1.0 - squashed * squashed)
            dz = jnp.concatenate(
                [
                    total_c * candidate * ingate * (1.0 - ingate),
                    total_c * before * forget * (1.0 - forget),
                    total_c * ingate * (1.0 - candidate * candidate),
                    total_h * squashed * outgate * (1.0 - outgate),
                ],
                axis=1,
            )
            grad_c[e][...] = total_c * forget
            for k, p in enumerate(at):
                dz_ref[e][p] = dz[16 * k : 16 * (k + 1)]
            work.append(dz)
        for e in range(2):
            hi, lo = split(work[e])
            rows = hi.shape[0]
            first = dot1(jnp.concatenate([hi, lo], axis=0), hi_ref[e], ABT)
            grad_h[e][...] = first[:rows] + first[rows:] + dot1(hi, lo_ref[e], ABT)
        return carry

    lax.fori_loop(0, steps, step, 0)


def states_backward(count, dy_flat, dh, h, w_out, g_out):
    hidden = h[0].shape[2]
    dy = split(dy_flat)
    for e in range(2):
        part = slice(hidden * e, hidden * (e + 1))
        dh[e][:count] = dot_parts(dy, split(w_out[part]), ABT).reshape(count, 16, hidden)
        g_out[part] = dot3_parts_first(h[e][:count].reshape(count * 16, hidden), dy)


def dot3_parts_first(a, b_parts):
    return dot_parts(split(a), b_parts, ATB)


def gates_backward(count, x_flat, dy_flat, dz_ref, hp, w_in, vec, g_in, g_rec, g_vec):
    dmodel = w_in.shape[1]
    hidden = hp[0].shape[2]
    hidden4 = 4 * hidden
    rows = count * 16
    unit, scale = norm_stats(x_flat)
    gain = 1.0 + vec[0:1, :dmodel]
    n = split(unit * gain + vec[0:1, dmodel : 2 * dmodel])
    dn = jnp.zeros((rows, dmodel), jnp.float32)
    for e in range(2):
        before = split(hp[e][:count].reshape(rows, hidden))
        for q in range(4):
            part = slice(hidden * q, hidden * (q + 1))
            dz_q = dz_ref[e][:count, :, part].reshape(rows, hidden)
            dz = split(dz_q)
            g_rec[e, :, part] = dot_parts(before, dz, ATB)
            g_in[e, :, part] = dot_parts(n, dz, ATB)
            dn = dn + dot_parts(dz, split(w_in[e, :, part]), ABT)
            base = 2 * dmodel + hidden4 * e + hidden * q
            g_vec[0:1, base : base + hidden] = column_sum(dz_q)
    g_vec[0:1, :dmodel] = column_sum(dn * unit)
    g_vec[0:1, dmodel : 2 * dmodel] = column_sum(dn)
    g_vec[0:1, vec.shape[1] - dmodel :] = column_sum(dy_flat)
    return dy_flat + norm_back(dn * gain, unit, scale)


def clip_places(clips, spare):
    def places(e, j):
        found = []
        for c in range(CLIPS):
            start, length = clips[0, c], clips[1, c]
            frame = start + j if e == 0 else start + length - 1 - j
            found.append(jnp.where(j < length, frame, spare))
        return found

    return places


def window_of(edge):
    base = pl.multiple_of((edge // LANES) * LANES, LANES)
    return base, lax.rem(edge, LANES)


def split_rows(spec, edge, width, frames):
    wmax = LANES
    base, shift = window_of(edge)
    window = spec[:, pl.ds(base, 2 * LANES)]
    taken = pltpu.roll(window, lax.rem(2 * LANES - shift, 2 * LANES), 1)[:, :wmax]
    taken = jnp.concatenate([taken[:frames], taken[frames:]], axis=1)
    lane = lax.broadcasted_iota(jnp.int32, (frames, wmax), 1)
    inside = (lane < width).astype(jnp.float32)
    valid = jnp.concatenate([inside, inside], axis=1)
    entries = jnp.maximum(2 * width, 1).astype(jnp.float32)
    mean = jnp.sum(taken * valid, axis=-1, keepdims=True) / entries
    center = (taken - mean) * valid
    spread = jnp.sum(center * center, axis=-1, keepdims=True) / entries
    scale = lax.rsqrt(jnp.maximum(spread, VAR_FLOOR))
    moving = jnp.where(spread > VAR_FLOOR, 1.0, jnp.where(spread == VAR_FLOOR, 0.5, 0.0))
    return center * scale, scale, valid, moving, entries


def time_forward_kernel(
    places_s, clips, spec, w_split, v_band, w_in, w_rec, w_out, vec,
    out, x, act0, act1, tc0, tc1, cp0, cp1, hp0, hp1, h0, h1,
    hi_ref, lo_ref, s0, s1, m0, m1, y, mixed,
):
    slots = w_split.shape[0]
    frames = x.shape[0]
    dmodel = w_split.shape[2]
    wide = w_split.shape[1]
    x[...] = jnp.zeros_like(x)
    for a in (act0, act1):
        a[frames] = jnp.zeros_like(a[frames])

    def one_slot(s, carry):
        unit, unused, valid, moving, entries = split_rows(spec, places_s[0, s], places_s[1, s], frames)
        row = v_band[s]
        z = (unit * (1.0 + row[:, :wide]) + row[:, wide : 2 * wide]) * valid
        y[s] = dot3(z, w_split[s], AB) + row[:, 2 * wide : 2 * wide + dmodel]
        return carry

    lax.fori_loop(0, slots, one_slot, 0)
    for s in range(slots):
        x[:, s, :] = y[s]
    act = (act0, act1)
    block = 256

    def x_flat(start, size):
        return x[pl.ds(start // 16, size // 16)].reshape(size, dmodel)

    gates_forward(x_flat, act, w_in, vec, frames * 16, block)
    run_forward(
        CLIP_MOST, clip_places(clips, frames), act, (tc0, tc1), (cp0, cp1), (hp0, hp1), (h0, h1),
        w_rec, hi_ref, lo_ref, (s0, s1), (m0, m1),
    )
    total = output_forward(frames, (h0, h1), w_out, vec)
    x_all = x[...].reshape(frames * 16, dmodel)
    mixed[...] = (x_all + total).reshape(frames, 16, dmodel)
    parts, unused_slots, quarter, unused = out.shape
    for s in range(slots):
        for q in range(parts):
            out[q, s] = mixed[q * quarter : (q + 1) * quarter, s, :]


def f32(shape):
    return jax.ShapeDtypeStruct(shape, jnp.float32)


def saved_shapes(count, hidden):
    wide = [f32((count, 16, 4 * hidden))] * 2
    thin = [f32((count, 16, hidden))] * 8
    return wide + thin


def rec_scratch(rows, hidden):
    return [
        pltpu.VMEM((2, hidden, 4 * hidden), jnp.bfloat16),
        pltpu.VMEM((2, hidden, 4 * hidden), jnp.bfloat16),
    ] + [pltpu.VMEM((rows, hidden), jnp.float32)] * 4


SMEM = pl.BlockSpec(memory_space=pltpu.SMEM)
VMEM = pl.BlockSpec(memory_space=pltpu.VMEM)
PARAMS = pltpu.CompilerParams(vmem_limit_bytes=VMEM_BYTES)


def time_forward(slot_places, clips, spec, w_split, v_band, w_in, w_rec, w_out, vec, parts):
    slots, wide, dmodel = w_split.shape
    hidden = w_rec.shape[1]
    frames = spec.shape[0] // 2
    return pl.pallas_call(
        time_forward_kernel,
        out_shape=[f32((parts, slots, frames // parts, dmodel)), f32((frames, 16, dmodel))]
        + saved_shapes(frames + 1, hidden),
        in_specs=[SMEM, SMEM] + [VMEM] * 7,
        out_specs=[VMEM] * 12,
        scratch_shapes=rec_scratch(16 * CLIPS, hidden)
        + [pltpu.VMEM((slots, frames, dmodel), jnp.float32)]
        + [pltpu.VMEM((frames, 16, dmodel), jnp.float32)],
        compiler_params=PARAMS,
        name="time_forward",
    )(slot_places, clips, spec, w_split, v_band, w_in, w_rec, w_out, vec)


def time_backward_kernel(
    places_s, clips, dy_in, spec, x, act0, act1, tc0, tc1, cp0, cp1, hp0, hp1, h0, h1,
    w_split, v_band, w_in, w_rec, w_out, vec,
    d_spec, g_split, g_band, g_in, g_rec, g_out, g_vec,
    hi_ref, lo_ref, s0, s1, m0, m1, dy, dh0, dh1, dz0, dz1,
):
    slots, wide, dmodel = w_split.shape
    frames = x.shape[0]
    parts, unused_slots, quarter, unused = dy_in.shape
    dy[...] = jnp.zeros_like(dy)
    for s in range(slots):
        for q in range(parts):
            dy[q * quarter : (q + 1) * quarter, s, :] = dy_in[q, s]
    dy_flat = dy[...].reshape(frames * 16, dmodel)
    states_backward(frames, dy_flat, (dh0, dh1), (h0, h1), w_out, g_out)
    for d in (dh0, dh1):
        d[frames] = jnp.zeros_like(d[frames])
    run_backward(
        CLIP_MOST, clip_places(clips, frames), (act0, act1), (dz0, dz1), (tc0, tc1), (cp0, cp1), (dh0, dh1),
        w_rec, hi_ref, lo_ref, (s0, s1), (m0, m1),
    )
    x_flat = x[...].reshape(frames * 16, dmodel)
    dx = gates_backward(frames, x_flat, dy[...].reshape(frames * 16, dmodel), (dz0, dz1), (hp0, hp1), w_in, vec, g_in, g_rec, g_vec)
    dy[...] = dx.reshape(frames, 16, dmodel)
    d_spec[...] = jnp.zeros_like(d_spec)

    for s in range(slots):
        edge, width = places_s[0, s], places_s[1, s]
        unit, scale, valid, moving, entries = split_rows(spec, edge, width, frames)
        row = v_band[s]
        gain = 1.0 + row[:, :wide]
        z = (unit * gain + row[:, wide : 2 * wide]) * valid
        demb = dy[:, s, :]
        demb_parts = split(demb)
        g_split[s] = dot_parts(split(z), demb_parts, ATB)
        dz = dot_parts(demb_parts, split(w_split[s]), ABT) * valid
        g_band[s, :, :wide] = column_sum(dz * unit)
        g_band[s, :, wide : 2 * wide] = column_sum(dz)
        g_band[s, :, 2 * wide :] = column_sum(demb)
        du = dz * gain
        first = jnp.sum(du, axis=-1, keepdims=True) / entries
        second = jnp.sum(du * unit, axis=-1, keepdims=True) / entries
        dt = scale * (du - first - moving * unit * second) * valid
        base, shift = window_of(edge)
        stacked = jnp.concatenate([dt[:, :LANES], dt[:, LANES:]], axis=0)
        padded = jnp.concatenate([stacked, jnp.zeros_like(stacked)], axis=1)
        d_spec[:, pl.ds(base, 2 * LANES)] += pltpu.roll(padded, shift, 1)


def time_backward(slot_places, clips, dy, spec, saved, w_split, v_band, w_in, w_rec, w_out, vec):
    slots, wide, dmodel = w_split.shape
    hidden = w_rec.shape[1]
    frames = spec.shape[0] // 2
    return pl.pallas_call(
        time_backward_kernel,
        out_shape=[
            f32(spec.shape), f32(w_split.shape), f32((slots, 1, 2 * wide + dmodel)),
            f32(w_in.shape), f32(w_rec.shape), f32(w_out.shape), f32(vec.shape),
        ],
        in_specs=[SMEM, SMEM] + [VMEM] * (3 + 10 + 6),
        out_specs=[VMEM] * 7,
        scratch_shapes=rec_scratch(16 * CLIPS, hidden)
        + [pltpu.VMEM((frames, 16, dmodel), jnp.float32)]
        + [pltpu.VMEM((frames + 1, 16, hidden), jnp.float32)] * 2
        + [pltpu.VMEM((frames + 1, 16, 4 * hidden), jnp.float32)] * 2,
        compiler_params=PARAMS,
        name="time_backward",
    )(slot_places, clips, dy, spec, *saved, w_split, v_band, w_in, w_rec, w_out, vec)


def band_places(bands):
    return lambda e, j: [j if e == 0 else bands - 1 - j]


def band_forward_kernel(
    slot_of, arrived, w_in, w_rec, w_out, vec,
    out, x, act0, act1, tc0, tc1, cp0, cp1, hp0, hp1, h0, h1,
    hi_ref, lo_ref, s0, s1, m0, m1,
):
    bands, unused, dmodel = x.shape

    def fetch(b, carry):
        x[b] = arrived[slot_of[0, b]]
        return carry

    lax.fori_loop(0, bands, fetch, 0)
    act = (act0, act1)

    def x_flat(start, size):
        return x[...].reshape(bands * 16, dmodel)

    gates_forward(x_flat, act, w_in, vec, bands * 16, bands * 16)
    run_forward(
        bands, band_places(bands), act, (tc0, tc1), (cp0, cp1), (hp0, hp1), (h0, h1),
        w_rec, hi_ref, lo_ref, (s0, s1), (m0, m1),
    )
    total = output_forward(bands, (h0, h1), w_out, vec)
    whole = (x[...].reshape(bands * 16, dmodel) + total).reshape(bands, 16, dmodel)
    out[...] = jnp.zeros_like(out)
    for b in range(bands):
        out[slot_of[0, b]] = whole[b]


def band_forward(slot_of, arrived, w_in, w_rec, w_out, vec):
    bands = slot_of.shape[1]
    hidden = w_rec.shape[1]
    dmodel = w_out.shape[1]
    return pl.pallas_call(
        band_forward_kernel,
        out_shape=[f32(arrived.shape), f32((bands, 16, dmodel))] + saved_shapes(bands, hidden),
        in_specs=[SMEM] + [VMEM] * 5,
        out_specs=[VMEM] * 12,
        scratch_shapes=rec_scratch(16, hidden),
        compiler_params=PARAMS,
        name="band_forward",
    )(slot_of, arrived, w_in, w_rec, w_out, vec)


def band_backward_kernel(
    slot_of, arrived, x, act0, act1, tc0, tc1, cp0, cp1, hp0, hp1, h0, h1,
    w_in, w_rec, w_out, vec,
    out, g_in, g_rec, g_out, g_vec,
    hi_ref, lo_ref, s0, s1, m0, m1, dy, dh0, dh1, dz0, dz1,
):
    bands, unused, dmodel = x.shape

    def fetch(b, carry):
        dy[b] = arrived[slot_of[0, b]]
        return carry

    lax.fori_loop(0, bands, fetch, 0)
    states_backward(bands, dy[...].reshape(bands * 16, dmodel), (dh0, dh1), (h0, h1), w_out, g_out)
    run_backward(
        bands, band_places(bands), (act0, act1), (dz0, dz1), (tc0, tc1), (cp0, cp1), (dh0, dh1),
        w_rec, hi_ref, lo_ref, (s0, s1), (m0, m1),
    )
    dx = gates_backward(
        bands, x[...].reshape(bands * 16, dmodel), dy[...].reshape(bands * 16, dmodel),
        (dz0, dz1), (hp0, hp1), w_in, vec, g_in, g_rec, g_vec,
    ).reshape(bands, 16, dmodel)
    out[...] = jnp.zeros_like(out)
    for b in range(bands):
        out[slot_of[0, b]] = dx[b]


def band_backward(slot_of, arrived, saved, w_in, w_rec, w_out, vec):
    bands = slot_of.shape[1]
    hidden = w_rec.shape[1]
    dmodel = w_out.shape[1]
    return pl.pallas_call(
        band_backward_kernel,
        out_shape=[
            f32(arrived.shape), f32(w_in.shape), f32(w_rec.shape), f32(w_out.shape), f32(vec.shape),
        ],
        in_specs=[SMEM] + [VMEM] * (2 + 10 + 4),
        out_specs=[VMEM] * 5,
        scratch_shapes=rec_scratch(16, hidden)
        + [pltpu.VMEM((bands, 16, dmodel), jnp.float32)]
        + [pltpu.VMEM((bands, 16, hidden), jnp.float32)] * 2
        + [pltpu.VMEM((bands, 16, 4 * hidden), jnp.float32)] * 2,
        compiler_params=PARAMS,
        name="band_backward",
    )(slot_of, arrived, *saved, w_in, w_rec, w_out, vec)


def mask_kernel(widths, arrived, cot, w_wide, w_mask, vec, masks, grad, g_wide, g_mask, g_vec):
    s = pl.program_id(0)
    parts, streams, unused, quarter, dmodel = arrived.shape
    mlp = w_wide.shape[2]
    wide = masks.shape[2]
    half = wide // 2
    x = jnp.concatenate(
        [arrived[q, g, 0] for g in range(streams) for q in range(parts)], axis=0
    )
    rows = x.shape[0]
    v = vec[0]
    gain = 1.0 + v[:, :dmodel]
    unit, scale = norm_stats(x)
    p = split(unit * gain + v[:, dmodel : 2 * dmodel])
    wide_parts = split(w_wide[0])
    mask_parts = split(w_mask[0])
    q = jnp.tanh(dot_parts(p, wide_parts, AB) + v[:, 2 * dmodel : 2 * dmodel + mlp])
    q_parts = split(q)
    r = dot_parts(q_parts, mask_parts, AB) + v[:, 2 * dmodel + mlp :]
    lane = lax.broadcasted_iota(jnp.int32, (1, half), 1)
    inside = (lane < widths[0, s]).astype(jnp.float32)
    valid = jnp.concatenate([inside, inside], axis=1)
    value = r[:, :wide]
    gate = sigmoid(r[:, wide:])
    masks[0] = value * gate * valid
    dm = cot[0] * valid
    dr = jnp.concatenate([dm * gate, dm * value * gate * (1.0 - gate)], axis=1)
    dr_parts = split(dr)
    g_mask[0] = dot_parts(q_parts, dr_parts, ATB)
    dq = dot_parts(dr_parts, mask_parts, ABT)
    da = dq * (1.0 - q * q)
    da_parts = split(da)
    g_wide[0] = dot_parts(p, da_parts, ATB)
    dp = dot_parts(da_parts, wide_parts, ABT)
    g_vec[0, :, :dmodel] = column_sum(dp * unit)
    g_vec[0, :, dmodel : 2 * dmodel] = column_sum(dp)
    g_vec[0, :, 2 * dmodel : 2 * dmodel + mlp] = column_sum(da)
    g_vec[0, :, 2 * dmodel + mlp :] = column_sum(dr)
    dx = norm_back(dp * gain, unit, scale)
    k = 0
    for g in range(streams):
        for q_ in range(parts):
            grad[q_, g, 0] = dx[k * quarter : (k + 1) * quarter]
            k += 1


def mask_network(widths, arrived, cot, w_wide, w_mask, vec):
    parts, streams, slots, quarter, dmodel = arrived.shape
    rows, wide = cot.shape[1:]
    mlp = w_wide.shape[2]
    moving = pl.BlockSpec((parts, streams, 1, quarter, dmodel), lambda s: (0, 0, s, 0, 0))

    def lead(shape):
        return pl.BlockSpec((1,) + shape, lambda s: (s,) + (0,) * len(shape))

    return pl.pallas_call(
        mask_kernel,
        grid=(slots,),
        out_shape=[
            f32(cot.shape), f32(arrived.shape), f32(w_wide.shape), f32(w_mask.shape), f32(vec.shape),
        ],
        in_specs=[
            SMEM, moving, lead((rows, wide)), lead(w_wide.shape[1:]), lead(w_mask.shape[1:]),
            lead(vec.shape[1:]),
        ],
        out_specs=[
            lead((rows, wide)), moving, lead(w_wide.shape[1:]), lead(w_mask.shape[1:]),
            lead(vec.shape[1:]),
        ],
        compiler_params=PARAMS,
        name="mask_network",
    )(widths, arrived, cot, w_wide, w_mask, vec)


def groups_of(size, slots):
    outer = math.gcd(size, slots)
    inner = size // outer
    across = [[g * inner + i for g in range(outer)] for i in range(inner)]
    within = [[g * inner + i for i in range(inner)] for g in range(outer)]
    return outer, inner, across, within


def sum_everywhere(values, sizes):
    n = sizes[0] * sizes[1]
    row = jnp.zeros((8, LANES), jnp.float32).at[0, : values.shape[0]].set(values)
    spread = jnp.broadcast_to(row[None], (n, 8, LANES))
    got = lax.all_to_all(spread, ("band", "stream"), 0, 0, tiled=True)
    return jnp.sum(got, axis=0)[0, : values.shape[0]]


def share_slots(shard, outer, across, within, axis):
    slots = shard.shape[0]
    sent = lax.all_to_all(
        shard.reshape((outer, slots // outer) + shard.shape[1:]), "stream", 0, 0,
        axis_index_groups=across, tiled=True,
    )
    inner = len(within[0])
    if inner == 2:
        me = lax.rem(lax.axis_index("stream"), 2)
        count = lax.axis_size("stream")
        other = lax.ppermute(sent, "stream", [(s, s ^ 1) for s in range(count)])
        return jnp.stack([jnp.where(me == 0, sent, other), jnp.where(me == 0, other, sent)])
    return lax.all_gather(sent, "stream", axis_index_groups=within)


def return_slots(grads, outer, inner, across, within):
    if inner == 2:
        me = lax.rem(lax.axis_index("stream"), 2)
        count = lax.axis_size("stream")
        other = lax.ppermute(
            lax.dynamic_index_in_dim(grads, 1 - me, 0, False), "stream",
            [(s, s ^ 1) for s in range(count)],
        )
        mine = lax.dynamic_index_in_dim(grads, me, 0, False) + other
    else:
        mine = lax.psum_scatter(grads, "stream", axis_index_groups=within, tiled=False)
    back = lax.all_to_all(mine, "stream", 0, 0, axis_index_groups=across, tiled=True)
    return back.reshape((-1,) + back.shape[2:])


def lamb_moments(gradient, mean_old, power_old, factor):
    clipped = gradient * factor
    mean_new = BETA_ONE * mean_old + (1.0 - BETA_ONE) * clipped
    power_new = BETA_TWO * power_old + (1.0 - BETA_TWO) * clipped * clipped
    return (mean_new, power_new)


def lamb_direction(weight_matrix, mean_new, power_new, decay):
    corrected = mean_new / (1.0 - BETA_ONE**STEP)
    scale_root = jnp.sqrt(power_new / (1.0 - BETA_TWO**STEP)) + ADAM_EPS
    return corrected / scale_root + decay * weight_matrix


def body(spectrum, segments, widths, groups, cotangent, *state):
    weights, means_old, powers_old = state[:8], state[8:16], state[16:]
    splitter, widener, masker, banding, intake, recurrence, outtake, scalers = weights
    group_count = lax.axis_size("band")
    stream_count = lax.axis_size("stream")
    my_group = lax.axis_index("band")
    my_stream = lax.axis_index("stream")
    slots = splitter.shape[0]
    frames = spectrum.shape[0]
    quarter = frames // group_count
    outer, inner, across, within = groups_of(stream_count, slots)
    share = slots // outer
    my_outer = my_stream // inner
    dmodel = splitter.shape[2]
    wide = splitter.shape[1] * stream_count
    wmax = wide // 2
    mlp = masker.shape[1] * stream_count
    bins = spectrum.shape[2]

    members = (groups[:, None] == jnp.arange(group_count, dtype=jnp.int32)[None, :]).astype(jnp.int32)
    ranking = jnp.sum(jnp.cumsum(members, axis=0) * members, axis=1) - 1
    band_slot_index = groups * slots + ranking
    local_slots = my_group * slots + jnp.arange(slots, dtype=jnp.int32)
    owned = (band_slot_index[None, :] == local_slots[:, None]).astype(jnp.int32)
    edges = jnp.cumsum(widths) - widths
    slot_edges = jnp.sum(owned * edges[None, :], axis=1)
    slot_widths = jnp.sum(owned * widths[None, :], axis=1)
    slot_places = jnp.stack([slot_edges, slot_widths])
    slot_of = band_slot_index[None, :]
    lengths = jnp.sum(
        (segments[0][None, :] == jnp.arange(CLIPS, dtype=jnp.int32)[:, None]).astype(jnp.int32), axis=1
    )
    clips = jnp.stack([jnp.cumsum(lengths) - lengths, lengths])
    share_widths = lax.dynamic_slice(slot_widths, (my_outer * share,), (share,))[None, :]

    w_split = lax.all_gather(splitter, "stream", axis=1, tiled=True)
    v_band = lax.all_gather(banding, "stream", axis=1, tiled=True)
    w_in = lax.all_gather(intake, "stream", axis=3, tiled=True)
    w_rec = lax.all_gather(recurrence, "stream", axis=3, tiled=True)
    w_out = lax.all_gather(outtake, "stream", axis=1, tiled=True)
    v_rnn = lax.all_gather(scalers, "stream", axis=1, tiled=True)

    w_wide = share_slots(widener, outer, across, within, 2)
    w_wide = w_wide.transpose(2, 3, 1, 0, 4).reshape(share, dmodel, mlp)
    w_mask = share_slots(masker, outer, across, within, 1)
    w_mask = w_mask.transpose(2, 1, 0, 3, 4).reshape(share, mlp, 2 * wide)
    cot_parts = cotangent.reshape(frames, outer, share, wide).transpose(1, 2, 0, 3)
    cot = lax.all_to_all(cot_parts, "stream", 0, 0, axis_index_groups=across, tiled=True)
    cot = cot.transpose(1, 0, 2, 3).reshape(share, outer * frames, wide)

    padded = ((bins - 1) // LANES + 2) * LANES
    spec = jnp.pad(
        spectrum.transpose(1, 0, 2).reshape(2 * frames, bins), ((0, 0), (0, padded - bins))
    )
    vec0, vec1 = v_rnn[0:1], v_rnn[1:2]
    v_band = v_band[:, None, :]
    base = 2 * wide + dmodel
    got = time_forward(
        slot_places, clips, spec, w_split, v_band, w_in[0], w_rec[0], w_out[0], vec0, group_count
    )
    time_out, time_saved = got[0], got[1:]
    arrived = lax.all_to_all(time_out, "band", 0, 0, tiled=True)
    got = band_forward(
        slot_of, arrived.reshape(group_count * slots, quarter, dmodel), w_in[1], w_rec[1], w_out[1], vec1
    )
    band_out, band_saved = got[0], got[1:]

    def to_masks(x):
        x = x.reshape(group_count, outer, share, quarter, dmodel)
        x = lax.all_to_all(x, "stream", 1, 1, axis_index_groups=across, tiled=True)
        return lax.all_to_all(x, "band", 0, 0, tiled=True)

    def from_masks(x):
        x = lax.all_to_all(x, "band", 0, 0, tiled=True)
        x = lax.all_to_all(x, "stream", 1, 1, axis_index_groups=across, tiled=True)
        return x.reshape(group_count * slots, quarter, dmodel)

    share_vec = lax.dynamic_slice_in_dim(v_band[:, :, base:], my_outer * share, share, 0)
    mask_parts, grad_mixed, g_wide, g_mask, g_mask_vec = mask_network(
        share_widths, to_masks(band_out), cot, w_wide, w_mask, share_vec
    )
    band_grad, band_gin, band_grec, band_gout, band_gvec = band_backward(
        slot_of, from_masks(grad_mixed), band_saved, w_in[1], w_rec[1], w_out[1], vec1
    )
    grad_time = lax.all_to_all(
        band_grad.reshape(group_count, slots, quarter, dmodel), "band", 0, 0, tiled=True
    )
    d_spec, g_split, g_split_vec, time_gin, time_grec, time_gout, time_gvec = time_backward(
        slot_places, clips, grad_time, spec, time_saved, w_split, v_band, w_in[0], w_rec[0], w_out[0], vec0
    )

    mask_parts = mask_parts.reshape(share, outer, frames, wide).transpose(1, 0, 2, 3)
    mask_parts = lax.all_to_all(mask_parts, "stream", 0, 0, axis_index_groups=across, tiled=True)
    masks = mask_parts.reshape(slots, frames, wide).transpose(1, 0, 2).reshape(cotangent.shape)
    d_spec = lax.psum(d_spec, "band")
    spectrum_grad = d_spec.reshape(2, frames, padded)[:, :, :bins].transpose(1, 0, 2)

    g_wide = g_wide.reshape(share, dmodel, outer, inner, -1).transpose(3, 2, 0, 1, 4)
    widened_reduced = return_slots(g_wide, outer, inner, across, within)
    g_mask = g_mask.reshape(share, outer, inner, -1, 2 * wide).transpose(2, 1, 0, 3, 4)
    mask_reduced = return_slots(g_mask, outer, inner, across, within)
    g_mask_vec = lax.dynamic_update_slice_in_dim(
        jnp.zeros((slots, g_mask_vec.shape[2]), jnp.float32), g_mask_vec[:, 0], my_outer * share, 0
    )
    g_band = jnp.concatenate([g_split_vec[:, 0], g_mask_vec], axis=1)
    rnn_grads = (
        lax.psum_scatter(jnp.stack([time_gin, band_gin]), "stream", scatter_dimension=3, tiled=True),
        lax.psum_scatter(jnp.stack([time_grec, band_grec]), "stream", scatter_dimension=3, tiled=True),
        lax.psum_scatter(jnp.stack([time_gout, band_gout]), "stream", scatter_dimension=1, tiled=True),
        lax.psum_scatter(
            jnp.concatenate([time_gvec, band_gvec], axis=0), "stream", scatter_dimension=1, tiled=True
        ),
    )
    rnn_grads = lax.psum(rnn_grads, "band")
    reduced = (
        lax.psum_scatter(g_split, "stream", scatter_dimension=1, tiled=True),
        widened_reduced,
        mask_reduced,
        lax.psum_scatter(g_band, "stream", scatter_dimension=1, tiled=True),
    ) + tuple(rnn_grads)

    shares = (1.0,) * 4 + (1.0 / group_count,) * 4
    decays = (DECAY_RATE,) * 3 + (0.0,) + (DECAY_RATE,) * 3 + (0.0,)
    sizes = (group_count, stream_count)
    sums = [sum(jnp.sum(g * g) * part for g, part in zip(reduced, shares))]
    sums += [jnp.sum(w * w) * part for w, part in zip(weights, shares)]
    totals = sum_everywhere(jnp.stack(sums), sizes)
    grad_norm = jnp.sqrt(totals[0])
    factor = jnp.minimum(1.0, CLIP_NORM / grad_norm)
    moments = [lamb_moments(g, m, p, factor) for g, m, p in zip(reduced, means_old, powers_old)]
    directions = [lamb_direction(w, m, p, d) for w, (m, p), d in zip(weights, moments, decays)]
    update_totals = sum_everywhere(
        jnp.stack([jnp.sum(d * d) * part for d, part in zip(directions, shares)]), sizes
    )
    ratios = jnp.sqrt(totals[1:]) / jnp.sqrt(update_totals + 1e-12)
    fresh = [w - LEARN_RATE * ratios[k] * d for k, (w, d) in enumerate(zip(weights, directions))]
    return (
        (masks, spectrum_grad, grad_norm)
        + tuple(fresh)
        + tuple(m for m, unused in moments)
        + tuple(p for unused, p in moments)
    )


def solution(mesh):
    stored = (
        P("band", "stream", None),
        P("band", None, "stream"),
        P("band", "stream", None),
        P("band", "stream"),
        P(None, None, None, "stream"),
        P(None, None, None, "stream"),
        P(None, "stream", None),
        P(None, "stream"),
    )
    frames_over = P("stream", None, None)
    mask_over = P("stream", "band", None, None)
    return jax.shard_map(
        body,
        mesh=mesh,
        in_specs=(frames_over, P("stream", None), P(), P(), mask_over) + stored * 3,
        out_specs=(mask_over, frames_over, P()) + stored * 3,
        check_vma=False,
    )
```

time: 1710 us -> 836 us (0.49)
  matrix products: 683 us -> 0 us
  other arithmetic: 382 us -> 66.6 us
  local copies, waits for them, and re-layouts: 238 us -> 56.4 us
  Pallas kernels: 0 us -> 168 us
  waiting for transfers between devices: 190 us -> 289 us
  blocking collectives: 135 us -> 166 us
  starting transfers between devices: 16.8 us -> 46 us
    dot_general x236 -> x0, matrix products: 683 us -> none  [the longest x104 283 us: retreat(): jnp.einsum('ebk,ehk->ebh', grad_gates, w_rec, precision=MATMUL_PRECISION)]
    pallas_call x0 -> x5, Pallas kernels: none -> 168 us  [the longest x1 50.6 us: time_backward(): pl.pallas_call(time_backward_kernel, out_shape=[f32(spec.shape), f32(w_sp...]
    scatter-add x1 -> x0, other arithmetic: 158 us -> none  [split_forward(): taken = jnp.take(spectrum, index.reshape(-1), axis=2)]
    psum x3 -> x1, blocking collectives: 87.2 us -> 9.74 us  [body(): rnn_grads = lax.psum(rnn_grads, 'band')]
    all_gather x3, blocking collectives: 47.9 us -> 114 us  [the longest x1 72.6 us: body(): w_out = lax.all_gather(outtake, 'stream', axis=1, tiled=True)]
    while x273 -> x0, other arithmetic: 64.8 us -> none
    mul x120 -> x2, other arithmetic: 52.8 us -> 0.29 us  [lamb_moments(): clipped = gradient * factor]
    dynamic_update_slice x52 -> x1, local copies, waits for them, and re-layouts: 51.2 us -> 0.35 us  [body(): lax.dynamic_update_slice_in_dim(jnp.zeros((slots, g_mask_vec.shape[2]), j...]
  transfers between devices with their start and end apart: 18 -> 25, of which waited for: 5 -> 14; matrix products, arithmetic and copies ran while one was open for 45% -> 9% of each run, Pallas kernels for 0% -> 8%
where the time goes in v1:
time: 836 us; the launch traced here: 824 us
  waiting for transfers between devices  289 us (35%)
  Pallas kernels  168 us (20%)
  blocking collectives  166 us (20%)
  other arithmetic  66.6 us (8%)
  local copies, waits for them, and re-layouts  56.4 us (7%)
  starting transfers between devices  46 us (6%)
  between operations  32.6 us (4%)
    all_gather x1, blocking collectives, body(): w_out = lax.all_gather(outtake, 'stream', axis=1, tiled=True)  72.6 us
    reduce_scatter x1, waiting for transfers between devices, body(): lax.psum_scatter(jnp.stack([time_grec, band_grec]), 'stream', scatter_dim...  64.1 us
    psum x1, waiting for transfers between devices, body(): d_spec = lax.psum(d_spec, 'band')  57.7 us
    pallas_call x1, Pallas kernels, time_backward(): pl.pallas_call(time_backward_kernel, out_shape=[f32(spec.shape), f32(w_sp...  50.6 us
    unnamed x12, waiting for transfers between devices  50.4 us
    pallas_call x1, Pallas kernels, band_backward(): pl.pallas_call(band_backward_kernel, out_shape=[f32(arrived.shape), f32(w...  43.7 us
    reduce_scatter x1, waiting for transfers between devices, body(): lax.psum_scatter(jnp.stack([time_gin, band_gin]), 'stream', scatter_dimen...  37.6 us
    pallas_call x1, Pallas kernels, time_forward(): pl.pallas_call(time_forward_kernel, out_shape=[f32((parts, slots, frames...  34.9 us
  transfers between devices with their start and end apart: 25, of which 14 were waited for; matrix products, arithmetic and copies ran while one was open for 9% of the time, Pallas kernels for 8%

profile of v1, /device:TPU:0, one launch (start us, length us, event | category | flops | bytes accessed | tf_op | source)
XLA Modules:
  0.0 824.2 jit_solution(6430548461265662948)
XLA Ops:
  8.8 6.3 all-to-all-start.4
  15.9 27.2 %all-gather = f32[8,240,12]{1,2,0:T(8,128)S(1)} all-gather(f32[1,240,12]{1,2,0:T(8,128)S(1)} %bitcast.181), channel_id=1, replica_groups=mesh['band'=4,'stream'=8] {'stream'}, dimensions={0}, use_global_device_ids=true | all-gather | bytes 103680 | tf_op jit(solution)/shard_map/all_gather | solution.py:682
  44.6 13.9 %all-gather.1 = f32[8,304,2]{1,2,0:T(2,128)S(1)} all-gather(f32[1,304,2]{1,2,0:T(2,128)S(1)} %bitcast.189), channel_id=1, replica_groups=mesh['band'=4,'stream'=8] {'stream'}, dimensions={0}, use_global_device_ids=true | all-gather | bytes 21888 | tf_op jit(solution)/shard_map/all_gather | solution.py:686
  60.3 3.8 all-to-all-start.5
  64.9 72.6 %all_gather.22 = f32[2,512,128]{2,1,0:T(8,128)S(1)} all-gather(f32[2,64,128]{2,1,0:T(8,128)S(1)} %copy-done.13), channel_id=1, replica_groups=mesh['band'=4,'stream'=8] {'stream'}, dimensions={1}, use_global_device_ids=true | all-gather | bytes 589824 | tf_op jit(solution)/shard_map/all_gather | solution.py:685
  138.9 3.2 slice_bitcast_fusion.2
  142.0 4.9 slice_bitcast_fusion
  146.9 11.8 %all-gather.6.cloned.1.call-done.w_split = f32[12,256,128]{2,1,0:T(8,128)} async-done(((f32[12,32,128]{2,1,0:T(8,128)}), f32[12,256,128]{2,1,0:T(8,128)}) %all-gather.6.cloned.1.call-update) | async-done | bytes 1572880 | tf_op jit(solution)/shard_map/all_gather | solution.py:681
  158.7 34.9 %time_forward.1 = (f32[4,12,16,128]{3,2,1,0:T(8,128)}, f32[64,16,128]{2,1,0:T(8,128)}, f32[65,16,1024]{2,1,0:T(8,128)}, f32[65,16,1024]{2,1,0:T(8,128)}, f32[65,...) custom-call(s32[2,12]{1,0:T(2,128)} %pad_add_fusion.places_s, ...), custom_call_target="tpu_custom_call" | custom-call | tf_op jit(solution)/shard_map/time_forward/pallas_call | solution.py:334
  193.7 3.7 all-to-all-start
  200.3 4.0 all-to-all-done
  204.4 3.5 all-to-all-start.3
  209.0 28.1 %band_forward.1 = (f32[48,16,128]{2,1,0:T(8,128)}, f32[41,16,128]{2,1,0:T(8,128)}, f32[41,16,1024]{2,1,0:T(8,128)}, f32[41,16,1024]{2,1,0:T(8,128)}, f32[41,16,2...) custom-call(s32[1,41]{1,0:T(1,128)} %bitcast.190, ...), custom_call_target="tpu_custom_call" | custom-call | tf_op jit(solution)/shard_map/band_forward/pallas_call | solution.py:455
  237.1 1.8 copy.130
  238.9 5.2 all-to-all-start.1
  248.2 7.8 all-to-all-done.1
  256.8 3.5 all-to-all-start.2
  260.3 1.8 select_bitcast_fusion.1
  262.6 2.0 copy.135
  264.6 1.7 all-to-all-done.2.arrived
  267.1 10.6 %mask_network.1 = (f32[3,256,256]{2,1,0:T(8,128)}, f32[4,4,3,16,128]{4,3,2,1,0:T(8,128)}, f32[3,128,512]{2,1,0:T(8,128)}, f32[3,512,512]{2,1,0:T(8,128)}, f32[3,1,1280]{2,1,0:T(1,128)}) custom-call(s32[1,3]{1,0:T(1,128)} %dynamic-slice_bitcast_fusion.1.widths, f32[4,4,3,16,128]{4,3,2,1,0:T(8,128)} %copy-done.12, f32[3,256,256]{2,1,0:T(8,128)} %bitcast.161, ...), custom_call_target="tpu_custom_call" | custom-call | tf_op jit(solution)/shard_map/mask_network/pallas_call | solution.py:568
  277.7 9.9 %all_to_all.70 = f32[4,4,3,16,128]{4,3,2,1,0:T(8,128)S(1)} all-to-all(f32[4,4,3,16,128]{4,3,2,1,0:T(8,128)} %get-tuple-element.95), channel_id=1, replica_groups=mesh['band'=4,'stream'=8] {'band'}, dimensions={0} | all-to-all | bytes 786432 | tf_op jit(solution)/shard_map/all_to_all | solution.py:719
  287.6 11.5 %all_to_all.71 = f32[4,4,3,16,128]{4,3,2,0,1:T(8,128)S(1)} all-to-all(f32[4,4,3,16,128]{4,3,2,0,1:T(8,128)S(1)} %copy.138), channel_id=1, replica_groups={{0,2,4,6},{1,3,5,7},{8,10,12,14},{9,11,13,15},{16,18,20,22},{17,19,21,2..., dimensions={1} | all-to-all | bytes 786432 | tf_op jit(solution)/shard_map/all_to_all | solution.py:720
  299.9 43.7 %band_backward.1 = (f32[48,16,128]{2,1,0:T(8,128)}, f32[2,128,1024]{2,1,0:T(8,128)}, f32[2,256,1024]{2,1,0:T(8,128)}, f32[512,128]{1,0:T(8,128)}, f32[1,2432]{1,0:T(1,128)}) custom-call(s32[1,41]{1,0:T(1,128)} %bitcast.191, f32[48,16,128]{2,1,0:T(8,128)} %bitcast.172, f32[41,16,128]{2,1,0:T(8,128)} %get-tuple-element.96.x, ...), custom_call_target="tpu_custom_call" | custom-call | tf_op jit(solution)/shard_map/band_backward/pallas_call | solution.py:497
  343.5 21.4 %all_to_all.72.dy_in = f32[4,12,16,128]{3,2,1,0:T(8,128)} all-to-all(f32[4,12,16,128]{3,2,1,0:T(8,128)} %bitcast.179), channel_id=1, replica_groups=mesh['band'=4,'stream'=8] {'band'}, dimensions={0} | all-to-all | bytes 786432 | tf_op jit(solution)/shard_map/all_to_all | solution.py:730
  364.9 50.6 %time_backward.1 = (f32[128,1280]{1,0:T(8,128)}, f32[12,256,128]{2,1,0:T(8,128)}, f32[12,1,640]{2,1,0:T(1,128)}, f32[2,128,1024]{2,1,0:T(8,128)}, f32[2,256,1024...) custom-call(s32[2,12]{1,0:T(2,128)} %pad_add_fusion.places_s, s32[2,3]{1,0:T(2,128)} %pad_add_fusion.1.clips, ...), custom_call_target="tpu_custom_call" | custom-call | tf_op jit(solution)/shard_map/time_backward/pallas_call | solution.py:401
  415.5 1.9 pad_maximum_fusion.2
  417.4 2.7 pad_maximum_fusion.1
  421.8 4.0 pad_maximum_fusion
  426.5 2.3 constant_dynamic-slice_fusion.1
  437.3 3.5 all-to-all-start.10
  440.8 2.9 fusion.1
  443.7 9.7 %all-to-all-done.10 = f32[4,3,128,64]{2,3,1,0:T(8,128)S(1)} async-done(((f32[4,3,128,64]{2,3,1,0:T(8,128)}), f32[4,3,128,64]{2,3,1,0:T(8,128)S(1)}, u32[]{:S(2)}, u32[]{:S(2)}) %all-to-all-start.10) | async-done | bytes 393248 | tf_op jit(solution)/shard_map/all_to_all | solution.py:629
  453.4 3.6 all-to-all-start.11
  457.7 2.5 copy.140
  460.2 37.6 %reduce-scatter.13.cloned.1.call-done = f32[2,2,128,128]{3,2,1,0:T(8,128)} async-done(((f32[2,2,128,1024]{3,2,1,0:T(8,128)}), f32[2,2,128,128]{3,2,1,0:T(8,128)}) %reduce-scatter.13.cloned.1.call-update) | async-done | bytes 262160 | tf_op jit(solution)/shard_map/reduce_scatter | solution.py:752
  497.9 64.1 %reduce-scatter.15.cloned.1.call-done = f32[2,2,256,128]{3,2,1,0:T(8,128)} async-done(((f32[2,2,256,1024]{3,2,1,0:T(8,128)}), f32[2,2,256,128]{3,2,1,0:T(8,128)}) %reduce-scatter.15.cloned.1.call-update) | async-done | bytes 524304 | tf_op jit(solution)/shard_map/reduce_scatter | solution.py:753
  565.3 2.4 multiply_reduce_fusion.1
  568.7 4.2 all-to-all-start.6
  576.8 23.1 %reduce-scatter.21.cloned.1.call-done = f32[304,2]{1,0:T(8,128)} async-done(((f32[2432,2]{1,0:T(8,128)}), f32[304,2]{1,0:T(8,128)}) %reduce-scatter.21.cloned.1.call-update) | async-done | bytes 2448
  600.8 9.7 %psum.39 = f32[2,304]{1,0:T(2,128)S(1)} all-reduce(f32[2,304]{1,0:T(2,128)S(1)} %copy.150), channel_id=1, replica_groups=mesh['band'=4,'stream'=8] {'band'}, use_global_device_ids=true, to_apply=%region_24.25 | all-reduce | flops 608 | bytes 4864 | tf_op jit(solution)/shard_map/psum | solution.py:759
  611.8 24.4 %reduce-scatter.19.cloned.1.call-done = f32[240,12]{1,0:T(8,128)} async-done(((f32[1920,12]{1,0:T(8,128)}), f32[240,12]{1,0:T(8,128)}) %reduce-scatter.19.cloned.1.call-update) | async-done | bytes 11536
  638.9 32.7 %reduce-scatter.11.cloned.1.call-done = f32[12,32,128]{2,1,0:T(8,128)} async-done(((f32[12,256,128]{2,1,0:T(8,128)}), f32[12,32,128]{2,1,0:T(8,128)}) %reduce-scatter.11.cloned.1.call-update) | async-done | bytes 196624 | tf_op jit(solution)/shard_map/reduce_scatter | solution.py:761
  671.6 1.6 multiply_reduce_fusion.14
  675.7 57.7 %all-reduce.6.cloned.1.call-done = (f32[2,64,1280]{2,0,1:T(2,128)}, f32[2,2,128,128]{3,2,1,0:T(8,128)}, f32[2,2,256,128]{3,2,1,0:T(8,128)}, f32[2,64,128]{2,1,0:T(8,128)}) async-done(((f32[2,64,1280]{2,0,1:T(2,128)}, f32[2,2,128,128]{3,2,1,0:T(8,128)}, f32[2,2,256,128]{3,2,1,0:T(8,128)}, f32[2,64,128]{2,1,0:T(8,128)}), (f32[2,64,1280]{2,0,1:T(2,128)}, f32[2,2,128,128]{3,2,1,0:T(8,128)}, ...) | async-done | bytes 1507344 | tf_op jit(solution)/shard_map/psum | solution.py:740
  733.4 1.6 multiply_reduce_fusion.11
  735.7 1.8 multiply_reduce_fusion.5
  740.3 2.7 stack.144
  743.6 4.6 all-to-all-start.12
  748.2 2.4 reshape.291
  750.6 2.3 copy.146
  752.9 3.5 all-to-all-done.12
  759.0 1.9 multiply_reduce_fusion.21
  761.5 2.2 multiply_reduce_fusion.15
  764.4 3.3 multiply_reduce_fusion.3
  768.4 2.7 multiply_reduce_fusion.9
  774.9 4.4 multiply_reduce_fusion
  779.3 1.6 multiply_reduce_fusion.6
  782.6 2.7 stack.153
  785.9 2.6 all-to-all-start.13
  788.5 1.9 slice_bitcast_fusion.4
  790.4 6.2 all-to-all-done.13
  806.7 2.4 multiply_subtract_fusion.1
  810.6 3.4 multiply_subtract_fusion
  (216 shorter events, 57.6 us)
Async XLA Ops:
  7.2 8.6 %copy-start.44 = (s32[41]{0:T(128)S(1)}, s32[41]{0:T(128)}, u32[]{:S(2)}) copy-start(s32[41]{0:T(128)} %param.36) | copy-start | bytes 496
  7.2 8.7 %copy-start.26 = (f32[12,240]{1,0:T(8,128)S(1)}, f32[12,240]{1,0:T(8,128)}, u32[]{:S(2)}) copy-start(f32[12,240]{1,0:T(8,128)} %param.41) | copy-start | bytes 34564
  7.2 35.8 %copy-start.45 = (s32[41]{0:T(128)S(1)}, s32[41]{0:T(128)}, u32[]{:S(2)}) copy-start(s32[41]{0:T(128)} %param.35) | copy-start | bytes 496
  7.2 37.1 %copy-start.46 = (s32[1,64]{1,0:T(1,128)S(1)}, s32[1,64]{1,0:T(1,128)}, u32[]{:S(2)}) copy-start(s32[1,64]{1,0:T(1,128)} %param.34) | copy-start | bytes 772
  7.2 37.3 %copy-start.34 = (f32[2,304]{1,0:T(2,128)S(1)}, f32[2,304]{1,0:T(2,128)}, u32[]{:S(2)}) copy-start(f32[2,304]{1,0:T(2,128)} %param.45) | copy-start | bytes 7300
  7.3 51.3 %copy-start.23 = (f32[64,2,1025]{2,1,0:T(2,128)S(1)}, f32[64,2,1025]{2,1,0:T(2,128)}, u32[]{:S(2)}) copy-start(f32[64,2,1025]{2,1,0:T(2,128)} %param.33) | copy-start | bytes 1574404
  7.3 131.6 %all-gather.8.cloned.1.call-start = ((), (), s32[]{:S(2)}) async-start(), calls=%async_computation.21 | async-start | bytes 2359296 | tf_op jit(solution)/shard_map/all_gather | solution.py:683
  8.0 134.0 %all-gather.10.cloned.1.call-start = ((), (), s32[]{:S(2)}) async-start(), calls=%async_computation.22 | async-start | bytes 4718592 | tf_op jit(solution)/shard_map/all_gather | solution.py:684
  8.8 51.5 %all-to-all-start.4 = ((f32[4,3,128,64]{2,3,1,0:T(8,128)}), f32[4,3,128,64]{2,3,1,0:T(8,128)S(1)}, u32[]{:S(2)}, u32[]{:S(2)}) async-start(f32[4,3,128,64]{2,3,1,0:T(8,128)} %bitcast.158), calls=%async_computation.4 | async-start | bytes 786432 | tf_op jit(solution)/shard_map/all_to_all | solution.py:605
  15.1 143.6 %all-gather.6.cloned.1.call-start = ((), (), s32[]{:S(2)}) async-start(), calls=%async_computation.20 | async-start | bytes 1769472 | tf_op jit(solution)/shard_map/all_gather | solution.py:681
  60.3 4.6 copy-start.13
  60.3 133.3 %all-to-all-start.5 = ((f32[4,3,64,512]{3,2,1,0:T(8,128)}), f32[4,3,64,512]{3,2,1,0:T(8,128)S(1)}, u32[]{:S(2)}, u32[]{:S(2)}) async-start(f32[4,3,64,512]{3,2,1,0:T(8,128)} %bitcast.35), calls=%async_computation.5 | async-start | bytes 3145728 | tf_op jit(solution)/shard_map/all_to_all | solution.py:605
  64.1 78.0 %copy-start.43 = (s32[41]{0:T(128)}, s32[41]{0:T(128)S(1)}, u32[]{:S(2)}) copy-start(s32[41]{0:T(128)S(1)} %add_add_fusion) | copy-start | bytes 496
  193.7 10.7 %all-to-all-start = ((f32[4,12,16,128]{3,2,1,0:T(8,128)}), f32[4,12,16,128]{3,2,1,0:T(8,128)S(1)}, u32[]{:S(2)}, u32[]{:S(2)}) async-start(f32[4,12,16,128]{3,2,1,0:T(8,128)} %get-tuple-element.92), calls=%async_computation | async-start | bytes 786432 | tf_op jit(solution)/shard_map/all_to_all | solution.py:707
  204.4 4.7 copy-start.11
  204.4 34.5 %all-to-all-start.3 = ((f32[4,3,64,256]{3,2,1,0:T(8,128)}), f32[4,3,64,256]{3,2,1,0:T(8,128)S(1)}, u32[]{:S(2)}, u32[]{:S(2)}) async-start(f32[4,3,64,256]{3,2,1,0:T(8,128)} %bitcast.27), calls=%async_computation.3 | async-start | bytes 1572864 | tf_op jit(solution)/shard_map/all_to_all | solution.py:693
  207.9 52.4 %collective-permute-start.1 = (f32[4,3,64,512]{3,2,1,0:T(8,128)S(1)}, f32[4,3,64,512]{3,2,1,0:T(8,128)}, u32[]{:S(2)}, u32[]{:S(2)}) collective-permute-start(f32[4,3,64,512]{3,2,1,0:T(8,128)S(1)} %all-to-all-done.5), channel_id=1, source_target_pairs={{0,1},{1,0},{2,3},{3,2},{4,5},{5,4},{6,7},{7,6},{8,9},{9,8},{10,11... | collective-permute-start | bytes 4718600 | tf_op jit(solution)/shard_map/ppermute | solution.py:613
  208.0 36.8 %collective-permute-start = (f32[4,3,128,64]{2,3,1,0:T(8,128)S(1)}, f32[4,3,128,64]{2,3,1,0:T(8,128)}, u32[]{:S(2)}, u32[]{:S(2)}) collective-permute-start(f32[4,3,128,64]{2,3,1,0:T(8,128)S(1)} %all-to-all-done.4), channel_id=1, source_target_pairs={{0,1},{1,0},{2,3},{3,2},{4,5},{5,4},{6,7},{7,6},{8,9},{9,8},{10,11... | collective-permute-start | bytes 1179656 | tf_op jit(solution)/shard_map/ppermute | solution.py:613
  237.1 7.1 slice-start
  238.9 17.1 %all-to-all-start.1 = ((f32[4,4,3,16,128]{4,3,2,0,1:T(8,128)}), f32[4,4,3,16,128]{4,3,2,0,1:T(8,128)S(1)}, u32[]{:S(2)}, u32[]{:S(2)}) async-start(f32[4,4,3,16,128]{4,3,2,0,1:T(8,128)} %copy.130), calls=%async_computation.1 | async-start | bytes 786432 | tf_op jit(solution)/shard_map/all_to_all | solution.py:715
  256.8 9.5 %all-to-all-start.2 = ((f32[4,4,3,16,128]{4,3,2,1,0:T(8,128)}), f32[4,4,3,16,128]{4,3,2,1,0:T(8,128)S(1)}, u32[]{:S(2)}, u32[]{:S(2)}) async-start(f32[4,4,3,16,128]{4,3,2,1,0:T(8,128)} %copy.131), calls=%async_computation.2 | async-start | bytes 786432 | tf_op jit(solution)/shard_map/all_to_all | solution.py:716
  260.3 200.0 %reduce-scatter.17.cloned.1.call-start = ((), (), s32[]{:S(2)}) async-start(), calls=%async_computation.26 | async-start | bytes 589824 | tf_op jit(solution)/shard_map/reduce_scatter | solution.py:754
  364.9 50.6 %copy-start.27 = (f32[512,128]{1,0:T(8,128)S(1)}, f32[512,128]{1,0:T(8,128)}, u32[]{:S(2)}) copy-start(f32[512,128]{1,0:T(8,128)} %get-tuple-element.130) | copy-start | bytes 786436
  415.5 2.0 copy-start.15
  417.4 80.5 %reduce-scatter.13.cloned.1.call-start = ((), (), s32[]{:S(2)}) async-start(), calls=%async_computation.24 | async-start | bytes 2359296 | tf_op jit(solution)/shard_map/reduce_scatter | solution.py:752
  420.2 141.7 %reduce-scatter.15.cloned.1.call-start = ((), (), s32[]{:S(2)}) async-start(), calls=%async_computation.25 | async-start | bytes 4718592 | tf_op jit(solution)/shard_map/reduce_scatter | solution.py:753
  425.8 174.0 %reduce-scatter.21.cloned.1.call-start = ((), (), s32[]{:S(2)}) async-start(), calls=%async_computation.28 | async-start | bytes 1400832
  428.8 3.2 copy-start.36
  430.1 10.7 %collective-permute-start.3 = (f32[4,3,64,512]{3,2,1,0:T(8,128)}, f32[4,3,64,512]{3,2,1,0:T(8,128)}, u32[]{:S(2)}, u32[]{:S(2)}) collective-permute-start(f32[4,3,64,512]{3,2,1,0:T(8,128)} %bitcast.153), channel_id=1, source_target_pairs={{0,1},{1,0},{2,3},{3,2},{4,5},{5,4},{6,7},{7,6},{8,9},{9,8},{10,11... | collective-permute-start | bytes 4718600 | tf_op jit(solution)/shard_map/ppermute | solution.py:622
  432.0 204.3 %reduce-scatter.19.cloned.1.call-start = ((), (), s32[]{:S(2)}) async-start(), calls=%async_computation.27 | async-start | bytes 1105920
  432.1 2.2 copy-start.19
  433.5 238.1 %reduce-scatter.11.cloned.1.call-start = ((), (), s32[]{:S(2)}) async-start(), calls=%async_computation.23 | async-start | bytes 1769472 | tf_op jit(solution)/shard_map/reduce_scatter | solution.py:761
  434.6 1.9 collective-permute-start.2
  437.3 16.1 %all-to-all-start.10 = ((f32[4,3,128,64]{2,3,1,0:T(8,128)}), f32[4,3,128,64]{2,3,1,0:T(8,128)S(1)}, u32[]{:S(2)}, u32[]{:S(2)}) async-start(f32[4,3,128,64]{2,3,1,0:T(8,128)} %copy.143), calls=%async_computation.11 | async-start | bytes 786432 | tf_op jit(solution)/shard_map/all_to_all | solution.py:629
  443.7 13.4 %copy-start.14 = (f32[2,64,128]{2,1,0:T(8,128)S(1)}, f32[2,64,128]{2,1,0:T(8,128)}, u32[]{:S(2)}) copy-start(f32[2,64,128]{2,1,0:T(8,128)} %param.44) | copy-start | bytes 196612
  453.4 115.3 %all-to-all-start.11 = ((f32[4,3,64,512]{3,2,1,0:T(8,128)}), f32[4,3,64,512]{3,2,1,0:T(8,128)S(1)}, u32[]{:S(2)}, u32[]{:S(2)}) async-start(f32[4,3,64,512]{3,2,1,0:T(8,128)} %fusion.1), calls=%async_computation.12 | async-start | bytes 3145728 | tf_op jit(solution)/shard_map/all_to_all | solution.py:629
  457.0 105.6 %copy-start.5 = (f32[12,32,128]{2,1,0:T(8,128)S(1)}, f32[12,32,128]{2,1,0:T(8,128)}, u32[]{:S(2)}) copy-start(f32[12,32,128]{2,1,0:T(8,128)} %param.38) | copy-start | bytes 589828
  457.0 106.2 %copy-start.4 = (f32[2,2,128,128]{3,2,1,0:T(8,128)S(1)}, f32[2,2,128,128]{3,2,1,0:T(8,128)}, u32[]{:S(2)}) copy-start(f32[2,2,128,128]{3,2,1,0:T(8,128)} %param.42) | copy-start | bytes 786436
  457.0 276.4 %all-reduce.6.cloned.1.call-start = ((), (), s32[]{:S(2)}) async-start(), calls=%async_computation.29 | async-start | bytes 3014656 | tf_op jit(solution)/shard_map/psum | solution.py:740
  457.7 106.2 %copy-start.3 = (f32[12,128,64]{1,2,0:T(8,128)S(1)}, f32[12,128,64]{1,2,0:T(8,128)}, u32[]{:S(2)}) copy-start(f32[12,128,64]{1,2,0:T(8,128)} %param.39) | copy-start | bytes 1179652
  457.7 106.9 %copy-start = (f32[2,2,256,128]{3,2,1,0:T(8,128)S(1)}, f32[2,2,256,128]{3,2,1,0:T(8,128)}, u32[]{:S(2)}) copy-start(f32[2,2,256,128]{3,2,1,0:T(8,128)} %param.43) | copy-start | bytes 1572868
  561.9 5.8 copy-start.18
  567.7 5.1 copy-start.35
  568.7 174.3 %all-to-all-start.6 = ((f32[4,3,64,256]{3,2,1,0:T(8,128)}), f32[4,3,64,256]{3,2,1,0:T(8,128)}, u32[]{:S(2)}, u32[]{:S(2)}) async-start(f32[4,3,64,256]{3,2,1,0:T(8,128)} %bitcast.163), calls=%async_computation.6 | async-start | bytes 1572864 | tf_op jit(solution)/shard_map/all_to_all | solution.py:738
  610.6 25.7 %copy-start.37 = (f32[2,304]{1,0:T(2,128)}, f32[2,304]{1,0:T(2,128)S(1)}, u32[]{:S(2)}) copy-start(f32[2,304]{1,0:T(2,128)S(1)} %psum.39) | copy-start | bytes 7300
  637.2 106.4 %copy-start.30 = (f32[12,240]{1,0:T(8,128)}, f32[12,240]{1,0:T(8,128)S(1)}, u32[]{:S(2)}) copy-start(f32[12,240]{1,0:T(8,128)S(1)} %copy.148) | copy-start | bytes 34564
  743.6 12.8 %all-to-all-start.12 = ((f32[32,8,128]{2,1,0:T(8,128)}), f32[32,8,128]{2,1,0:T(8,128)S(1)}, u32[]{:S(2)}, u32[]{:S(2)}) async-start(f32[32,8,128]{2,1,0:T(8,128)} %broadcast_in_dim.45), calls=%async_computation.16 | async-start | bytes 262144 | tf_op jit(solution)/shard_map/all_to_all | solution.py:599
  767.7 4.0 copy-start.31
  767.7 4.0 copy-start.38
  767.7 4.0 copy-start.39
  773.0 1.9 copy-start.8
  774.9 4.4 copy-start.24
  774.9 4.4 copy-start.25
  779.3 31.4 %copy-start.1 = (f32[12,64,512]{2,1,0:T(8,128)}, f32[12,64,512]{2,1,0:T(8,128)S(1)}, u32[]{:S(2)}) copy-start(f32[12,64,512]{2,1,0:T(8,128)S(1)} %get-tuple-element.264) | copy-start | bytes 4718596
  779.3 1.7 copy-start.28
  779.3 1.8 copy-start.29
  781.0 33.0 %copy-start.9 = (f32[12,128,64]{1,2,0:T(8,128)}, f32[12,128,64]{1,2,0:T(8,128)S(1)}, u32[]{:S(2)}) copy-start(f32[12,128,64]{1,2,0:T(8,128)S(1)} %get-tuple-element.267) | copy-start | bytes 1179652
  785.9 10.8 %all-to-all-start.13 = ((f32[32,8,128]{2,1,0:T(8,128)}), f32[32,8,128]{2,1,0:T(8,128)S(1)}, u32[]{:S(2)}, u32[]{:S(2)}) async-start(f32[32,8,128]{2,1,0:T(8,128)} %broadcast_in_dim.48), calls=%async_computation.17 | async-start | bytes 262144 | tf_op jit(solution)/shard_map/all_to_all | solution.py:599
  797.3 11.8 %copy-start.16 = (f32[2,2,128,128]{3,2,1,0:T(8,128)S(1)}, f32[2,2,128,128]{3,2,1,0:T(8,128)}, u32[]{:S(2)}) copy-start(f32[2,2,128,128]{3,2,1,0:T(8,128)} %get-tuple-element.258) | copy-start | bytes 786436
  797.3 11.8 %copy-start.17 = (f32[2,2,128,128]{3,2,1,0:T(8,128)S(1)}, f32[2,2,128,128]{3,2,1,0:T(8,128)}, u32[]{:S(2)}) copy-start(f32[2,2,128,128]{3,2,1,0:T(8,128)} %get-tuple-element.259) | copy-start | bytes 786436
  806.7 3.3 copy-start.32
  806.7 3.3 copy-start.33
  806.7 3.9 copy-start.2
  810.6 3.4 copy-start.10
  (9 other events, 11.5 us)
Sparse Core Ops, SparseCore 0:
  9.7 38.7 all-gather.7
  50.1 82.0 all-gather.9
  133.8 24.8 all-gather.5
  417.5 28.5 reduce-scatter.16
  448.4 49.4 reduce-scatter.12
  500.1 61.7 reduce-scatter.14
  564.9 34.9 reduce-scatter.20
  602.2 33.9 reduce-scatter.18
  639.1 32.3 reduce-scatter.10
  674.9 58.4 all-reduce.5

commit v2 on v1

v2 whole, which is shorter than its diff:
```python
from functools import partial
import math

import jax
import jax.numpy as jnp
from jax import lax
from jax.experimental import pallas as pl
from jax.experimental.pallas import tpu as pltpu
from jax.sharding import PartitionSpec as P

STEP = 10
CLIP_NORM = 5.0
LEARN_RATE = 0.5
BETA_ONE = 0.9
BETA_TWO = 0.999
ADAM_EPS = 1e-06
DECAY_RATE = 0.01
NORM_EPS = 1e-05
VAR_FLOOR = 0.25
CLIPS = 3
CLIP_MOST = 32
LANES = 128
VMEM_BYTES = 60 * 1024 * 1024
CORES = 2
MESH = pl.DeviceIdType.MESH

AB = (((1,), (0,)), ((), ()))
ABT = (((1,), (1,)), ((), ()))
ATB = (((0,), (0,)), ((), ()))


def split(x):
    hi = x.astype(jnp.bfloat16)
    lo = (x - hi.astype(jnp.float32)).astype(jnp.bfloat16)
    return hi, lo


def dot1(a, b, dims):
    return lax.dot_general(a, b, dims, preferred_element_type=jnp.float32)


def dot_parts(a, b, dims):
    return dot1(a[0], b[0], dims) + (dot1(a[1], b[0], dims) + dot1(a[0], b[1], dims))


def dot3(a, b, dims):
    return dot_parts(split(a), split(b), dims)


def sigmoid(x):
    return 0.5 * jnp.tanh(0.5 * x) + 0.5


def norm_stats(x):
    center = x - jnp.mean(x, axis=-1, keepdims=True)
    spread = jnp.mean(center * center, axis=-1, keepdims=True)
    scale = lax.rsqrt(spread + NORM_EPS)
    return center * scale, scale


def norm_back(grad_unit, unit, scale):
    first = jnp.mean(grad_unit, axis=-1, keepdims=True)
    second = jnp.mean(grad_unit * unit, axis=-1, keepdims=True)
    return scale * (grad_unit - first - unit * second)


def column_sum(x):
    return jnp.sum(x, axis=0, keepdims=True)


def pack_rows(dmodel, hidden):
    blocks = 4 * hidden // LANES
    out_rows = 2 * hidden // blocks
    weight_rows = 2 * dmodel + 2 * hidden + out_rows
    share = (2 * dmodel + 8 * hidden + dmodel) // blocks
    vec_rows = -(-share // LANES)
    return blocks, out_rows, weight_rows, share, vec_rows, -(-(weight_rows + vec_rows) // 32) * 32


def pack_rnn(w_in, w_rec, w_out, vec, rows, share):
    count = w_in.shape[2] // LANES
    parts = [
        w.reshape(2 * w.shape[1], count, LANES).transpose(1, 0, 2) for w in (w_in, w_rec)
    ] + [w_out.reshape(count, -1, LANES)]
    used = sum(p.shape[1] for p in parts)
    flat = jnp.pad(vec.reshape(count, share), ((0, 0), (0, (rows - used) * LANES - share)))
    return jnp.concatenate(parts + [flat.reshape(count, rows - used, LANES)], axis=1)


def unpack_rnn(pack, dmodel, hidden):
    blocks, out_rows, weight_rows, share, vec_rows, rows = pack_rows(dmodel, hidden)
    count = pack.shape[0]
    cuts = (0, 2 * dmodel, 2 * dmodel + 2 * hidden)
    w_in = pack[:, : cuts[1]].reshape(count, 2, dmodel, LANES).transpose(1, 2, 0, 3)
    w_rec = pack[:, cuts[1] : cuts[2]].reshape(count, 2, hidden, LANES).transpose(1, 2, 0, 3)
    return (
        w_in.reshape(2, dmodel, count * LANES),
        w_rec.reshape(2, hidden, count * LANES),
        pack[:, cuts[2] : weight_rows].reshape(count * out_rows, LANES),
        unpack_vec(pack, weight_rows, vec_rows, share),
    )


def unpack_vec(pack, weight_rows, vec_rows, share):
    count = pack.shape[0]
    flat = pack[:, weight_rows : weight_rows + vec_rows].reshape(count, vec_rows * LANES)
    return flat[:, :share].reshape(1, count * share)


class Pack:
    def __init__(self, ref, dmodel, hidden):
        self.ref, self.dmodel, self.hidden = ref, dmodel, hidden
        self.blocks, self.out_rows = pack_rows(dmodel, hidden)[:2]

    def intake(self, e, first, last):
        rows = slice(e * self.dmodel, (e + 1) * self.dmodel)
        return jnp.concatenate([self.ref[k, rows] for k in range(first, last)], axis=1)

    def recurrence(self, e, k):
        base = 2 * self.dmodel + e * self.hidden
        return self.ref[k, base : base + self.hidden]

    def outtake(self, e):
        base = 2 * self.dmodel + 2 * self.hidden
        half = self.blocks // 2
        return jnp.concatenate(
            [self.ref[k, base : base + self.out_rows] for k in range(half * e, half * (e + 1))], axis=0
        )

    def put(self, k, base, value):
        self.ref[k, base : base + value.shape[0]] = value

    def put_intake(self, e, q, value):
        for h in range(value.shape[1] // LANES):
            self.put(q * value.shape[1] // LANES + h, e * self.dmodel, value[:, h * LANES : (h + 1) * LANES])

    def put_recurrence(self, e, q, value):
        base = 2 * self.dmodel + e * self.hidden
        for h in range(value.shape[1] // LANES):
            self.put(q * value.shape[1] // LANES + h, base, value[:, h * LANES : (h + 1) * LANES])

    def put_outtake(self, e, value):
        base = 2 * self.dmodel + 2 * self.hidden
        for k in range(self.blocks // 2):
            self.put(self.blocks // 2 * e + k, base, value[k * self.out_rows : (k + 1) * self.out_rows])

    def put_vec(self, value):
        unused, unused, base, share, vec_rows, rows = pack_rows(self.dmodel, self.hidden)
        for k in range(self.blocks):
            self.ref[k, base:rows] = jnp.zeros((rows - base, LANES), jnp.float32)
            for r in range(vec_rows):
                width = min(LANES, share - r * LANES)
                at = k * share + r * LANES
                self.ref[k, base + r : base + r + 1, :width] = value[:, at : at + width]


def split_recurrence(pack, hi_ref, lo_ref):
    for e in range(2):
        for k in range(pack.blocks):
            part = slice(k * LANES, (k + 1) * LANES)
            hi_ref[e, :, part], lo_ref[e, :, part] = split(pack.recurrence(e, k))


def gates_forward(x_flat, act, pack, vec, rows, block):
    hidden4 = 4 * pack.hidden
    dmodel = pack.dmodel
    parts = [split(pack.intake(e, 0, pack.blocks)) for e in range(2)]

    def one(r, carry):
        start = pl.multiple_of(r * block, block)
        unit, unused = norm_stats(x_flat(start, block))
        n = split(unit * (1.0 + vec[0:1, :dmodel]) + vec[0:1, dmodel : 2 * dmodel])
        for e in range(2):
            bias = vec[0:1, 2 * dmodel + hidden4 * e : 2 * dmodel + hidden4 * (e + 1)]
            z = dot_parts(n, parts[e], AB) + bias
            act[e][pl.ds(r * (block // 16), block // 16)] = z.reshape(block // 16, 16, hidden4)
        return carry

    lax.fori_loop(0, rows // block, one, 0)


def run_forward(steps, places, act, tc, cp, hp, h, pack, hi_ref, lo_ref, state, memory):
    hidden = pack.hidden
    split_recurrence(pack, hi_ref, lo_ref)
    for e in range(2):
        state[e][...] = jnp.zeros_like(state[e])
        memory[e][...] = jnp.zeros_like(memory[e])

    def step(j, carry):
        work = []
        for e in range(2):
            at = places(e, j)
            prior = state[e][...]
            hi, lo = split(prior)
            rows = prior.shape[0]
            first = dot1(jnp.concatenate([hi, lo], axis=0), hi_ref[e], AB)
            drive = [act[e][p] for p in at]
            drive = drive[0] if len(drive) == 1 else jnp.concatenate(drive, axis=0)
            z = first[:rows] + first[rows:] + dot1(hi, lo_ref[e], AB) + drive
            work.append((at, prior, z))
        for e in range(2):
            at, prior, z = work[e]
            ingate = sigmoid(z[:, :hidden])
            forget = sigmoid(z[:, hidden : 2 * hidden])
            candidate = jnp.tanh(z[:, 2 * hidden : 3 * hidden])
            outgate = sigmoid(z[:, 3 * hidden :])
            before = memory[e][...]
            now = forget * before + ingate * candidate
            squashed = jnp.tanh(now)
            out = outgate * squashed
            memory[e][...] = now
            state[e][...] = out
            for k, p in enumerate(at):
                part = slice(16 * k, 16 * (k + 1))
                act[e][p, :, :hidden] = ingate[part]
                act[e][p, :, hidden : 2 * hidden] = forget[part]
                act[e][p, :, 2 * hidden : 3 * hidden] = candidate[part]
                act[e][p, :, 3 * hidden :] = outgate[part]
                tc[e][p] = squashed[part]
                cp[e][p] = before[part]
                hp[e][p] = prior[part]
                h[e][p] = out[part]
        return carry

    lax.fori_loop(0, steps, step, 0)


def output_forward(count, h, pack, vec):
    hidden = h[0].shape[2]
    dmodel = pack.dmodel
    total = vec[0:1, vec.shape[1] - dmodel :]
    for e in range(2):
        states = h[e][:count].reshape(count * 16, hidden)
        total = total + dot3(states, pack.outtake(e), AB)
    return total


def run_backward(steps, places, act, dz_ref, tc, cp, dh, pack, hi_ref, lo_ref, grad_h, grad_c):
    hidden = pack.hidden
    split_recurrence(pack, hi_ref, lo_ref)
    for e in range(2):
        grad_h[e][...] = jnp.zeros_like(grad_h[e])
        grad_c[e][...] = jnp.zeros_like(grad_c[e])

    def load(ref, at):
        got = [ref[p] for p in at]
        return got[0] if len(got) == 1 else jnp.concatenate(got, axis=0)

    def step(back, carry):
        j = steps - 1 - back
        work = []
        for e in range(2):
            at = places(e, j)
            gates = load(act[e], at)
            ingate = gates[:, :hidden]
            forget = gates[:, hidden : 2 * hidden]
            candidate = gates[:, 2 * hidden : 3 * hidden]
            outgate = gates[:, 3 * hidden :]
            squashed = load(tc[e], at)
            before = load(cp[e], at)
            total_h = load(dh[e], at) + grad_h[e][...]
            total_c = grad_c[e][...] + total_h * outgate * (1.0 - squashed * squashed)
            dz = jnp.concatenate(
                [
                    total_c * candidate * ingate * (1.0 - ingate),
                    total_c * before * forget * (1.0 - forget),
                    total_c * ingate * (1.0 - candidate * candidate),
                    total_h * squashed * outgate * (1.0 - outgate),
                ],
                axis=1,
            )
            grad_c[e][...] = total_c * forget
            for k, p in enumerate(at):
                dz_ref[e][p] = dz[16 * k : 16 * (k + 1)]
            work.append(dz)
        for e in range(2):
            hi, lo = split(work[e])
            rows = hi.shape[0]
            first = dot1(jnp.concatenate([hi, lo], axis=0), hi_ref[e], ABT)
            grad_h[e][...] = first[:rows] + first[rows:] + dot1(hi, lo_ref[e], ABT)
        return carry

    lax.fori_loop(0, steps, step, 0)


def states_backward(count, dy_flat, dh, h, pack, g_pack):
    hidden = h[0].shape[2]
    dy = split(dy_flat)
    for e in range(2):
        dh[e][:count] = dot_parts(dy, split(pack.outtake(e)), ABT).reshape(count, 16, hidden)
        g_pack.put_outtake(e, dot3_parts_first(h[e][:count].reshape(count * 16, hidden), dy))


def dot3_parts_first(a, b_parts):
    return dot_parts(split(a), b_parts, ATB)


def gates_backward(count, x_flat, dy_flat, dz_ref, hp, pack, vec, g_pack, g_vec):
    dmodel = pack.dmodel
    hidden = hp[0].shape[2]
    hidden4 = 4 * hidden
    rows = count * 16
    unit, scale = norm_stats(x_flat)
    gain = 1.0 + vec[0:1, :dmodel]
    n = split(unit * gain + vec[0:1, dmodel : 2 * dmodel])
    dn = jnp.zeros((rows, dmodel), jnp.float32)
    for e in range(2):
        before = split(hp[e][:count].reshape(rows, hidden))
        for q in range(4):
            part = slice(hidden * q, hidden * (q + 1))
            dz_q = dz_ref[e][:count, :, part].reshape(rows, hidden)
            dz = split(dz_q)
            g_pack.put_recurrence(e, q, dot_parts(before, dz, ATB))
            g_pack.put_intake(e, q, dot_parts(n, dz, ATB))
            dn = dn + dot_parts(dz, split(pack.intake(e, q * pack.blocks // 4, (q + 1) * pack.blocks // 4)), ABT)
            base = 2 * dmodel + hidden4 * e + hidden * q
            g_vec[0:1, base : base + hidden] = column_sum(dz_q)
    g_vec[0:1, :dmodel] = column_sum(dn * unit)
    g_vec[0:1, dmodel : 2 * dmodel] = column_sum(dn)
    g_vec[0:1, vec.shape[1] - dmodel :] = column_sum(dy_flat)
    g_pack.put_vec(g_vec[...])
    return dy_flat + norm_back(dn * gain, unit, scale)


def clip_places(clips, spare):
    def places(e, j):
        found = []
        for c in range(CLIPS):
            start, length = clips[0, c], clips[1, c]
            frame = start + j if e == 0 else start + length - 1 - j
            found.append(jnp.where(j < length, frame, spare))
        return found

    return places


def window_of(edge):
    base = pl.multiple_of((edge // LANES) * LANES, LANES)
    return base, lax.rem(edge, LANES)


def split_rows(spec, edge, width, frames):
    wmax = LANES
    base, shift = window_of(edge)
    window = spec[:, pl.ds(base, 2 * LANES)]
    taken = pltpu.roll(window, lax.rem(2 * LANES - shift, 2 * LANES), 1)[:, :wmax]
    taken = jnp.concatenate([taken[:frames], taken[frames:]], axis=1)
    lane = lax.broadcasted_iota(jnp.int32, (frames, wmax), 1)
    inside = (lane < width).astype(jnp.float32)
    valid = jnp.concatenate([inside, inside], axis=1)
    entries = jnp.maximum(2 * width, 1).astype(jnp.float32)
    mean = jnp.sum(taken * valid, axis=-1, keepdims=True) / entries
    center = (taken - mean) * valid
    spread = jnp.sum(center * center, axis=-1, keepdims=True) / entries
    scale = lax.rsqrt(jnp.maximum(spread, VAR_FLOOR))
    moving = jnp.where(spread > VAR_FLOOR, 1.0, jnp.where(spread == VAR_FLOOR, 0.5, 0.0))
    return center * scale, scale, valid, moving, entries


def slot_weights(w_split, s, slot_rows):
    count = w_split.shape[0]
    at = pl.ds(pl.multiple_of(s * slot_rows, slot_rows), slot_rows)
    return jnp.concatenate([w_split[k, at, :] for k in range(count)], axis=0)


def time_forward_kernel(
    slot_rows, places_s, clips, spec, w_split, v_band, rnn, vec,
    out, x, act0, act1, tc0, tc1, cp0, cp1, hp0, hp1, h0, h1,
    hi_ref, lo_ref, s0, s1, m0, m1, y, mixed,
):
    slots = v_band.shape[0]
    frames, unused, dmodel = x.shape
    wide = w_split.shape[0] * slot_rows
    pack = Pack(rnn, dmodel, h0.shape[2])
    x[...] = jnp.zeros_like(x)
    for a in (act0, act1):
        a[frames] = jnp.zeros_like(a[frames])

    def one_slot(s, carry):
        unit, unused, valid, moving, entries = split_rows(spec, places_s[0, s], places_s[1, s], frames)
        row = v_band[s]
        z = (unit * (1.0 + row[:, :wide]) + row[:, wide : 2 * wide]) * valid
        y[s] = dot3(z, slot_weights(w_split, s, slot_rows), AB) + row[:, 2 * wide : 2 * wide + dmodel]
        return carry

    lax.fori_loop(0, slots, one_slot, 0)
    for s in range(slots):
        x[:, s, :] = y[s]
    act = (act0, act1)

    def x_flat(start, size):
        return x[pl.ds(start // 16, size // 16)].reshape(size, dmodel)

    gates_forward(x_flat, act, pack, vec, frames * 16, 256)
    run_forward(
        CLIP_MOST, clip_places(clips, frames), act, (tc0, tc1), (cp0, cp1), (hp0, hp1), (h0, h1),
        pack, hi_ref, lo_ref, (s0, s1), (m0, m1),
    )
    total = output_forward(frames, (h0, h1), pack, vec)
    x_all = x[...].reshape(frames * 16, dmodel)
    mixed[...] = (x_all + total).reshape(frames, 16, dmodel)
    parts, unused_slots, quarter, unused = out.shape
    for s in range(slots):
        for q in range(parts):
            out[q, s] = mixed[q * quarter : (q + 1) * quarter, s, :]


def f32(shape):
    return jax.ShapeDtypeStruct(shape, jnp.float32)


def saved_shapes(count, hidden):
    wide = [f32((count, 16, 4 * hidden))] * 2
    thin = [f32((count, 16, hidden))] * 8
    return wide + thin


def rec_scratch(rows, hidden):
    return [
        pltpu.VMEM((2, hidden, 4 * hidden), jnp.bfloat16),
        pltpu.VMEM((2, hidden, 4 * hidden), jnp.bfloat16),
    ] + [pltpu.VMEM((rows, hidden), jnp.float32)] * 4


SMEM = pl.BlockSpec(memory_space=pltpu.SMEM)
VMEM = pl.BlockSpec(memory_space=pltpu.VMEM)
ANY = pl.BlockSpec(memory_space=pl.ANY)
PARAMS = pltpu.CompilerParams(vmem_limit_bytes=VMEM_BYTES)


def cost(micros):
    return pl.CostEstimate(flops=int(micros * 1.1e9), bytes_accessed=int(micros * 3e6), transcendentals=0)


def time_forward(slot_places, clips, spec, w_split, v_band, rnn, vec, parts, slot_rows, hidden):
    slots = v_band.shape[0]
    dmodel = w_split.shape[2]
    frames = spec.shape[0] // 2
    return pl.pallas_call(
        partial(time_forward_kernel, slot_rows),
        out_shape=[f32((parts, slots, frames // parts, dmodel)), f32((frames, 16, dmodel))]
        + saved_shapes(frames + 1, hidden),
        in_specs=[SMEM, SMEM] + [VMEM] * 5,
        out_specs=[VMEM] * 12,
        scratch_shapes=rec_scratch(16 * CLIPS, hidden)
        + [pltpu.VMEM((slots, frames, dmodel), jnp.float32)]
        + [pltpu.VMEM((frames, 16, dmodel), jnp.float32)],
        compiler_params=PARAMS,
        cost_estimate=cost(35),
        name="time_forward",
    )(slot_places, clips, spec, w_split, v_band, rnn, vec)


def time_backward_kernel(
    slot_rows, places_s, clips, dy_in, spec, x, act0, act1, tc0, tc1, cp0, cp1, hp0, hp1, h0, h1,
    w_split, v_band, rnn, vec,
    d_spec, g_split, g_band, g_rnn,
    hi_ref, lo_ref, s0, s1, m0, m1, dy, g_vec, dh0, dh1, dz0, dz1,
):
    slots = v_band.shape[0]
    frames, unused, dmodel = x.shape
    wide = w_split.shape[0] * slot_rows
    parts, unused_slots, quarter, unused = dy_in.shape
    pack, g_pack = Pack(rnn, dmodel, h0.shape[2]), Pack(g_rnn, dmodel, h0.shape[2])
    dy[...] = jnp.zeros_like(dy)
    for s in range(slots):
        for q in range(parts):
            dy[q * quarter : (q + 1) * quarter, s, :] = dy_in[q, s]
    dy_flat = dy[...].reshape(frames * 16, dmodel)
    states_backward(frames, dy_flat, (dh0, dh1), (h0, h1), pack, g_pack)
    for d in (dh0, dh1):
        d[frames] = jnp.zeros_like(d[frames])
    run_backward(
        CLIP_MOST, clip_places(clips, frames), (act0, act1), (dz0, dz1), (tc0, tc1), (cp0, cp1),
        (dh0, dh1), pack, hi_ref, lo_ref, (s0, s1), (m0, m1),
    )
    x_flat = x[...].reshape(frames * 16, dmodel)
    dx = gates_backward(
        frames, x_flat, dy[...].reshape(frames * 16, dmodel), (dz0, dz1), (hp0, hp1), pack, vec, g_pack, g_vec
    )
    dy[...] = dx.reshape(frames, 16, dmodel)
    d_spec[...] = jnp.zeros_like(d_spec)
    g_split[:, slots * slot_rows :] = jnp.zeros_like(g_split[:, slots * slot_rows :])

    for s in range(slots):
        edge, width = places_s[0, s], places_s[1, s]
        unit, scale, valid, moving, entries = split_rows(spec, edge, width, frames)
        row = v_band[s]
        gain = 1.0 + row[:, :wide]
        z = (unit * gain + row[:, wide : 2 * wide]) * valid
        demb = dy[:, s, :]
        demb_parts = split(demb)
        g_slot = dot_parts(split(z), demb_parts, ATB)
        for k in range(w_split.shape[0]):
            g_split[k, s * slot_rows : (s + 1) * slot_rows] = g_slot[k * slot_rows : (k + 1) * slot_rows]
        dz = dot_parts(demb_parts, split(slot_weights(w_split, s, slot_rows)), ABT) * valid
        g_band[s, :, :wide] = column_sum(dz * unit)
        g_band[s, :, wide : 2 * wide] = column_sum(dz)
        g_band[s, :, 2 * wide :] = column_sum(demb)
        du = dz * gain
        first = jnp.sum(du, axis=-1, keepdims=True) / entries
        second = jnp.sum(du * unit, axis=-1, keepdims=True) / entries
        dt = scale * (du - first - moving * unit * second) * valid
        base, shift = window_of(edge)
        stacked = jnp.concatenate([dt[:, :LANES], dt[:, LANES:]], axis=0)
        padded = jnp.concatenate([stacked, jnp.zeros_like(stacked)], axis=1)
        d_spec[:, pl.ds(base, 2 * LANES)] += pltpu.roll(padded, shift, 1)


def time_backward(slot_places, clips, dy, spec, saved, w_split, v_band, rnn, vec, slot_rows, hidden):
    slots = v_band.shape[0]
    dmodel = w_split.shape[2]
    wide = w_split.shape[0] * slot_rows
    frames = spec.shape[0] // 2
    return pl.pallas_call(
        partial(time_backward_kernel, slot_rows),
        out_shape=[
            f32(spec.shape), f32(w_split.shape), f32((slots, 1, 2 * wide + dmodel)), f32(rnn.shape),
        ],
        in_specs=[SMEM, SMEM] + [VMEM] * (3 + 10 + 4),
        out_specs=[VMEM] * 4,
        scratch_shapes=rec_scratch(16 * CLIPS, hidden)
        + [pltpu.VMEM((frames, 16, dmodel), jnp.float32), pltpu.VMEM(vec.shape, jnp.float32)]
        + [pltpu.VMEM((frames + 1, 16, hidden), jnp.float32)] * 2
        + [pltpu.VMEM((frames + 1, 16, 4 * hidden), jnp.float32)] * 2,
        compiler_params=PARAMS,
        cost_estimate=cost(50),
        name="time_backward",
    )(slot_places, clips, dy, spec, *saved, w_split, v_band, rnn, vec)


def band_places(bands):
    return lambda e, j: [j if e == 0 else bands - 1 - j]


def band_forward_kernel(
    slot_of, arrived, rnn, vec,
    out, x, act0, act1, tc0, tc1, cp0, cp1, hp0, hp1, h0, h1,
    hi_ref, lo_ref, s0, s1, m0, m1,
):
    bands, unused, dmodel = x.shape
    pack = Pack(rnn, dmodel, h0.shape[2])

    def fetch(b, carry):
        x[b] = arrived[slot_of[0, b]]
        return carry

    lax.fori_loop(0, bands, fetch, 0)
    act = (act0, act1)

    def x_flat(start, size):
        return x[...].reshape(bands * 16, dmodel)

    gates_forward(x_flat, act, pack, vec, bands * 16, bands * 16)
    run_forward(
        bands, band_places(bands), act, (tc0, tc1), (cp0, cp1), (hp0, hp1), (h0, h1),
        pack, hi_ref, lo_ref, (s0, s1), (m0, m1),
    )
    total = output_forward(bands, (h0, h1), pack, vec)
    whole = (x[...].reshape(bands * 16, dmodel) + total).reshape(bands, 16, dmodel)
    out[...] = jnp.zeros_like(out)
    for b in range(bands):
        out[slot_of[0, b]] = whole[b]


def band_forward(slot_of, arrived, rnn, vec, hidden):
    bands = slot_of.shape[1]
    dmodel = arrived.shape[2]
    return pl.pallas_call(
        band_forward_kernel,
        out_shape=[f32(arrived.shape), f32((bands, 16, dmodel))] + saved_shapes(bands, hidden),
        in_specs=[SMEM] + [VMEM] * 3,
        out_specs=[VMEM] * 12,
        scratch_shapes=rec_scratch(16, hidden),
        compiler_params=PARAMS,
        cost_estimate=cost(28),
        name="band_forward",
    )(slot_of, arrived, rnn, vec)


def band_backward_kernel(
    slot_of, arrived, x, act0, act1, tc0, tc1, cp0, cp1, hp0, hp1, h0, h1, rnn, vec,
    out, g_rnn,
    hi_ref, lo_ref, s0, s1, m0, m1, dy, g_vec, dh0, dh1, dz0, dz1,
):
    bands, unused, dmodel = x.shape
    pack, g_pack = Pack(rnn, dmodel, h0.shape[2]), Pack(g_rnn, dmodel, h0.shape[2])

    def fetch(b, carry):
        dy[b] = arrived[slot_of[0, b]]
        return carry

    lax.fori_loop(0, bands, fetch, 0)
    states_backward(bands, dy[...].reshape(bands * 16, dmodel), (dh0, dh1), (h0, h1), pack, g_pack)
    run_backward(
        bands, band_places(bands), (act0, act1), (dz0, dz1), (tc0, tc1), (cp0, cp1), (dh0, dh1),
        pack, hi_ref, lo_ref, (s0, s1), (m0, m1),
    )
    dx = gates_backward(
        bands, x[...].reshape(bands * 16, dmodel), dy[...].reshape(bands * 16, dmodel),
        (dz0, dz1), (hp0, hp1), pack, vec, g_pack, g_vec,
    ).reshape(bands, 16, dmodel)
    out[...] = jnp.zeros_like(out)
    for b in range(bands):
        out[slot_of[0, b]] = dx[b]


def band_backward(slot_of, arrived, saved, rnn, vec, hidden):
    bands = slot_of.shape[1]
    dmodel = arrived.shape[2]
    return pl.pallas_call(
        band_backward_kernel,
        out_shape=[f32(arrived.shape), f32(rnn.shape)],
        in_specs=[SMEM] + [VMEM] * (2 + 10 + 2),
        out_specs=[VMEM] * 2,
        scratch_shapes=rec_scratch(16, hidden)
        + [pltpu.VMEM((bands, 16, dmodel), jnp.float32), pltpu.VMEM(vec.shape, jnp.float32)]
        + [pltpu.VMEM((bands, 16, hidden), jnp.float32)] * 2
        + [pltpu.VMEM((bands, 16, 4 * hidden), jnp.float32)] * 2,
        compiler_params=PARAMS,
        cost_estimate=cost(43),
        name="band_backward",
    )(slot_of, arrived, *saved, rnn, vec)


def in_turn(core, mine, other):
    return [jnp.where(core == 0, mine, other), jnp.where(core == 0, other, mine)]


def mask_kernel(
    places, arrived, cot, wide_mine, wide_other, mask_mine, mask_other, vec,
    masks, grad, g_wide_keep, g_wide_send, g_mask_keep, g_mask_send, g_vec,
):
    s = pl.program_id(0)
    parts, streams, unused, quarter, dmodel = arrived.shape
    outer, unused, frames, wide = cot.shape
    half = wide // 2
    core = places[1, 0]
    x = jnp.concatenate([arrived[q, g, 0] for g in range(streams) for q in range(parts)], axis=0)
    w_wide, w_mask = [], []
    for g in range(outer):
        w_wide += in_turn(core, wide_mine[g, 0], wide_other[g, 0])
        w_mask += in_turn(core, mask_mine[g, 0], mask_other[g, 0])
    w_wide, w_mask = jnp.concatenate(w_wide, axis=1), jnp.concatenate(w_mask, axis=0)
    mlp = w_mask.shape[0]
    piece = mlp // (2 * outer)
    v = vec[0]
    gain = 1.0 + v[:, :dmodel]
    unit, scale = norm_stats(x)
    p = split(unit * gain + v[:, dmodel : 2 * dmodel])
    wide_parts = split(w_wide)
    mask_parts = split(w_mask)
    q = jnp.tanh(dot_parts(p, wide_parts, AB) + v[:, 2 * dmodel : 2 * dmodel + mlp])
    q_parts = split(q)
    r = dot_parts(q_parts, mask_parts, AB) + v[:, 2 * dmodel + mlp :]
    lane = lax.broadcasted_iota(jnp.int32, (1, half), 1)
    inside = (lane < places[0, s]).astype(jnp.float32)
    valid = jnp.concatenate([inside, inside], axis=1)
    value = r[:, :wide]
    gate = sigmoid(r[:, wide:])
    masks[...] = (value * gate * valid).reshape(masks.shape)
    dm = cot[...].reshape(outer * frames, wide) * valid
    dr = jnp.concatenate([dm * gate, dm * value * gate * (1.0 - gate)], axis=1)
    dr_parts = split(dr)
    g_mask = dot_parts(q_parts, dr_parts, ATB)
    dq = dot_parts(dr_parts, mask_parts, ABT)
    da = dq * (1.0 - q * q)
    da_parts = split(da)
    g_wide = dot_parts(p, da_parts, ATB)
    for g in range(outer):
        first, second = slice(2 * g * piece, (2 * g + 1) * piece), slice((2 * g + 1) * piece, (2 * g + 2) * piece)
        g_mask_keep[g, 0], g_mask_send[g, 0] = in_turn(core, g_mask[first], g_mask[second])
        g_wide_keep[g, 0], g_wide_send[g, 0] = in_turn(core, g_wide[:, first], g_wide[:, second])
    dp = dot_parts(da_parts, wide_parts, ABT)
    g_vec[0, :, :dmodel] = column_sum(dp * unit)
    g_vec[0, :, dmodel : 2 * dmodel] = column_sum(dp)
    g_vec[0, :, 2 * dmodel : 2 * dmodel + mlp] = column_sum(da)
    g_vec[0, :, 2 * dmodel + mlp :] = column_sum(dr)
    dx = norm_back(dp * gain, unit, scale)
    k = 0
    for g in range(streams):
        for q_ in range(parts):
            grad[q_, g, 0] = dx[k * quarter : (k + 1) * quarter]
            k += 1


def mask_network(places, arrived, cot, w_wide, w_mask, vec):
    parts, streams, slots, quarter, dmodel = arrived.shape

    def second(shape):
        return pl.BlockSpec(
            (shape[0], 1) + shape[2:], lambda s: (0, s) + (0,) * (len(shape) - 2)
        )

    moving = pl.BlockSpec((parts, streams, 1, quarter, dmodel), lambda s: (0, 0, s, 0, 0))
    vector = pl.BlockSpec((1,) + vec.shape[1:], lambda s: (s, 0, 0))
    pieces = [w_wide[0].shape] * 2 + [w_mask[0].shape] * 2
    return pl.pallas_call(
        mask_kernel,
        grid=(slots,),
        out_shape=[f32(cot.shape), f32(arrived.shape)] + [f32(p) for p in pieces] + [f32(vec.shape)],
        in_specs=[SMEM, moving, second(cot.shape)] + [second(p) for p in pieces] + [vector],
        out_specs=[second(cot.shape), moving] + [second(p) for p in pieces] + [vector],
        compiler_params=PARAMS,
        cost_estimate=cost(12),
        name="mask_network",
    )(places, arrived, cot, *w_wide, *w_mask, vec)


class Links:
    def __init__(self, bands, layers, send_sems, recv_sems):
        self.bands, self.layers = bands, layers
        self.band, self.stream = lax.axis_index("band"), lax.axis_index("stream")
        self.layer, self.core = lax.div(self.stream, CORES), lax.rem(self.stream, CORES)
        self.other = self.stream + 1 - 2 * self.core
        self.send_sems, self.recv_sems = send_sems, recv_sems
        self.started = []

    def band_to(self, m):
        return lax.rem(self.band + m, self.bands)

    def band_from(self, m):
        return lax.rem(self.band + self.bands - m, self.bands)

    def layer_to(self, k):
        return lax.rem(self.layer + k, self.layers)

    def layer_from(self, k):
        return lax.rem(self.layer + self.layers - k, self.layers)

    def own(self, layer):
        return layer * CORES + self.core

    def across(self, layer):
        return layer * CORES + 1 - self.core

    def greet(self, partners):
        barrier = pltpu.get_barrier_semaphore()
        for partner in partners:
            pl.semaphore_signal(barrier, inc=1, device_id=partner, device_id_type=MESH)
        pl.semaphore_wait(barrier, len(partners))

    def copy(self, source, target, index, partner):
        return pltpu.make_async_remote_copy(
            src_ref=source, dst_ref=target, send_sem=self.send_sems.at[index],
            recv_sem=self.recv_sems.at[index], device_id=partner, device_id_type=MESH,
        )

    def send(self, source, target, index, partner):
        copy = self.copy(source, target, index, partner)
        copy.start()
        self.started.append(copy)

    def arrive(self, target, index):
        self.copy(target, target, index, (self.band, self.other)).wait_recv()

    def finish(self):
        for copy in self.started:
            copy.wait_send()


def gather_kernel(bands, layers, rnn, own_split, rnn_all, split_all, send_sems, recv_sems, local_sems):
    at = Links(bands, layers, send_sems, recv_sems)
    band, stream, other = at.band, at.stream, at.other
    quarter = rnn.shape[0] // bands
    at.greet(
        [(at.band_to(m), stream) for m in range(1, bands)]
        + [(band, at.own(at.layer_to(k))) for k in range(1, layers)]
        + [(band, other)]
    )
    steps = range(1, layers)
    turns = range(1, bands)

    def rows(b):
        return pl.ds(b * quarter, quarter)

    to_layer, to_layer_split, to_band = 0, layers, 2 * layers
    to_core = to_band + layers * bands
    to_core_split = to_core + layers * bands
    for k in steps:
        at.send(rnn.at[rows(band)], rnn_all.at[stream, rows(band)], to_layer + k, (band, at.own(at.layer_to(k))))
    for k in steps:
        at.send(own_split, split_all.at[stream], to_layer_split + k, (band, at.own(at.layer_to(k))))
    at.send(rnn, rnn_all.at[stream], to_core, (band, other))
    at.send(own_split, split_all.at[stream], to_core_split, (band, other))
    local = [
        pltpu.make_async_copy(rnn, rnn_all.at[stream], local_sems.at[0]),
        pltpu.make_async_copy(own_split, split_all.at[stream], local_sems.at[1]),
    ]
    for copy in local:
        copy.start()
    for k in steps:
        source = at.own(at.layer_from(k))
        piece = rnn_all.at[source, rows(band)]
        at.arrive(piece, to_layer + k)
        for m in turns:
            at.send(piece, piece, to_band + k * bands + m, (at.band_to(m), stream))
        at.send(piece, piece, to_core + k * bands, (band, other))
    for k in steps:
        source = at.own(at.layer_from(k))
        for m in turns:
            piece = rnn_all.at[source, rows(at.band_from(m))]
            at.arrive(piece, to_band + k * bands + m)
            at.send(piece, piece, to_core + k * bands + m, (band, other))
    for k in steps:
        piece = split_all.at[at.own(at.layer_from(k))]
        at.arrive(piece, to_layer_split + k)
        at.send(piece, piece, to_core_split + k, (band, other))
    at.arrive(rnn_all.at[other], to_core)
    at.arrive(split_all.at[other], to_core_split)
    for k in steps:
        source = at.across(at.layer_from(k))
        for m in range(bands):
            at.arrive(rnn_all.at[source, rows(at.band_from(m))], to_core + k * bands + m)
        at.arrive(split_all.at[source], to_core_split + k)
    at.finish()
    for copy in local:
        copy.wait()


def gather_front(rnn, own_split, bands, layers):
    count = 2 * layers + 2 * layers * bands + layers
    return pl.pallas_call(
        partial(gather_kernel, bands, layers),
        out_shape=[f32((layers * CORES,) + rnn.shape), f32((layers * CORES,) + own_split.shape)],
        in_specs=[ANY] * 2,
        out_specs=[ANY] * 2,
        scratch_shapes=[
            pltpu.SemaphoreType.DMA((count,)), pltpu.SemaphoreType.DMA((count,)), pltpu.SemaphoreType.DMA((2,)),
        ],
        compiler_params=pltpu.CompilerParams(collective_id=0, has_side_effects=True),
        cost_estimate=cost(30),
        name="gather_front",
    )(rnn, own_split)


def exchange_kernel(bands, layers, source, target, send_sems, recv_sems, local_sem):
    at = Links(bands, layers, send_sems, recv_sems)
    wide = source.shape[1] == layers
    turns = [(m, k) for k in range(layers if wide else 1) for m in range(bands) if m + k]

    def place(ref, band, layer):
        return ref.at[band, layer] if wide else ref.at[band]

    def stream_of(layer):
        return at.own(layer) if wide else at.stream

    at.greet([(at.band_to(m), stream_of(at.layer_to(k))) for m, k in turns])
    for m, k in turns:
        band, layer = at.band_to(m), at.layer_to(k)
        at.send(
            place(source, band, layer), place(target, at.band, at.layer), k * bands + m, (band, stream_of(layer))
        )
    local = pltpu.make_async_copy(
        place(source, at.band, at.layer), place(target, at.band, at.layer), local_sem
    )
    local.start()
    for m, k in turns:
        at.arrive(place(target, at.band_from(m), at.layer_from(k)), k * bands + m)
    at.finish()
    local.wait()


def exchange(x, bands, layers, number):
    count = bands * layers
    return pl.pallas_call(
        partial(exchange_kernel, bands, layers),
        out_shape=f32(x.shape),
        in_specs=[ANY],
        out_specs=ANY,
        scratch_shapes=[
            pltpu.SemaphoreType.DMA((count,)), pltpu.SemaphoreType.DMA((count,)), pltpu.SemaphoreType.DMA,
        ],
        compiler_params=pltpu.CompilerParams(collective_id=number, has_side_effects=True),
        cost_estimate=cost(8),
        name="exchange",
    )(x)


def reduce_kernel(
    bands, layers, g_rnn, g_split, rnn_out, split_out,
    from_core, from_core_split, from_band, held, from_layer, from_layer_split, send_sems, recv_sems,
):
    at = Links(bands, layers, send_sems, recv_sems)
    band, stream, other = at.band, at.stream, at.other
    quarter = g_rnn.shape[1] // bands
    at.greet(
        [(at.band_to(m), stream) for m in range(1, bands)]
        + [(band, at.own(at.layer_to(k))) for k in range(1, layers)]
        + [(band, other)]
    )
    order = list(range(1, layers)) + [0]
    turns = range(1, bands)

    def rows(b):
        return pl.ds(pl.multiple_of(b * quarter, 8), quarter)

    to_core, to_core_split, to_layer, to_layer_split = 0, layers, 2 * layers, 3 * layers
    to_band = 4 * layers
    to_all = to_band + bands * layers
    for k in order:
        at.send(g_rnn.at[at.across(at.layer_to(k))], from_core.at[k], to_core + k, (band, other))
    for k in order:
        at.send(g_split.at[at.across(at.layer_to(k))], from_core_split.at[k], to_core_split + k, (band, other))
    for k in order:
        at.arrive(from_core.at[k], to_core + k)
        from_core[k] += g_rnn[at.own(at.layer_to(k))]
        for m in turns:
            to = at.band_to(m)
            at.send(
                from_core.at[k, rows(to)], from_band.at[m - 1, k], to_band + m * layers + k, (to, stream)
            )
    for k in order:
        at.arrive(from_core_split.at[k], to_core_split + k)
        from_core_split[k] += g_split[at.own(at.layer_to(k))]
        if k:
            at.send(
                from_core_split.at[k], from_layer_split.at[k - 1], to_layer_split + k,
                (band, at.own(at.layer_to(k))),
            )
    for k in order:
        total = from_core[k, rows(band)]
        for m in turns:
            at.arrive(from_band.at[m - 1, k], to_band + m * layers + k)
            total = total + from_band[m - 1, k]
        held[k] = total
        if k:
            at.send(held.at[k], from_layer.at[k - 1], to_layer + k, (band, at.own(at.layer_to(k))))
    total = held[0]
    for k in range(1, layers):
        at.arrive(from_layer.at[k - 1], to_layer + k)
        total = total + from_layer[k - 1]
    rnn_out[rows(band)] = total
    for m in turns:
        at.send(rnn_out.at[rows(band)], rnn_out.at[rows(band)], to_all + m, (at.band_to(m), stream))
    total = from_core_split[0]
    for k in range(1, layers):
        at.arrive(from_layer_split.at[k - 1], to_layer_split + k)
        total = total + from_layer_split[k - 1]
    split_out[...] = total
    for m in turns:
        at.arrive(rnn_out.at[rows(at.band_from(m))], to_all + m)
    at.finish()


def reduce_back(g_rnn, g_split, bands, layers):
    rows, split_rows_count = g_rnn.shape[1], g_split.shape[1]
    quarter = rows // bands
    count = 4 * layers + bands * layers + bands
    return pl.pallas_call(
        partial(reduce_kernel, bands, layers),
        out_shape=[f32((rows, LANES)), f32((split_rows_count, LANES))],
        in_specs=[VMEM] * 2,
        out_specs=[VMEM] * 2,
        scratch_shapes=[
            pltpu.VMEM((layers, rows, LANES), jnp.float32),
            pltpu.VMEM((layers, split_rows_count, LANES), jnp.float32),
            pltpu.VMEM((bands - 1, layers, quarter, LANES), jnp.float32),
            pltpu.VMEM((layers, quarter, LANES), jnp.float32),
            pltpu.VMEM((layers - 1, quarter, LANES), jnp.float32),
            pltpu.VMEM((layers - 1, split_rows_count, LANES), jnp.float32),
            pltpu.SemaphoreType.DMA((count,)),
            pltpu.SemaphoreType.DMA((count,)),
        ],
        compiler_params=pltpu.CompilerParams(
            collective_id=5, has_side_effects=True, vmem_limit_bytes=VMEM_BYTES
        ),
        cost_estimate=cost(40),
        name="reduce_back",
    )(g_rnn, g_split)


def groups_of(size, slots):
    outer = math.gcd(size, slots)
    inner = size // outer
    across = [[g * inner + i for g in range(outer)] for i in range(inner)]
    within = [[g * inner + i for i in range(inner)] for g in range(outer)]
    return outer, inner, across, within


def sum_everywhere(values, sizes):
    n = sizes[0] * sizes[1]
    row = jnp.zeros((8, LANES), jnp.float32).at[0, : values.shape[0]].set(values)
    spread = jnp.broadcast_to(row[None], (n, 8, LANES))
    got = lax.all_to_all(spread, ("band", "stream"), 0, 0, tiled=True)
    return jnp.sum(got, axis=0)[0, : values.shape[0]]


def swap_cores(x):
    return lax.ppermute(x, "stream", [(s, s ^ 1) for s in range(lax.axis_size("stream"))])


def share_slots(shard, outer, across, within, axis):
    slots = shard.shape[0]
    mine = lax.all_to_all(
        shard.reshape((outer, slots // outer) + shard.shape[1:]), "stream", 0, 0,
        axis_index_groups=across, tiled=True,
    )
    inner = len(within[0])
    if inner == CORES:
        return mine, swap_cores(mine)
    both = lax.all_gather(mine, "stream", axis_index_groups=within)
    both = both.reshape((CORES, inner // CORES) + mine.shape)
    if axis == 1:
        both = both.transpose(0, 2, 3, 1, 4, 5)
        both = both.reshape(both.shape[:3] + (-1, both.shape[5]))
    else:
        both = both.transpose(0, 2, 3, 4, 1, 5)
        both = both.reshape(both.shape[:4] + (-1,))
    return both[0], both[1]


def return_slots(keep, send, outer, inner, across, within, axis):
    if inner == CORES:
        mine = keep + swap_cores(send)
    else:
        both = jnp.stack([keep, send])
        half = inner // CORES
        if axis == 1:
            both = both.reshape(both.shape[:3] + (half, -1, both.shape[4])).transpose(0, 3, 1, 2, 4, 5)
        else:
            both = both.reshape(both.shape[:4] + (half, -1)).transpose(0, 4, 1, 2, 3, 5)
        both = both.reshape((inner,) + both.shape[2:])
        mine = lax.psum_scatter(both, "stream", axis_index_groups=within, tiled=False)
    back = lax.all_to_all(mine, "stream", 0, 0, axis_index_groups=across, tiled=True)
    return back.reshape((-1,) + back.shape[2:])


def lamb_moments(gradient, mean_old, power_old, factor):
    clipped = gradient * factor
    mean_new = BETA_ONE * mean_old + (1.0 - BETA_ONE) * clipped
    power_new = BETA_TWO * power_old + (1.0 - BETA_TWO) * clipped * clipped
    return (mean_new, power_new)


def lamb_direction(weight_matrix, mean_new, power_new, decay):
    corrected = mean_new / (1.0 - BETA_ONE**STEP)
    scale_root = jnp.sqrt(power_new / (1.0 - BETA_TWO**STEP)) + ADAM_EPS
    return corrected / scale_root + decay * weight_matrix


def pack_split(splitter, banding, blocks):
    slots, wide, dmodel = splitter.shape
    columns = banding.shape[1] // blocks
    rows = -(-slots * columns // (8 * LANES)) * 8
    body_rows = splitter.reshape(slots, blocks, wide // blocks, dmodel).transpose(1, 0, 2, 3)
    flat = banding.reshape(slots, blocks, columns).transpose(1, 0, 2).reshape(blocks, slots * columns)
    flat = jnp.pad(flat, ((0, 0), (0, rows * LANES - slots * columns))).reshape(blocks, rows, LANES)
    return jnp.concatenate([body_rows.reshape(blocks, slots * wide // blocks, dmodel), flat], axis=1)


def unpack_banding(pack, start, slots, columns):
    blocks = pack.shape[0]
    flat = pack[:, start:].reshape(blocks, -1)[:, : slots * columns]
    return flat.reshape(blocks, slots, columns).transpose(1, 0, 2).reshape(slots, blocks * columns)


def body(spectrum, segments, widths, groups, cotangent, *state):
    weights, means_old, powers_old = state[:8], state[8:16], state[16:]
    splitter, widener, masker, banding, intake, recurrence, outtake, scalers = weights
    group_count = lax.axis_size("band")
    stream_count = lax.axis_size("stream")
    my_group = lax.axis_index("band")
    my_stream = lax.axis_index("stream")
    slots = splitter.shape[0]
    frames = spectrum.shape[0]
    quarter = frames // group_count
    outer, inner, across, within = groups_of(stream_count, slots)
    share = slots // outer
    my_outer = my_stream // inner
    dmodel = splitter.shape[2]
    hidden = recurrence.shape[2]
    wide = splitter.shape[1] * stream_count
    bins = spectrum.shape[2]
    blocks, out_rows, weight_rows, vec_share, vec_rows, rows = pack_rows(dmodel, hidden)
    slot_rows = wide // blocks
    columns = banding.shape[1] * stream_count // blocks
    direct = stream_count == blocks and inner == CORES

    members = (groups[:, None] == jnp.arange(group_count, dtype=jnp.int32)[None, :]).astype(jnp.int32)
    ranking = jnp.sum(jnp.cumsum(members, axis=0) * members, axis=1) - 1
    band_slot_index = groups * slots + ranking
    local_slots = my_group * slots + jnp.arange(slots, dtype=jnp.int32)
    owned = (band_slot_index[None, :] == local_slots[:, None]).astype(jnp.int32)
    edges = jnp.cumsum(widths) - widths
    slot_edges = jnp.sum(owned * edges[None, :], axis=1)
    slot_widths = jnp.sum(owned * widths[None, :], axis=1)
    slot_places = jnp.stack([slot_edges, slot_widths])
    slot_of = band_slot_index[None, :]
    lengths = jnp.sum(
        (segments[0][None, :] == jnp.arange(CLIPS, dtype=jnp.int32)[:, None]).astype(jnp.int32), axis=1
    )
    clips = jnp.stack([jnp.cumsum(lengths) - lengths, lengths])
    share_widths = lax.dynamic_slice(slot_widths, (my_outer * share,), (share,))
    core = (my_stream % CORES).astype(jnp.int32)
    mask_places = jnp.stack([share_widths, jnp.broadcast_to(core if direct else 0, (share,))]).astype(jnp.int32)

    padded = ((bins - 1) // LANES + 2) * LANES
    spec = jnp.pad(
        spectrum.transpose(1, 0, 2).reshape(2 * frames, bins), ((0, 0), (0, padded - bins))
    )
    cot_parts = cotangent.reshape(frames, outer, share, wide).transpose(1, 2, 0, 3)

    if direct:
        packs = [
            pack_rnn(intake[k], recurrence[k], outtake[k], scalers[k : k + 1], rows, vec_share)[0]
            for k in range(2)
        ]
        rnn0, w_split = gather_front(packs[0], pack_split(splitter, banding, 1)[0], group_count, outer)
        later, w_wide, w_mask, cot_parts, rnn0 = lax.optimization_barrier(
            (packs[1], widener, masker, cot_parts, rnn0)
        )
        rnn1 = lax.all_gather(later, "stream")
    else:
        whole = (
            lax.all_gather(intake, "stream", axis=3, tiled=True),
            lax.all_gather(recurrence, "stream", axis=3, tiled=True),
            lax.all_gather(outtake, "stream", axis=1, tiled=True),
            lax.all_gather(scalers, "stream", axis=1, tiled=True),
        )
        rnn0, rnn1 = (
            pack_rnn(whole[0][k], whole[1][k], whole[2][k], whole[3][k : k + 1], rows, vec_share)
            for k in range(2)
        )
        w_split = pack_split(
            lax.all_gather(splitter, "stream", axis=1, tiled=True),
            lax.all_gather(banding, "stream", axis=1, tiled=True),
            blocks,
        )
        w_wide, w_mask = widener, masker
    vec0, vec1 = (unpack_vec(p, weight_rows, vec_rows, vec_share) for p in (rnn0, rnn1))
    v_band = unpack_banding(w_split, slots * slot_rows, slots, columns)[:, None, :]

    w_mask = share_slots(w_mask, outer, across, within, 1)
    w_wide = share_slots(w_wide, outer, across, within, 2)
    cot = lax.all_to_all(cot_parts, "stream", 0, 0, axis_index_groups=across, tiled=True)

    def by_band(x, number):
        if direct:
            return exchange(x, group_count, outer, number)
        return lax.all_to_all(x, "band", 0, 0, tiled=True)

    def to_masks(x):
        x = x.reshape(group_count, outer, share, quarter, dmodel)
        if direct:
            return exchange(x, group_count, outer, 2)
        x = lax.all_to_all(x, "stream", 1, 1, axis_index_groups=across, tiled=True)
        return lax.all_to_all(x, "band", 0, 0, tiled=True)

    def from_masks(x):
        if direct:
            x = exchange(x, group_count, outer, 3)
        else:
            x = lax.all_to_all(x, "band", 0, 0, tiled=True)
            x = lax.all_to_all(x, "stream", 1, 1, axis_index_groups=across, tiled=True)
        return x.reshape(group_count * slots, quarter, dmodel)

    base = 2 * wide + dmodel
    got = time_forward(
        slot_places, clips, spec, w_split, v_band, rnn0, vec0, group_count, slot_rows, hidden
    )
    time_out, time_saved = got[0], got[1:]
    arrived = by_band(time_out, 1)
    got = band_forward(
        slot_of, arrived.reshape(group_count * slots, quarter, dmodel), rnn1, vec1, hidden
    )
    band_out, band_saved = got[0], got[1:]
    share_vec = lax.dynamic_slice_in_dim(v_band[:, :, base:], my_outer * share, share, 0)
    (
        mask_parts, grad_mixed, g_wide_keep, g_wide_send, g_mask_keep, g_mask_send, g_mask_vec,
    ) = mask_network(mask_places, to_masks(band_out), cot, w_wide, w_mask, share_vec)
    mask_reduced = return_slots(g_mask_keep, g_mask_send, outer, inner, across, within, 1)
    widened_reduced = return_slots(g_wide_keep, g_wide_send, outer, inner, across, within, 2)
    mask_parts = lax.all_to_all(mask_parts, "stream", 0, 0, axis_index_groups=across, tiled=True)
    band_grad, g_rnn1 = band_backward(slot_of, from_masks(grad_mixed), band_saved, rnn1, vec1, hidden)
    grad_time = by_band(band_grad.reshape(group_count, slots, quarter, dmodel), 4)
    if direct:
        g_rnn1 = lax.psum(lax.psum_scatter(g_rnn1, "stream", scatter_dimension=0, tiled=True), "band")
    d_spec, g_split, g_split_vec, g_rnn0 = time_backward(
        slot_places, clips, grad_time, spec, time_saved, w_split, v_band, rnn0, vec0, slot_rows, hidden
    )

    masks = mask_parts.reshape(slots, frames, wide).transpose(1, 0, 2).reshape(cotangent.shape)
    d_spec = lax.psum(d_spec, "band")
    spectrum_grad = d_spec.reshape(2, frames, padded)[:, :, :bins].transpose(1, 0, 2)

    g_mask_vec = lax.dynamic_update_slice_in_dim(
        jnp.zeros((slots, g_mask_vec.shape[2]), jnp.float32), g_mask_vec[:, 0], my_outer * share, 0
    )
    g_band = jnp.concatenate([g_split_vec[:, 0], g_mask_vec], axis=1)
    if direct:
        tail_rows = g_split.shape[1] - slots * slot_rows
        flat = g_band.reshape(slots, blocks, columns).transpose(1, 0, 2).reshape(blocks, slots * columns)
        flat = jnp.pad(flat, ((0, 0), (0, tail_rows * LANES - slots * columns)))
        g_split = lax.dynamic_update_slice_in_dim(
            g_split, flat.reshape(blocks, tail_rows, LANES), slots * slot_rows, 1
        )
        g_rnn0, g_split = reduce_back(g_rnn0, g_split, group_count, outer)
        first = unpack_rnn(g_rnn0[None], dmodel, hidden)
        second = unpack_rnn(g_rnn1, dmodel, hidden)
        rnn_grads = [jnp.stack([a, b]) for a, b in zip(first[:3], second[:3])]
        rnn_grads.append(jnp.concatenate([first[3], second[3]], axis=0))
        split_reduced = g_split[: slots * slot_rows].reshape(splitter.shape)
        band_reduced = unpack_banding(g_split[None], slots * slot_rows, slots, columns)
    else:
        first, second = unpack_rnn(g_rnn0, dmodel, hidden), unpack_rnn(g_rnn1, dmodel, hidden)
        rnn_grads = [jnp.stack([a, b]) for a, b in zip(first[:3], second[:3])]
        rnn_grads.append(jnp.concatenate([first[3], second[3]], axis=0))
        rnn_grads = [
            lax.psum(lax.psum_scatter(g, "stream", scatter_dimension=d, tiled=True), "band")
            for g, d in zip(rnn_grads, (3, 3, 1, 1))
        ]
        g_split = g_split[:, : slots * slot_rows].reshape(blocks, slots, slot_rows, dmodel)
        g_split = g_split.transpose(1, 0, 2, 3).reshape(slots, wide, dmodel)
        split_reduced = lax.psum_scatter(g_split, "stream", scatter_dimension=1, tiled=True)
        band_reduced = lax.psum_scatter(g_band, "stream", scatter_dimension=1, tiled=True)
    reduced = (split_reduced, widened_reduced, mask_reduced, band_reduced) + tuple(rnn_grads)

    shares = (1.0,) * 4 + (1.0 / group_count,) * 4
    decays = (DECAY_RATE,) * 3 + (0.0,) + (DECAY_RATE,) * 3 + (0.0,)
    sizes = (group_count, stream_count)
    sums = [sum(jnp.sum(g * g) * part for g, part in zip(reduced, shares))]
    sums += [jnp.sum(w * w) * part for w, part in zip(weights, shares)]
    totals = sum_everywhere(jnp.stack(sums), sizes)
    grad_norm = jnp.sqrt(totals[0])
    factor = jnp.minimum(1.0, CLIP_NORM / grad_norm)
    moments = [lamb_moments(g, m, p, factor) for g, m, p in zip(reduced, means_old, powers_old)]
    directions = [lamb_direction(w, m, p, d) for w, (m, p), d in zip(weights, moments, decays)]
    update_totals = sum_everywhere(
        jnp.stack([jnp.sum(d * d) * part for d, part in zip(directions, shares)]), sizes
    )
    ratios = jnp.sqrt(totals[1:]) / jnp.sqrt(update_totals + 1e-12)
    fresh = [w - LEARN_RATE * ratios[k] * d for k, (w, d) in enumerate(zip(weights, directions))]
    return (
        (masks, spectrum_grad, grad_norm)
        + tuple(fresh)
        + tuple(m for m, unused in moments)
        + tuple(p for unused, p in moments)
    )


def solution(mesh):
    stored = (
        P("band", "stream", None),
        P("band", None, "stream"),
        P("band", "stream", None),
        P("band", "stream"),
        P(None, None, None, "stream"),
        P(None, None, None, "stream"),
        P(None, "stream", None),
        P(None, "stream"),
    )
    frames_over = P("stream", None, None)
    mask_over = P("stream", "band", None, None)
    return jax.shard_map(
        body,
        mesh=mesh,
        in_specs=(frames_over, P("stream", None), P(), P(), mask_over) + stored * 3,
        out_specs=(mask_over, frames_over, P()) + stored * 3,
        check_vma=False,
    )
```

time: 836 us -> 520 us (0.62)
  waiting for transfers between devices: 289 us -> 34 us
  blocking collectives: 166 us -> 0 us
  Pallas kernels: 168 us -> 303 us
  local copies, waits for them, and re-layouts: 56.4 us -> 44.9 us
  starting transfers between devices: 46 us -> 37.5 us
    reduce_scatter x4 -> x1, waiting for transfers between devices: 134 us -> 0.01 us  [body(): lax.psum_scatter(g_rnn1, 'stream', scatter_dimension=0, tiled=True)]
    pallas_call x3 -> x9, Pallas kernels: 129 us -> 263 us  [the longest x1 52.5 us: time_backward(): pl.pallas_call(partial(time_backward_kernel, slot_rows), out_shape=[f32(s...]
    all_gather x3 -> x0, blocking collectives: 114 us -> none  [the longest x1 72.6 us: body(): w_out = lax.all_gather(outtake, 'stream', axis=1, tiled=True)]
    psum x1, waiting for transfers between devices: 57.7 us -> 0.02 us  [body(): d_spec = lax.psum(d_spec, 'band')]
    unnamed x12 -> x3, waiting for transfers between devices: 50.4 us -> 0.05 us
    all_to_all x3 -> x0, blocking collectives: 42.8 us -> none  [the longest x1 21.4 us: body(): lax.all_to_all(band_grad.reshape(group_count, slots, quarter, dmodel), 'b...]
    all_to_all x3 -> x0, waiting for transfers between devices: 13.6 us -> none  [the longest x1 7.84 us: to_masks(): x = lax.all_to_all(x, 'stream', 1, 1, axis_index_groups=across, tiled=True)]
    all_to_all x2, waiting for transfers between devices: 0.01 us -> 13.4 us  [share_slots(): lax.all_to_all(shard.reshape((outer, slots // outer) + shard.shape[1:]),...]
  transfers between devices with their start and end apart: 25 -> 15, of which waited for: 14 -> 4; matrix products, arithmetic and copies ran while one was open for 9% -> 10% of each run, Pallas kernels for 8% -> 47%
where the time goes in v2:
time: 520 us; the launch traced here: 512 us
  Pallas kernels  303 us (58%)
  other arithmetic  60.5 us (12%)
  local copies, waits for them, and re-layouts  44.9 us (9%)
  starting transfers between devices  37.5 us (7%)
  waiting for transfers between devices  34 us (7%)
  between operations  32.7 us (6%)
    pallas_call x1, Pallas kernels, time_backward(): pl.pallas_call(partial(time_backward_kernel, slot_rows), out_shape=[f32(s...  52.5 us
    pallas_call x1, Pallas kernels, reduce_back(): pl.pallas_call(partial(reduce_kernel, bands, layers), out_shape=[f32((row...  52.2 us
    pallas_call x1, Pallas kernels, band_backward(): pl.pallas_call(band_backward_kernel, out_shape=[f32(arrived.shape), f32(r...  44.8 us
    pallas_call x4, Pallas kernels, exchange(): pl.pallas_call(partial(exchange_kernel, bands, layers), out_shape=f32(x.s...  44.2 us
    pallas_call x1, Pallas kernels, time_forward(): pl.pallas_call(partial(time_forward_kernel, slot_rows), out_shape=[f32((p...  35.3 us
    pallas_call x1, Pallas kernels, gather_front(): pl.pallas_call(partial(gather_kernel, bands, layers), out_shape=[f32((lay...  33.8 us
    pallas_call x1, Pallas kernels, band_forward(): pl.pallas_call(band_forward_kernel, out_shape=[f32(arrived.shape), f32((b...  28.3 us
    reduce_sum x8, other arithmetic, body(): jnp.sum(d * d) * part  19.6 us
  transfers between devices with their start and end apart: 15, of which 4 were waited for; matrix products, arithmetic and copies ran while one was open for 10% of the time, Pallas kernels for 47%

profile of v2, /device:TPU:0, one launch (start us, length us, event | category | flops | bytes accessed | tf_op | source)
XLA Modules:
  0.0 512.4 jit_solution(12591738961017860354)
XLA Ops:
  7.3 1.1 fusion.23
  8.4 1.0 fusion.24
  10.0 1.5 reshape.318
  12.2 1.0 maximum_bitcast_fusion
  13.2 33.8 %gather_front.1 = (f32[8,864,128]{2,1,0:T(8,128)}, f32[8,408,128]{2,1,0:T(8,128)}) custom-call(f32[864,128]{1,0:T(8,128)} %get-tuple-element.269.rnn, f32[408,128]{1,0:T(8,128)} %maximum_bitcast_fusion.2.own_split), custom_call_target="tpu_custom_call" | custom-call | flops 32999999488 | bytes 90000000 | tf_op jit(solution)/shard_map/gather_front/pallas_call | solution.py:823
  47.1 6.2 %all-to-all-start.1 = ((f32[4,3,128,64]{2,3,1,0:T(8,128)}), f32[4,3,128,64]{2,3,1,0:T(8,128)S(1)}, u32[]{:S(2)}, u32[]{:S(2)}) async-start(f32[4,3,128,64]{2,3,1,0:T(8,128)} %bitcast.25), calls=%async_computation.1 | async-start | bytes 786432 | tf_op jit(solution)/shard_map/all_to_all | solution.py:995
  59.9 13.4 %all-to-all-done.1 = f32[4,3,128,64]{2,3,1,0:T(8,128)S(1)} async-done(((f32[4,3,128,64]{2,3,1,0:T(8,128)}), f32[4,3,128,64]{2,3,1,0:T(8,128)S(1)}, u32[]{:S(2)}, u32[]{:S(2)}) %all-to-all-start.1) | async-done | bytes 393248 | tf_op jit(solution)/shard_map/all_to_all | solution.py:995
  73.4 4.0 all-to-all-start.2
  77.4 35.3 %time_forward.1 = (f32[4,12,16,128]{3,2,1,0:T(8,128)}, f32[64,16,128]{2,1,0:T(8,128)}, f32[65,16,1024]{2,1,0:T(8,128)}, f32[65,16,1024]{2,1,0:T(8,128)}, f32[65,...) custom-call(s32[2,12]{1,0:T(2,128)} %pad_add_fusion.places_s, ...), custom_call_target="tpu_custom_call" | custom-call | flops 38499999744 | bytes 105000000 | tf_op jit(solution)/shard_map/time_forward/pallas_call | solution.py:439
  116.8 7.3 %exchange.4 = f32[4,12,16,128]{3,2,1,0:T(8,128)} custom-call(f32[4,12,16,128]{3,2,1,0:T(8,128)} %get-tuple-element.100.source), custom_call_target="tpu_custom_call" | custom-call | flops 8800000000 | bytes 24000000 | tf_op jit(solution)/shard_map/exchange/pallas_call | solution.py:866
  126.7 1.1 copy.92.wide_mine
  127.8 1.2 copy.93.wide_other
  129.0 5.1 all-to-all-start
  136.3 28.3 %band_forward.1 = (f32[48,16,128]{2,1,0:T(8,128)}, f32[41,16,128]{2,1,0:T(8,128)}, f32[41,16,1024]{2,1,0:T(8,128)}, f32[41,16,1024]{2,1,0:T(8,128)}, f32[41,16,2...) custom-call(s32[1,41]{1,0:T(1,128)} %bitcast.182, ...), custom_call_target="tpu_custom_call" | custom-call | flops 30799998976 | bytes 84000000 | tf_op jit(solution)/shard_map/band_forward/pallas_call | solution.py:569
  164.6 14.2 %exchange.5.arrived = f32[4,4,3,16,128]{4,3,2,1,0:T(8,128)} custom-call(f32[4,4,3,16,128]{4,3,2,1,0:T(8,128)} %bitcast.193), custom_call_target="tpu_custom_call" | custom-call | flops 8800000000 | bytes 24000000 | tf_op jit(solution)/shard_map/exchange/pallas_call | solution.py:866
  179.7 11.6 %mask_network.1 = (f32[4,3,64,256]{3,2,1,0:T(8,128)}, f32[4,4,3,16,128]{4,3,2,1,0:T(8,128)}, f32[4,3,128,64]{3,2,1,0:T(8,128)}, f32[4,3,128,64]{3,2,1,0:T(8,128)...) custom-call(s32[2,3]{1,0:T(2,128)} %stack.87.places, ...), custom_call_target="tpu_custom_call" | custom-call | flops 13200000000 | bytes 36000000 | tf_op jit(solution)/shard_map/mask_network/pallas_call | solution.py:698
  191.3 14.7 %exchange.6 = f32[4,4,3,16,128]{4,3,2,1,0:T(8,128)} custom-call(f32[4,4,3,16,128]{4,3,2,1,0:T(8,128)} %get-tuple-element.107.source), custom_call_target="tpu_custom_call" | custom-call | flops 8800000000 | bytes 24000000 | tf_op jit(solution)/shard_map/exchange/pallas_call | solution.py:866
  206.1 44.8 %band_backward.1 = (f32[48,16,128]{2,1,0:T(8,128)}, f32[8,864,128]{2,1,0:T(8,128)}) custom-call(s32[1,41]{1,0:T(1,128)} %bitcast.183, f32[48,16,128]{2,1,0:T(8,128)} %bitcast.192, f32[41,16,128]{2,1,0:T(8,128)} %get-tuple-element.108.x, f32[41,16,1024]{2,1,0:T(8,128)} %get-tuple-element.109.act0, f32[41,16,1024]{2,1,0:T(8,128)} %get-tuple-element.110.act1, ...), custom_call_target="tpu_custom_call" | custom-call | flops 47300001792 | bytes 129000000 | tf_op jit(solution)/shard_map/band_backward/pallas_call | solution.py:611
  253.9 1.8 multiply_reduce_fusion.7
  255.6 2.4 multiply_reduce_fusion.1
  258.4 1.0 copy.98
  259.4 4.8 all-to-all-start.4
  264.3 8.1 %exchange.7.dy_in = f32[4,12,16,128]{3,2,1,0:T(8,128)} custom-call(f32[4,12,16,128]{3,2,1,0:T(8,128)} %bitcast.191), custom_call_target="tpu_custom_call" | custom-call | flops 8800000000 | bytes 24000000 | tf_op jit(solution)/shard_map/exchange/pallas_call | solution.py:866
  272.4 2.9 add.208
  275.3 7.9 %all-to-all-done.4 = f32[4,3,128,64]{2,3,1,0:T(8,128)S(1)} async-done(((f32[4,3,128,64]{2,3,1,0:T(8,128)}), f32[4,3,128,64]{2,3,1,0:T(8,128)S(1)}, u32[]{:S(2)}, u32[]{:S(2)}) %all-to-all-start.4) | async-done | bytes 393248 | tf_op jit(solution)/shard_map/all_to_all | solution.py:1025
  283.1 3.6 all-to-all-start.5
  286.8 52.5 %time_backward.1 = (f32[128,1280]{1,0:T(8,128)}, f32[8,408,128]{2,1,0:T(8,128)}, f32[12,1,640]{2,1,0:T(1,128)}, f32[8,864,128]{2,1,0:T(8,128)}) custom-call(s32[2,12]{1,0:T(2,128)} %pad_add_fusion.places_s, s32[2,3]{1,0:T(2,128)} %pad_add_fusion.1.clips, f32[4,12,16,128]{3,2,1,0:T(8,128)} %exchange.7.dy_in, f32[128,1280]{1,0:T(8,128)} %pad.29.spec, ...), custom_call_target="tpu_custom_call" | custom-call | flops 54999998464 | bytes 150000000 | tf_op jit(solution)/shard_map/time_backward/pallas_call | solution.py:515
  341.0 1.3 copy.94
  343.1 4.8 all-to-all-start.3
  347.9 52.2 %reduce_back.1 = (f32[864,128]{1,0:T(8,128)}, f32[408,128]{1,0:T(8,128)}) custom-call(f32[8,864,128]{2,1,0:T(8,128)} %get-tuple-element.132.g_rnn, f32[8,408,128]{2,1,0:T(8,128)} %bitcast_dynamic-update-slice_fusion.g_split), custom_call_target="tpu_custom_call" | custom-call | flops 44000002048 | bytes 120000000 | tf_op jit(solution)/shard_map/reduce_back/pallas_call | solution.py:950
  400.2 1.4 slice.217
  401.5 1.0 slice.215
  402.5 1.0 slice.213
  406.1 1.6 multiply_reduce_fusion.14
  409.7 1.0 multiply_reduce_fusion.2
  412.0 1.4 slice.218
  413.4 1.0 slice.216
  414.4 1.0 slice.214
  416.7 1.3 multiply_reduce_fusion.24
  418.6 1.4 multiply_reduce_fusion.17
  423.4 2.7 stack.104
  426.7 4.1 all-to-all-start.6
  431.5 1.1 copy.99
  432.6 6.4 %all-to-all-done.6 = f32[32,8,128]{2,1,0:T(8,128)} async-done(((f32[32,8,128]{2,1,0:T(8,128)}), f32[32,8,128]{2,1,0:T(8,128)}, u32[]{:S(2)}, u32[]{:S(2)}) %all-to-all-start.6) | async-done | bytes 131104 | tf_op jit(solution)/shard_map/all_to_all | solution.py:985
  441.3 1.6 slice_multiply_fusion
  442.9 1.2 multiply_reduce_fusion.22
  444.8 2.1 multiply_reduce_fusion.15
  447.7 3.2 multiply_reduce_fusion.3
  451.6 2.7 multiply_reduce_fusion.9
  455.0 1.2 multiply_reduce_fusion.18
  456.5 1.1 copy-done.12
  458.1 4.4 multiply_reduce_fusion
  462.6 3.3 multiply_reduce_fusion.6
  465.9 1.5 multiply_reduce_fusion.12
  467.5 3.2 stack.113
  472.0 3.3 all-to-all-start.7
  475.3 1.9 slice_bitcast_fusion
  477.2 6.2 %all-to-all-done.7 = f32[32,8,128]{2,1,0:T(8,128)} async-done(((f32[32,8,128]{2,1,0:T(8,128)}), f32[32,8,128]{2,1,0:T(8,128)}, u32[]{:S(2)}, u32[]{:S(2)}) %all-to-all-start.7) | async-done | bytes 131104 | tf_op jit(solution)/shard_map/all_to_all | solution.py:985
  483.4 1.5 reduce_sum.299
  491.5 1.3 multiply_subtract_fusion.7
  492.8 1.5 multiply_subtract_fusion.5
  494.3 2.2 multiply_subtract_fusion.1
  498.1 3.4 multiply_subtract_fusion
  501.5 2.0 multiply_subtract_fusion.2
  (232 shorter events, 35.3 us)
Async XLA Ops:
  7.2 127.6 %all-gather.3.cloned.1.call-start = ((), (), s32[]{:S(2)}) async-start(), calls=%async_computation.10 | async-start | bytes 3981312 | tf_op jit(solution)/shard_map/all_gather | solution.py:1113
  13.2 40.1 %copy-start.59 = (s32[41]{0:T(128)S(1)}, s32[41]{0:T(128)}, u32[]{:S(2)}) copy-start(s32[41]{0:T(128)} %param.36) | copy-start | bytes 496
  13.2 40.9 %copy-start.62 = (s32[1,64]{1,0:T(1,128)S(1)}, s32[1,64]{1,0:T(1,128)}, u32[]{:S(2)}) copy-start(s32[1,64]{1,0:T(1,128)} %param.34) | copy-start | bytes 772
  13.2 42.8 %copy-start.60 = (s32[41]{0:T(128)S(1)}, s32[41]{0:T(128)}, u32[]{:S(2)}) copy-start(s32[41]{0:T(128)} %param.35) | copy-start | bytes 496
  47.0 11.0 %copy-start.34 = (f32[64,2,1025]{2,1,0:T(2,128)S(1)}, f32[64,2,1025]{2,1,0:T(2,128)}, u32[]{:S(2)}) copy-start(f32[64,2,1025]{2,1,0:T(2,128)} %param.33) | copy-start | bytes 1574404
  47.1 26.3 %all-to-all-start.1 = ((f32[4,3,128,64]{2,3,1,0:T(8,128)}), f32[4,3,128,64]{2,3,1,0:T(8,128)S(1)}, u32[]{:S(2)}, u32[]{:S(2)}) async-start(f32[4,3,128,64]{2,3,1,0:T(8,128)} %bitcast.25), calls=%async_computation.1 | async-start | bytes 786432 | tf_op jit(solution)/shard_map/all_to_all | solution.py:995
  59.2 14.2 %copy-start.61 = (s32[41]{0:T(128)}, s32[41]{0:T(128)S(1)}, u32[]{:S(2)}) copy-start(s32[41]{0:T(128)S(1)} %add_add_fusion) | copy-start | bytes 496
  73.4 55.6 %all-to-all-start.2 = ((f32[4,3,64,512]{3,2,1,0:T(8,128)}), f32[4,3,64,512]{3,2,1,0:T(8,128)S(1)}, u32[]{:S(2)}, u32[]{:S(2)}) async-start(f32[4,3,64,512]{3,2,1,0:T(8,128)} %bitcast.26), calls=%async_computation.2 | async-start | bytes 3145728 | tf_op jit(solution)/shard_map/all_to_all | solution.py:995
  77.4 35.4 %copy-start.4 = (f32[2,2,128,128]{3,2,1,0:T(8,128)S(1)}, f32[2,2,128,128]{3,2,1,0:T(8,128)}, u32[]{:S(2)}) copy-start(f32[2,2,128,128]{3,2,1,0:T(8,128)} %param.42) | copy-start | bytes 786436
  77.4 36.7 %copy-start = (f32[2,2,256,128]{3,2,1,0:T(8,128)S(1)}, f32[2,2,256,128]{3,2,1,0:T(8,128)}, u32[]{:S(2)}) copy-start(f32[2,2,256,128]{3,2,1,0:T(8,128)} %param.43) | copy-start | bytes 1572868
  116.7 9.3 %slice-start = ((f32[12,1,1920]{2,1,0:T(1,128)}), f32[12,1,1280]{2,1,0:T(1,128)S(1)}, s32[]{:S(2)}) async-start(f32[12,1,1920]{2,1,0:T(1,128)} %broadcast_in_dim_reshape.3.v_band), calls=%async_computation.12 | async-start | bytes 122880 | tf_op jit(solution)/shard_map/slice | solution.py:1168
  124.1 3.7 collective-permute-start
  129.0 35.6 %copy-start.14 = (f32[4,3,64,512]{3,2,1,0:T(8,128)}, f32[4,3,64,512]{3,2,1,0:T(8,128)S(1)}, u32[]{:S(2)}) copy-start(f32[4,3,64,512]{3,2,1,0:T(8,128)S(1)} %all-to-all-done.2.mask_mine) | copy-start | bytes 4718596
  129.0 49.8 %all-to-all-start = ((f32[4,3,64,256]{3,2,1,0:T(8,128)}), f32[4,3,64,256]{3,2,1,0:T(8,128)S(1)}, u32[]{:S(2)}, u32[]{:S(2)}) async-start(f32[4,3,64,256]{3,2,1,0:T(8,128)} %bitcast.21), calls=%async_computation | async-start | bytes 1572864 | tf_op jit(solution)/shard_map/all_to_all | solution.py:1136
  134.1 208.9 %reduce-scatter.2.cloned.1.call-start = ((), (), s32[]{:S(2)}) async-start(), calls=%async_computation.9 | async-start | bytes 3981312 | tf_op jit(solution)/shard_map/reduce_scatter | solution.py:1178
  134.6 44.3 %collective-permute-start.1 = (f32[4,3,64,512]{3,2,1,0:T(8,128)S(1)}, f32[4,3,64,512]{3,2,1,0:T(8,128)}, u32[]{:S(2)}, u32[]{:S(2)}) collective-permute-start(f32[4,3,64,512]{3,2,1,0:T(8,128)S(1)} %all-to-all-done.2.mask_mine), channel_id=1, source_target_pairs={{0,1},{1,0},{2,3},{3,2},{4,5},{5,4},{6,7},{7,6},{8,9},{9,8},{10,11... | collective-permute-start | bytes 4718600 | tf_op jit(solution)/shard_map/ppermute | solution.py:990
  206.0 66.3 %collective-permute-start.3 = (f32[4,3,64,512]{3,2,1,0:T(8,128)}, f32[4,3,64,512]{3,2,1,0:T(8,128)}, u32[]{:S(2)}, u32[]{:S(2)}) collective-permute-start(f32[4,3,64,512]{3,2,1,0:T(8,128)} %get-tuple-element.140), channel_id=1, source_target_pairs={{0,1},{1,0},{2,3},{3,2},{4,5},{5,4},{6,7},{7,6},{8,9},{9,8},{10,11... | collective-permute-start | bytes 4718600 | tf_op jit(solution)/shard_map/ppermute | solution.py:990
  252.7 5.4 %collective-permute-start.2 = (f32[4,3,128,64]{2,3,1,0:T(8,128)S(1)}, f32[4,3,128,64]{2,3,1,0:T(8,128)S(1)}, u32[]{:S(2)}, u32[]{:S(2)}) collective-permute-start(f32[4,3,128,64]{2,3,1,0:T(8,128)S(1)} %copy.96), channel_id=1, source_target_pairs={{0,1},{1,0},{2,3},{3,2},{4,5},{5,4},{6,7},{7,6},{8,9},{9,8},{10,11... | collective-permute-start | bytes 1179656 | tf_op jit(solution)/shard_map/ppermute | solution.py:990
  253.9 4.5 copy-start.29
  259.4 23.7 %all-to-all-start.4 = ((f32[4,3,128,64]{2,3,1,0:T(8,128)}), f32[4,3,128,64]{2,3,1,0:T(8,128)S(1)}, u32[]{:S(2)}, u32[]{:S(2)}) async-start(f32[4,3,128,64]{2,3,1,0:T(8,128)} %copy.98), calls=%async_computation.4 | async-start | bytes 786432 | tf_op jit(solution)/shard_map/all_to_all | solution.py:1025
  264.3 8.1 %copy-start.17 = (f32[4,3,64,512]{3,2,1,0:T(8,128)S(1)}, f32[4,3,64,512]{3,2,1,0:T(8,128)}, u32[]{:S(2)}) copy-start(f32[4,3,64,512]{3,2,1,0:T(8,128)} %get-tuple-element.139) | copy-start | bytes 4718596
  283.1 59.9 %all-to-all-start.5 = ((f32[4,3,64,512]{3,2,1,0:T(8,128)}), f32[4,3,64,512]{3,2,1,0:T(8,128)S(1)}, u32[]{:S(2)}, u32[]{:S(2)}) async-start(f32[4,3,64,512]{3,2,1,0:T(8,128)} %add.208), calls=%async_computation.5 | async-start | bytes 3145728 | tf_op jit(solution)/shard_map/all_to_all | solution.py:1025
  286.7 125.3 %all-reduce.11.cloned.1.call-start = ((), (), s32[]{:S(2)}) async-start(), calls=%async_computation.11 | async-start | bytes 2195456 | tf_op jit(solution)/shard_map/psum | solution.py:1184
  286.8 53.3 %copy-start.52 = (f32[3,1,1280]{2,1,0:T(1,128)S(1)}, f32[3,1,1280]{2,1,0:T(1,128)}, u32[]{:S(2)}) copy-start(f32[3,1,1280]{2,1,0:T(1,128)} %get-tuple-element.135) | copy-start | bytes 46084
  343.1 83.0 %all-to-all-start.3 = ((f32[4,3,64,256]{3,2,1,0:T(8,128)}), f32[4,3,64,256]{3,2,1,0:T(8,128)S(1)}, u32[]{:S(2)}, u32[]{:S(2)}) async-start(f32[4,3,64,256]{3,2,1,0:T(8,128)} %get-tuple-element.106), calls=%async_computation.3 | async-start | bytes 1572864 | tf_op jit(solution)/shard_map/all_to_all | solution.py:1174
  402.5 28.4 %copy-start.9 = (f32[1,512,128]{2,1,0:T(8,128)}, f32[1,512,128]{2,1,0:T(8,128)S(1)}, u32[]{:S(2)}) copy-start(f32[1,512,128]{2,1,0:T(8,128)S(1)} %slice.215) | copy-start | bytes 786436
  403.5 18.5 %copy-start.18 = (f32[1,256,128]{2,1,0:T(8,128)}, f32[1,256,128]{2,1,0:T(8,128)S(1)}, u32[]{:S(2)}) copy-start(f32[1,256,128]{2,1,0:T(8,128)S(1)} %slice.213) | copy-start | bytes 393220
  405.5 7.9 %copy-start.43 = (f32[1,24,128]{2,1,0:T(8,128)}, f32[1,24,128]{2,1,0:T(8,128)S(1)}, u32[]{:S(2)}) copy-start(f32[1,24,128]{2,1,0:T(8,128)S(1)} %slice.211) | copy-start | bytes 36868
  414.4 16.5 %copy-start.10 = (f32[1,512,128]{2,1,0:T(8,128)}, f32[1,512,128]{2,1,0:T(8,128)S(1)}, u32[]{:S(2)}) copy-start(f32[1,512,128]{2,1,0:T(8,128)S(1)} %slice.216) | copy-start | bytes 786436
  415.4 15.5 %copy-start.20 = (f32[1,256,128]{2,1,0:T(8,128)}, f32[1,256,128]{2,1,0:T(8,128)S(1)}, u32[]{:S(2)}) copy-start(f32[1,256,128]{2,1,0:T(8,128)S(1)} %slice.214) | copy-start | bytes 393220
  426.7 12.3 %all-to-all-start.6 = ((f32[32,8,128]{2,1,0:T(8,128)}), f32[32,8,128]{2,1,0:T(8,128)}, u32[]{:S(2)}, u32[]{:S(2)}) async-start(f32[32,8,128]{2,1,0:T(8,128)} %broadcast_in_dim.45), calls=%async_computation.7 | async-start | bytes 262144 | tf_op jit(solution)/shard_map/all_to_all | solution.py:985
  431.3 9.9 %copy-start.44 = (f32[1,24,128]{2,1,0:T(8,128)S(1)}, f32[1,24,128]{2,1,0:T(8,128)}, u32[]{:S(2)}) copy-start(f32[1,24,128]{2,1,0:T(8,128)} %copy-done.43) | copy-start | bytes 36868
  431.3 11.6 %copy-start.49 = (f32[2,304]{1,0:T(2,128)S(1)}, f32[2,304]{1,0:T(2,128)}, u32[]{:S(2)}) copy-start(f32[2,304]{1,0:T(2,128)} %param.45) | copy-start | bytes 7300
  431.4 11.6 %copy-start.53 = (f32[1,1,3,128]{3,1,2,0:T(1,128)S(1)}, f32[1,1,3,128]{3,1,2,0:T(1,128)}, u32[]{:S(2)}) copy-start(f32[1,1,3,128]{3,1,2,0:T(1,128)} %copy.122) | copy-start | bytes 4612
  431.4 11.5 %copy-start.55 = (f32[1,1,3,128]{3,1,2,0:T(1,128)S(1)}, f32[1,1,3,128]{3,1,2,0:T(1,128)}, u32[]{:S(2)}) copy-start(f32[1,1,3,128]{3,1,2,0:T(1,128)} %copy-done.54) | copy-start | bytes 4612
  431.4 11.5 %copy-start.57 = (f32[2,304]{1,0:T(2,128)S(1)}, f32[2,304]{1,0:T(2,128)}, u32[]{:S(2)}) copy-start(f32[2,304]{1,0:T(2,128)} %param.53) | copy-start | bytes 7300
  431.4 11.5 %copy-start.58 = (f32[2,304]{1,0:T(2,128)S(1)}, f32[2,304]{1,0:T(2,128)}, u32[]{:S(2)}) copy-start(f32[2,304]{1,0:T(2,128)} %param.61) | copy-start | bytes 7300
  431.4 13.4 %copy-start.22 = (f32[2,64,128]{2,1,0:T(8,128)S(1)}, f32[2,64,128]{2,1,0:T(8,128)}, u32[]{:S(2)}) copy-start(f32[2,64,128]{2,1,0:T(8,128)} %param.44) | copy-start | bytes 196612
  431.4 13.4 %copy-start.37 = (f32[1,64,128]{2,1,0:T(8,128)S(1)}, f32[1,64,128]{2,1,0:T(8,128)}, u32[]{:S(2)}) copy-start(f32[1,64,128]{2,1,0:T(8,128)} %slice.217) | copy-start | bytes 98308
  431.4 13.4 %copy-start.38 = (f32[1,64,128]{2,1,0:T(8,128)S(1)}, f32[1,64,128]{2,1,0:T(8,128)}, u32[]{:S(2)}) copy-start(f32[1,64,128]{2,1,0:T(8,128)} %slice.218) | copy-start | bytes 98308
  431.4 13.4 %copy-start.45 = (f32[2,64,128]{2,1,0:T(8,128)S(1)}, f32[2,64,128]{2,1,0:T(8,128)}, u32[]{:S(2)}) copy-start(f32[2,64,128]{2,1,0:T(8,128)} %param.52) | copy-start | bytes 196612
  431.5 16.2 %copy-start.1 = (f32[2,2,256,128]{3,2,1,0:T(8,128)S(1)}, f32[2,2,256,128]{3,2,1,0:T(8,128)}, u32[]{:S(2)}) copy-start(f32[2,2,256,128]{3,2,1,0:T(8,128)} %param.43) | copy-start | bytes 1572868
  440.0 7.0 %copy-start.56 = (f32[8,128]{1,0:T(8,128)}, f32[8,128]{1,0:T(8,128)S(1)}, u32[]{:S(2)}) copy-start(f32[8,128]{1,0:T(8,128)S(1)} %reduce_sum.290) | copy-start | bytes 12292
  447.6 3.9 copy-start.5
  447.6 3.9 copy-start.19
  450.9 43.5 %copy-start.11 = (f32[2,2,256,128]{3,2,1,0:T(8,128)}, f32[2,2,256,128]{3,2,1,0:T(8,128)S(1)}, u32[]{:S(2)}) copy-start(f32[2,2,256,128]{3,2,1,0:T(8,128)S(1)} %get-tuple-element.236) | copy-start | bytes 1572868
  450.9 4.2 copy-start.50
  450.9 4.2 copy-start.51
  458.1 4.4 copy-start.35
  458.1 4.5 copy-start.36
  462.5 35.6 %copy-start.2 = (f32[12,64,512]{2,1,0:T(8,128)}, f32[12,64,512]{2,1,0:T(8,128)S(1)}, u32[]{:S(2)}) copy-start(f32[12,64,512]{2,1,0:T(8,128)S(1)} %get-tuple-element.245) | copy-start | bytes 4718596
  462.5 3.4 copy-start.8
  462.5 3.4 copy-start.30
  462.5 3.4 copy-start.41
  462.5 3.4 copy-start.42
  465.9 35.6 %copy-start.15 = (f32[12,128,64]{1,2,0:T(8,128)}, f32[12,128,64]{1,2,0:T(8,128)S(1)}, u32[]{:S(2)}) copy-start(f32[12,128,64]{1,2,0:T(8,128)S(1)} %get-tuple-element.248) | copy-start | bytes 1179652
  465.9 26.9 %copy-start.23 = (f32[2,64,128]{2,1,0:T(8,128)S(1)}, f32[2,64,128]{2,1,0:T(8,128)}, u32[]{:S(2)}) copy-start(f32[2,64,128]{2,1,0:T(8,128)} %param.44) | copy-start | bytes 196612
  472.0 11.4 %all-to-all-start.7 = ((f32[32,8,128]{2,1,0:T(8,128)}), f32[32,8,128]{2,1,0:T(8,128)}, u32[]{:S(2)}, u32[]{:S(2)}) async-start(f32[32,8,128]{2,1,0:T(8,128)} %broadcast_in_dim.48), calls=%async_computation.8 | async-start | bytes 262144 | tf_op jit(solution)/shard_map/all_to_all | solution.py:985
  484.9 11.6 %copy-start.24 = (f32[2,2,128,128]{3,2,1,0:T(8,128)S(1)}, f32[2,2,128,128]{3,2,1,0:T(8,128)}, u32[]{:S(2)}) copy-start(f32[2,2,128,128]{3,2,1,0:T(8,128)} %get-tuple-element.239) | copy-start | bytes 786436
  484.9 11.6 %copy-start.25 = (f32[2,2,128,128]{3,2,1,0:T(8,128)S(1)}, f32[2,2,128,128]{3,2,1,0:T(8,128)}, u32[]{:S(2)}) copy-start(f32[2,2,128,128]{3,2,1,0:T(8,128)} %get-tuple-element.240) | copy-start | bytes 786436
  494.3 3.1 copy-start.46
  494.3 3.1 copy-start.47
  494.3 3.7 copy-start.3
  498.1 3.4 copy-start.16
  (15 other events, 26.5 us)
Sparse Core Ops, SparseCore 0:
  47.2 74.4 all-gather.2
  251.0 64.0 reduce-scatter.1
  343.2 63.5 all-reduce.10
